TPU v7x, 32 devices: a whole 2x2x4 slice. The times are simulated.
32 devices in a mesh: expert: 4 (over x, core), dp: 8 (over z, y).
Axes of the slice: x: 2, y: 2, z: 4, core: 2. Of those that a mesh axis runs over, the one named last changes fastest.
Arguments:
- tokens: bfloat16 [4096, 1280], P(('expert', 'dp')), may hold values from -6 to 6
- expert_ids: int32 [4096], P(('expert', 'dp')), may hold values from 0 to 15, as said below
- up_weight: bfloat16 [16, 1280, 4096], P('expert', None, 'dp'), may hold values from -0.15625 to 0.15625
- down_weight: bfloat16 [16, 4096, 1280], P('expert', 'dp'), may hold values from -0.09375 to 0.09375
- out_grad: bfloat16 [4096, 1280], P(('expert', 'dp')), may hold values from -0.1875 to 0.1875
Outputs:
- expert_out: bfloat16 [4096, 1280], P(('expert', 'dp'))
- up_grad: bfloat16 [16, 1280, 4096], P('expert', None, 'dp')
- down_grad: bfloat16 [16, 4096, 1280], P('expert', 'dp')
Inputs may be any that keep to these rules, and one draw needn't show every extreme that they name: `expert_ids`: within each aligned block of 128 tokens (the tokens of one device) no expert id appears more than 10 times, and in every draw one expert appears exactly 10 times in every block.
All inputs are finite; a program needn't handle non-finite values.
Results may differ from a plain program's by a relative error of at most 0.005.
Values may be sent and summed in bfloat16 or wider, within the bound.
No kernel may reach another device: no remote copies, remote signals or barrier semaphores. Data moves between devices by JAX's collectives and lax.ppermute only.
A program may use at most 128 MiB of HBM per device.

v0:
```python
import math

import jax
import jax.numpy as jnp
from jax import lax
from jax.sharding import PartitionSpec as P

gelu_scale = math.sqrt(2.0 / math.pi)
cubic_term = 0.044715


def gelu_value(values):
    inner_arg = gelu_scale * (values + cubic_term * values * values * values)
    return 0.5 * values * (1.0 + jnp.tanh(inner_arg))


def gelu_slope(values):
    tangent = jnp.tanh(gelu_scale * (values + cubic_term * values * values * values))
    return 0.5 * (1.0 + tangent) + 0.5 * values * (1.0 - tangent * tangent) * gelu_scale * (
        1.0 + 3.0 * cubic_term * values * values
    )


def on_device(tokens, expert_ids, up_weight, down_weight, out_grad):
    owners = lax.axis_size("expert")
    local_experts = up_weight.shape[0]
    all_experts = owners * local_experts
    tok_rows = tokens.shape[0]
    width = tokens.shape[1]
    capacity = 5 * tok_rows // (4 * all_experts)
    onehot = (expert_ids[:, None] == jnp.arange(all_experts, dtype=jnp.int32)[None, :]).astype(
        jnp.int32
    )
    ranks = jnp.cumsum(onehot, axis=0) - 1
    slot_index = jnp.sum(onehot * ranks, axis=1)
    target = expert_ids * capacity + slot_index
    owner_id = expert_ids // local_experts
    local_id = expert_ids % local_experts
    back_index = (owner_id * capacity + slot_index) * local_experts + local_id

    def pack_rows(values):
        filled = jnp.zeros((all_experts * capacity, width), values.dtype).at[target].set(values)
        return filled.reshape(owners, local_experts, capacity, width)

    got_tok = lax.all_to_all(pack_rows(tokens), "expert", split_axis=0, concat_axis=2, tiled=True)
    rows_tok = lax.all_gather(got_tok, "dp", axis=2, tiled=True)[0]
    hidden_pre = jnp.einsum("erd,edf->erf", rows_tok, up_weight, preferred_element_type=jnp.float32)
    active = gelu_value(hidden_pre).astype(jnp.bfloat16)
    portion = active
    summed = lax.psum_scatter(
        jnp.einsum("erf,efd->red", portion, down_weight, preferred_element_type=jnp.float32),
        "dp",
        scatter_dimension=0,
        tiled=True,
    )
    sendback = summed.astype(jnp.bfloat16).reshape(owners, capacity, local_experts, width)
    returned = lax.all_to_all(sendback, "expert", split_axis=0, concat_axis=0, tiled=True)
    combined = returned.reshape(owners * capacity * local_experts, width)[back_index]
    hidden_pre, active, combined = (hidden_pre, active, combined)
    got_grad = lax.all_to_all(
        pack_rows(out_grad), "expert", split_axis=0, concat_axis=2, tiled=True
    )
    rows_grad = lax.all_gather(got_grad, "dp", axis=2, tiled=True)[0]
    back_grad = jnp.einsum(
        "erd,efd->erf", rows_grad, down_weight, preferred_element_type=jnp.float32
    )
    pre_grad = (back_grad * gelu_slope(hidden_pre)).astype(jnp.bfloat16)
    down_part = jnp.einsum(
        "erf,erd->efd", active, rows_grad, preferred_element_type=jnp.float32
    ).astype(jnp.bfloat16)
    up_part = jnp.einsum(
        "erd,erf->edf", rows_tok, pre_grad, preferred_element_type=jnp.float32
    ).astype(jnp.bfloat16)
    return (combined, up_part, down_part)


def solution(mesh):
    in_specs = (
        P(("expert", "dp"), None),
        P(("expert", "dp")),
        P("expert", None, "dp"),
        P("expert", "dp", None),
        P(("expert", "dp"), None),
    )
    out_specs = (P(("expert", "dp"), None), P("expert", None, "dp"), P("expert", "dp", None))
    return jax.shard_map(
        on_device, mesh=mesh, in_specs=in_specs, out_specs=out_specs, check_vma=False
    )
```

profile of v0, /device:TPU:0, one launch (start us, length us, event | category | flops | bytes accessed | tf_op | source)
XLA Modules:
  0.0 295.7 jit_solution(3183009938010657015)
XLA Ops:
  7.2 0.7 fusion.21
  8.0 0.2 reduce_window_sum.11
  8.1 0.8 select_reduce_fusion
  9.0 0.7 compare_select_fusion
  9.6 1.7 scatter_custom_fusion
  11.5 0.2 copy.14
  11.7 11.6 %all_to_all.41 = bf16[4,4,10,1280]{3,1,2,0:T(4,128)(2,1)S(1)} all-to-all(bf16[4,4,10,1280]{3,1,2,0:T(4,128)(2,1)S(1)} %copy.14), channel_id=1, replica_groups=mesh['expert'=4,'dp'=8] {'expert'}, dimensions={0} | all-to-all | bytes 819200 | tf_op jit(solution)/shard_map/all_to_all | solution.py:45
  23.3 0.8 copy.15
  24.2 1.7 scatter_custom_fusion.1
  26.0 0.2 copy.17
  26.2 10.0 %all_to_all.42 = bf16[4,4,10,1280]{3,1,2,0:T(4,128)(2,1)S(1)} all-to-all(bf16[4,4,10,1280]{3,1,2,0:T(4,128)(2,1)S(1)} %copy.17), channel_id=1, replica_groups=mesh['expert'=4,'dp'=8] {'expert'}, dimensions={0} | all-to-all | bytes 819200 | tf_op jit(solution)/shard_map/all_to_all | solution.py:60
  36.2 0.8 copy.18
  37.1 49.5 %all-gather.3.cloned.1.call-done = bf16[1,4,320,1280]{3,2,1,0:T(8,128)(2,1)} async-done(((bf16[1,4,40,1280]{3,2,1,0:T(8,128)(2,1)}), bf16[1,4,320,1280]{3,2,1,0:T(8,128)(2,1)}) %all-gather.3.cloned.1.call-update) | async-done | bytes 3276816 | tf_op jit(solution)/shard_map/all_gather | solution.py:46
  86.5 5.3 %fusion.4 = f32[4,320,512]{2,1,0:T(8,128)S(1)} fusion(bf16[4,1280,512]{2,1,0:T(8,128)(2,1)} %param.7, bf16[1,4,320,1280]{3,2,1,0:T(8,128)(2,1)} %all-gather.3.cloned.1.call-done), kind=kOutput, calls=%fused_computation.12 | convolution fusion | flops 1677721600 | bytes 11141120 | tf_op jit(solution)/shard_map/erd,edf->erf/dot_general | solution.py:47
  91.9 7.2 %convolution_bitcast_fusion = f32[320,4,1280]{2,0,1:T(8,128)} fusion(bf16[4,512,1280]{2,1,0:T(8,128)(2,1)} %param.8, f32[4,320,512]{2,1,0:T(8,128)S(1)} %fusion.4), kind=kOutput, calls=%fused_computation.5 | convolution fusion | flops 1683619840 | bytes 14417920 | tf_op jit(solution)/shard_map/erf,efd->red/dot_general | solution.py:51
  99.1 50.8 %all-gather.5.cloned.1.call-done = bf16[1,4,320,1280]{3,2,1,0:T(8,128)(2,1)} async-done(((bf16[1,4,40,1280]{3,2,1,0:T(8,128)(2,1)}), bf16[1,4,320,1280]{3,2,1,0:T(8,128)(2,1)}) %all-gather.5.cloned.1.call-update) | async-done | bytes 3276816 | tf_op jit(solution)/shard_map/all_gather | solution.py:63
  149.9 12.0 %convolution_convert_fusion.1 = bf16[4,1280,512]{2,1,0:T(8,128)(2,1)} fusion(bf16[1,4,320,1280]{3,2,1,0:T(8,128)(2,1)} %all-gather.3.cloned.1.call-done, f32[4,320,512]{2,1,0:T(8,128)S(1)} %fusion.4, bf16[4,512,1280]{2,1,0:T(8,128)(2,1)} %param.8, bf16[1,4,320,1280]{3,2,1,0:T(8,128)(2,1)} %all-gather.5.cloned.1.call-done), kind=kOutput, calls=%fused_computation.4 | convolution fusion | flops 3370516480 | bytes 19660800 | tf_op jit(solution)/shard_map/erd,erf->edf/dot_general | solution.py:71
  161.9 112.4 %reduce-scatter.2.cloned.1.call-done = f32[40,4,1280]{2,0,1:T(8,128)} async-done(((f32[320,4,1280]{2,0,1:T(8,128)}), f32[40,4,1280]{2,0,1:T(8,128)}) %reduce-scatter.2.cloned.1.call-update) | async-done | bytes 819216 | tf_op jit(solution)/shard_map/reduce_scatter | solution.py:50
  274.3 1.2 convert_element_type.20
  275.5 0.9 copy.16
  276.4 3.5 %all-to-all-start.1 = ((bf16[4,10,4,1280]{3,2,1,0:T(4,128)(2,1)}), bf16[4,10,4,1280]{3,2,1,0:T(4,128)(2,1)S(1)}, u32[]{:S(2)}, u32[]{:S(2)}) async-start(bf16[4,10,4,1280]{3,2,1,0:T(4,128)(2,1)} %bitcast.5), calls=%async_computation.2 | async-start | bytes 819200 | tf_op jit(solution)/shard_map/all_to_all | solution.py:57
  279.8 6.7 %convolution_convert_fusion = bf16[4,512,1280]{2,1,0:T(8,128)(2,1)} fusion(bf16[1,4,320,1280]{3,2,1,0:T(8,128)(2,1)} %all-gather.5.cloned.1.call-done, f32[4,320,512]{2,1,0:T(8,128)S(1)} %fusion.4), kind=kOutput, calls=%fused_computation.3 | convolution fusion | flops 1686241280 | bytes 11141120 | tf_op jit(solution)/shard_map/erf,erd->efd/dot_general | solution.py:68
  286.5 0.9 all-to-all-done.1
  287.5 1.6 gather_fusion
  (10 shorter events, 0.5 us)
Async XLA Ops:
  7.2 79.4 %all-gather.3.cloned.1.call-start = ((), (), s32[]{:S(2)}) async-start(), calls=%async_computation.4 | async-start | bytes 3686400 | tf_op jit(solution)/shard_map/all_gather | solution.py:46
  24.1 125.8 %all-gather.5.cloned.1.call-start = ((), (), s32[]{:S(2)}) async-start(), calls=%async_computation.6 | async-start | bytes 3686400 | tf_op jit(solution)/shard_map/all_gather | solution.py:63
  37.0 237.2 %reduce-scatter.2.cloned.1.call-start = ((), (), s32[]{:S(2)}) async-start(), calls=%async_computation.5 | async-start | bytes 7372800 | tf_op jit(solution)/shard_map/reduce_scatter | solution.py:50
  276.4 11.1 %all-to-all-start.1 = ((bf16[4,10,4,1280]{3,2,1,0:T(4,128)(2,1)}), bf16[4,10,4,1280]{3,2,1,0:T(4,128)(2,1)S(1)}, u32[]{:S(2)}, u32[]{:S(2)}) async-start(bf16[4,10,4,1280]{3,2,1,0:T(4,128)(2,1)} %bitcast.5), calls=%async_computation.2 | async-start | bytes 819200 | tf_op jit(solution)/shard_map/all_to_all | solution.py:57
Sparse Core Ops, SparseCore 0:
  24.3 62.2 all-gather.2
  89.4 60.5 all-gather.4
  153.6 120.6 reduce-scatter.1
where the time goes:
time: 296 us
  waiting for transfers between devices  214 us (72%)
  matrix products  31.1 us (11%)
  blocking collectives  21.6 us (7%)
  between operations  13.8 us (5%)
  local copies, waits for them, and re-layouts  8.26 us (3%)
  other arithmetic  3.6 us (1%)
  starting transfers between devices  3.58 us (1%)
    reduce_scatter x1, waiting for transfers between devices, on_device(): lax.psum_scatter(jnp.einsum('erf,efd->red', portion, down_weight, preferr...  112 us
    all_gather x1, waiting for transfers between devices, on_device(): rows_grad = lax.all_gather(got_grad, 'dp', axis=2, tiled=True)[0]  50.8 us
    all_gather x1, waiting for transfers between devices, on_device(): rows_tok = lax.all_gather(got_tok, 'dp', axis=2, tiled=True)[0]  49.5 us
    dot_general x1, matrix products, on_device(): jnp.einsum('erd,erf->edf', rows_tok, pre_grad, preferred_element_type=jnp...  12 us
    all_to_all x1, blocking collectives, on_device(): lax.all_to_all(pack_rows(tokens), 'expert', split_axis=0, concat_axis=2,...  11.6 us
    all_to_all x1, blocking collectives, on_device(): lax.all_to_all(pack_rows(out_grad), 'expert', split_axis=0, concat_axis=2...  9.98 us
    dot_general x1, matrix products, on_device(): jnp.einsum('erf,efd->red', portion, down_weight, preferred_element_type=j...  7.17 us
    dot_general x1, matrix products, on_device(): jnp.einsum('erf,erd->efd', active, rows_grad, preferred_element_type=jnp....  6.69 us
  transfers between devices with their start and end apart: 4, of which 4 were waited for; matrix products, arithmetic and copies ran while one was open for 11% of the time, Pallas kernels for 0%

commit v1 on v0

v1 whole, which is shorter than its diff:
```python
import math

import jax
import jax.numpy as jnp
from jax import lax
from jax.sharding import PartitionSpec as P

gelu_scale = math.sqrt(2.0 / math.pi)
cubic_term = 0.044715


def gelu_value(values):
    inner_arg = gelu_scale * (values + cubic_term * values * values * values)
    return 0.5 * values * (1.0 + jnp.tanh(inner_arg))


def gelu_slope(values):
    tangent = jnp.tanh(gelu_scale * (values + cubic_term * values * values * values))
    return 0.5 * (1.0 + tangent) + 0.5 * values * (1.0 - tangent * tangent) * gelu_scale * (
        1.0 + 3.0 * cubic_term * values * values
    )


def grid_of(n):
    cols = 1
    while cols * cols * 4 <= n and n % (cols * 2) == 0:
        cols *= 2
    return n // cols, cols


def ring_z(value, step):
    n = lax.axis_size("dp")
    rows, cols = grid_of(n)
    perm = [(i, ((i // cols + step) % rows) * cols + i % cols) for i in range(n)]
    return lax.ppermute(value, "dp", perm)


def ring_y(value, step):
    n = lax.axis_size("dp")
    cols = grid_of(n)[1]
    perm = [(i, i // cols * cols + (i % cols + step) % cols) for i in range(n)]
    return lax.ppermute(value, "dp", perm)


def swap_expert(value, mask):
    n = lax.axis_size("expert")
    return lax.ppermute(value, "expert", [(i, i ^ mask) for i in range(n)])


def exchange(packed):
    return [packed[0]] + [swap_expert(packed[m], m) for m in range(1, packed.shape[0])]


def gather_dp(block):
    rows, cols = grid_of(lax.axis_size("dp"))
    blocks = []
    for k in range(rows):
        line = [block]
        for _ in range(cols - 1):
            line.append(ring_y(line[-1], 1))
        blocks.append(line)
        if k < rows - 1:
            block = ring_z(block, 1)
    return blocks


def scatter_dp(parts):
    rows, cols = grid_of(lax.axis_size("dp"))
    total = None
    for k in reversed(range(rows)):
        line = parts[k][cols - 1]
        for j in reversed(range(cols - 1)):
            line = ring_y(line.astype(jnp.bfloat16), -1).astype(jnp.float32) + parts[k][j]
        if total is None:
            total = line
        else:
            total = ring_z(total.astype(jnp.bfloat16), -1).astype(jnp.float32) + line
    return total


def on_device(tokens, expert_ids, up_weight, down_weight, out_grad):
    owners = lax.axis_size("expert")
    rows, cols = grid_of(lax.axis_size("dp"))
    local_experts = up_weight.shape[0]
    all_experts = owners * local_experts
    tok_rows, width = tokens.shape
    capacity = 5 * tok_rows // (4 * all_experts)
    slots = all_experts * capacity
    me = lax.axis_index("expert")
    index = jnp.arange(tok_rows, dtype=jnp.int32)
    earlier = (expert_ids[:, None] == expert_ids[None, :]) & (index[:, None] < index[None, :])
    slot_index = jnp.sum(earlier.astype(jnp.int32), axis=0)
    owner_id = expert_ids // local_experts
    local_id = expert_ids % local_experts
    target = ((owner_id ^ me) * local_experts + local_id) * capacity + slot_index
    place = (target[None, :] == jnp.arange(slots, dtype=jnp.int32)[:, None]).astype(jnp.bfloat16)

    def dispatch(values):
        packed = jnp.dot(place, values, preferred_element_type=jnp.float32).astype(values.dtype)
        got = exchange(packed.reshape(owners, local_experts, capacity, width))
        return jnp.stack(got, axis=1).reshape(local_experts, owners * capacity, width)

    def rows_of(blocks):
        return jnp.concatenate([b for line in blocks for b in line], axis=1)

    rows_tok = rows_of(gather_dp(dispatch(tokens)))
    rows_grad = rows_of(gather_dp(dispatch(out_grad)))

    hidden_pre = jnp.einsum("erd,edf->erf", rows_tok, up_weight, preferred_element_type=jnp.float32)
    active = gelu_value(hidden_pre).astype(jnp.bfloat16)
    part = jnp.einsum("erf,efd->erd", active, down_weight, preferred_element_type=jnp.float32)
    part = jnp.split(part, rows * cols, axis=1)
    summed = scatter_dp([part[k * cols : (k + 1) * cols] for k in range(rows)]).astype(jnp.bfloat16)
    summed = summed.reshape(local_experts, owners, capacity, width).transpose(1, 0, 2, 3)
    returned = jnp.concatenate(exchange(summed), axis=0).reshape(slots, width)
    combined = jnp.einsum("rt,rd->td", place, returned, preferred_element_type=jnp.float32)
    combined = combined.astype(jnp.bfloat16)

    back_grad = jnp.einsum(
        "erd,efd->erf", rows_grad, down_weight, preferred_element_type=jnp.float32
    )
    pre_grad = (back_grad * gelu_slope(hidden_pre)).astype(jnp.bfloat16)
    down_part = jnp.einsum(
        "erf,erd->efd", active, rows_grad, preferred_element_type=jnp.float32
    ).astype(jnp.bfloat16)
    up_part = jnp.einsum(
        "erd,erf->edf", rows_tok, pre_grad, preferred_element_type=jnp.float32
    ).astype(jnp.bfloat16)
    return (combined, up_part, down_part)


def solution(mesh):
    in_specs = (
        P(("expert", "dp"), None),
        P(("expert", "dp")),
        P("expert", None, "dp"),
        P("expert", "dp", None),
        P(("expert", "dp"), None),
    )
    out_specs = (P(("expert", "dp"), None), P("expert", None, "dp"), P("expert", "dp", None))
    return jax.shard_map(
        on_device, mesh=mesh, in_specs=in_specs, out_specs=out_specs, check_vma=False
    )
```

time: 296 us -> 158 us (0.53)
  waiting for transfers between devices: 214 us -> 87.4 us
  starting transfers between devices: 3.58 us -> 37.8 us
  blocking collectives: 21.6 us -> 0 us
  between operations: 13.8 us -> 1.02 us
  matrix products: 31.1 us -> 23.1 us
  local copies, waits for them, and re-layouts: 8.26 us -> 3.93 us
    reduce_scatter x1 -> x0, waiting for transfers between devices: 112 us -> none  [on_device(): lax.psum_scatter(jnp.einsum('erf,efd->red', portion, down_weight, preferr...]
    all_gather x2 -> x0, waiting for transfers between devices: 100 us -> none  [the longest x1 50.8 us: on_device(): rows_grad = lax.all_gather(got_grad, 'dp', axis=2, tiled=True)[0]]
    ppermute x0 -> x30, waiting for transfers between devices: none -> 87.4 us  [the longest x12 56.3 us: ring_y(): return lax.ppermute(value, 'dp', perm)]
    ppermute x0 -> x30, starting transfers between devices: none -> 37.8 us  [the longest x12 16.7 us: ring_y(): return lax.ppermute(value, 'dp', perm)]
    all_to_all x2 -> x0, blocking collectives: 21.6 us -> none  [the longest x1 11.6 us: on_device(): lax.all_to_all(pack_rows(tokens), 'expert', split_axis=0, concat_axis=2,...]
    dot_general x1, matrix products: 5.33 us -> 1.85 us  [on_device(): jnp.einsum('erd,edf->erf', rows_tok, up_weight, preferred_element_type=jn...]
    all_to_all x1 -> x0, starting transfers between devices: 3.46 us -> none  [on_device(): lax.all_to_all(sendback, 'expert', split_axis=0, concat_axis=0, tiled=True)]
    scatter x2 -> x0, local copies, waits for them, and re-layouts: 3.37 us -> none  [pack_rows(): jnp.zeros((all_experts * capacity, width), values.dtype).at[target]]
  transfers between devices with their start and end apart: 4 -> 30, of which waited for: 4 -> 17; matrix products, arithmetic and copies ran while one was open for 11% -> 16% of each run, Pallas kernels for 0% -> 0%
where the time goes in v1:
time: 158 us
  waiting for transfers between devices  87.4 us (55%)
  starting transfers between devices  37.8 us (24%)
  matrix products  23.1 us (15%)
  other arithmetic  4.75 us (3%)
  local copies, waits for them, and re-layouts  3.93 us (2%)
    ppermute x12, waiting for transfers between devices, ring_y(): return lax.ppermute(value, 'dp', perm)  56.3 us
    ppermute x9, waiting for transfers between devices, ring_z(): return lax.ppermute(value, 'dp', perm)  22.4 us
    ppermute x12, starting transfers between devices, ring_y(): return lax.ppermute(value, 'dp', perm)  16.7 us
    ppermute x9, starting transfers between devices, ring_z(): return lax.ppermute(value, 'dp', perm)  12.9 us
    dot_general x1, matrix products, on_device(): jnp.einsum('erd,erf->edf', rows_tok, pre_grad, preferred_element_type=jnp...  12 us
    ppermute x9, waiting for transfers between devices, swap_expert(): return lax.ppermute(value, 'expert', [(i, i ^ mask) for i in range(n)])  8.58 us
    ppermute x9, starting transfers between devices, swap_expert(): return lax.ppermute(value, 'expert', [(i, i ^ mask) for i in range(n)])  8.17 us
    dot_general x1, matrix products, on_device(): jnp.einsum('erf,erd->efd', active, rows_grad, preferred_element_type=jnp....  4.76 us
  transfers between devices with their start and end apart: 30, of which 17 were waited for; matrix products, arithmetic and copies ran while one was open for 16% of the time, Pallas kernels for 0%

profile of v1, /device:TPU:0, one launch (start us, length us, event | category | flops | bytes accessed | tf_op | source)
XLA Modules:
  0.0 158.0 jit_solution(12113734432371664386)
XLA Ops:
  2.5 2.4 %collective-permute-start.2 = (bf16[4,10,1280]{2,1,0:T(8,128)(2,1)S(1)}, bf16[4,10,1280]{2,1,0:T(8,128)(2,1)S(1)}, u32[]{:S(2)}, u32[]{:S(2)}) collective-permute-start(bf16[4,10,1280]{2,1,0:T(8,128)(2,1)S(1)} %squeeze.32), channel_id=1, source_target_pairs={{0,24},{8,16},{16,8},{24,0},{1,25},{9,17},{17,9},{25,1},{2,26},{10... | collective-permute-start | bytes 307208 | tf_op jit(solution)/shard_map/ppermute | solution.py:47
  10.4 3.7 %collective-permute-done.1 = bf16[4,10,1280]{2,1,0:T(8,128)(2,1)S(1)} collective-permute-done((bf16[4,10,1280]{2,1,0:T(8,128)(2,1)S(1)}, bf16[4,10,1280]{2,1,0:T(8,128)(2,1)S(1)}, u32[]{:S(2)}, u32[]{:S(2)}) %collective-permute-start.1) | collective-permute-done | bytes 102432 | tf_op jit(solution)/shard_map/ppermute | solution.py:47
  16.6 3.7 %collective-permute-done.21 = bf16[4,10,1280]{2,1,0:T(8,128)(2,1)S(1)} collective-permute-done((bf16[4,10,1280]{2,1,0:T(8,128)(2,1)S(1)}, bf16[4,10,1280]{2,1,0:T(8,128)(2,1)S(1)}, u32[]{:S(2)}, u32[]{:S(2)}) %collective-permute-start.21) | collective-permute-done | bytes 102432 | tf_op jit(solution)/shard_map/ppermute | solution.py:47
  20.7 2.4 %collective-permute-start.24 = (bf16[4,40,1280]{2,1,0:T(8,128)(2,1)S(1)}, bf16[4,40,1280]{2,1,0:T(8,128)(2,1)S(1)}, u32[]{:S(2)}, u32[]{:S(2)}) collective-permute-start(bf16[4,40,1280]{2,1,0:T(8,128)(2,1)S(1)} %get-tuple-element.7), channel_id=1, source_target_pairs={{0,2},{1,3},{2,4},{3,5},{4,6},{5,7},{6,0},{7,1},{8,10},{9,11},{10,... | collective-permute-start | bytes 1228808 | tf_op jit(solution)/shard_map/ppermute | solution.py:35
  25.1 3.5 %collective-permute-done.4 = bf16[4,40,1280]{2,1,0:T(8,128)(2,1)S(1)} collective-permute-done((bf16[4,40,1280]{2,1,0:T(8,128)(2,1)S(1)}, bf16[4,40,1280]{2,1,0:T(8,128)(2,1)S(1)}, u32[]{:S(2)}, u32[]{:S(2)}) %collective-permute-start.4) | collective-permute-done | bytes 409632 | tf_op jit(solution)/shard_map/ppermute | solution.py:35
  30.2 7.2 %collective-permute-done.24 = bf16[4,40,1280]{2,1,0:T(8,128)(2,1)S(1)} collective-permute-done((bf16[4,40,1280]{2,1,0:T(8,128)(2,1)S(1)}, bf16[4,40,1280]{2,1,0:T(8,128)(2,1)S(1)}, u32[]{:S(2)}, u32[]{:S(2)}) %collective-permute-start.24) | collective-permute-done | bytes 409632 | tf_op jit(solution)/shard_map/ppermute | solution.py:35
  39.0 5.2 %collective-permute-done.23 = bf16[4,40,1280]{2,1,0:T(8,128)(2,1)S(1)} collective-permute-done((bf16[4,40,1280]{2,1,0:T(8,128)(2,1)S(1)}, bf16[4,40,1280]{2,1,0:T(8,128)(2,1)S(1)}, u32[]{:S(2)}, u32[]{:S(2)}) %collective-permute-start.23) | collective-permute-done | bytes 409632 | tf_op jit(solution)/shard_map/ppermute | solution.py:42
  44.3 1.9 %collective-permute-done.6 = bf16[4,40,1280]{2,1,0:T(8,128)(2,1)S(1)} collective-permute-done((bf16[4,40,1280]{2,1,0:T(8,128)(2,1)S(1)}, bf16[4,40,1280]{2,1,0:T(8,128)(2,1)S(1)}, u32[]{:S(2)}, u32[]{:S(2)}) %collective-permute-start.6) | collective-permute-done | bytes 409632 | tf_op jit(solution)/shard_map/ppermute | solution.py:35
  47.7 5.3 %collective-permute-done.5 = bf16[4,40,1280]{2,1,0:T(8,128)(2,1)S(1)} collective-permute-done((bf16[4,40,1280]{2,1,0:T(8,128)(2,1)S(1)}, bf16[4,40,1280]{2,1,0:T(8,128)(2,1)S(1)}, u32[]{:S(2)}, u32[]{:S(2)}) %collective-permute-start.5) | collective-permute-done | bytes 409632 | tf_op jit(solution)/shard_map/ppermute | solution.py:42
  53.1 9.8 %collective-permute-done.8 = bf16[4,40,1280]{2,1,0:T(8,128)(2,1)S(1)} collective-permute-done((bf16[4,40,1280]{2,1,0:T(8,128)(2,1)S(1)}, bf16[4,40,1280]{2,1,0:T(8,128)(2,1)S(1)}, u32[]{:S(2)}, u32[]{:S(2)}) %collective-permute-start.8) | collective-permute-done | bytes 409632 | tf_op jit(solution)/shard_map/ppermute | solution.py:35
  64.4 6.2 %collective-permute-done.7 = bf16[4,40,1280]{2,1,0:T(8,128)(2,1)S(1)} collective-permute-done((bf16[4,40,1280]{2,1,0:T(8,128)(2,1)S(1)}, bf16[4,40,1280]{2,1,0:T(8,128)(2,1)S(1)}, u32[]{:S(2)}, u32[]{:S(2)}) %collective-permute-start.7) | collective-permute-done | bytes 409632 | tf_op jit(solution)/shard_map/ppermute | solution.py:42
  70.7 7.5 %collective-permute-done.9 = bf16[4,40,1280]{2,1,0:T(8,128)(2,1)S(1)} collective-permute-done((bf16[4,40,1280]{2,1,0:T(8,128)(2,1)S(1)}, bf16[4,40,1280]{2,1,0:T(8,128)(2,1)S(1)}, u32[]{:S(2)}, u32[]{:S(2)}) %collective-permute-start.9) | collective-permute-done | bytes 409632 | tf_op jit(solution)/shard_map/ppermute | solution.py:42
  79.9 1.8 %fusion.31 = f32[4,320,512]{2,1,0:T(8,128)S(1)} fusion(bf16[4,320,1280]{2,1,0:T(8,128)(2,1)S(1)} %constant_dynamic-update-slice_fusion, bf16[4,1280,512]{2,1,0:T(8,128)(2,1)S(1)} %bitcast.41), kind=kOutput, calls=%fused_computation.75 | convolution fusion | flops 1677721600 | bytes 11141120 | tf_op jit(solution)/shard_map/erd,edf->erf/dot_general | solution.py:109
  82.0 2.0 %fusion.30 = (bf16[4,320,1280]{2,1,0:T(8,128)(2,1)S(1)}, f32[4,320,1280]{2,1,0:T(8,128)S(1)}) fusion(bf16[4,512,1280]{2,1,0:T(8,128)(2,1)S(1)} %bitcast.30, f32[4,320,512]{2,1,0:T(8,128)S(1)} %fusion.31), kind=kOutput, calls=%fused_computation.74 | convolution fusion | flops 1685258240 | bytes 17694720 | tf_op jit(solution)/shard_map/erf,efd->erd/dot_general | solution.py:111
  89.5 7.1 %collective-permute-done.10 = bf16[4,40,1280]{2,1,0:T(8,128)(2,1)S(1)} collective-permute-done((bf16[4,40,1280]{2,1,0:T(8,128)(2,1)S(1)}, bf16[4,40,1280]{2,1,0:T(8,128)(2,1)S(1)}, u32[]{:S(2)}, u32[]{:S(2)}) %collective-permute-start.10) | collective-permute-done | bytes 409632 | tf_op jit(solution)/shard_map/ppermute | solution.py:42
  96.7 2.4 %collective-permute-start.11 = (bf16[4,40,1280]{2,1,0:T(8,128)(2,1)S(1)}, bf16[4,40,1280]{2,1,0:T(8,128)(2,1)S(1)}, u32[]{:S(2)}, u32[]{:S(2)}) collective-permute-start(bf16[4,40,1280]{2,1,0:T(8,128)(2,1)S(1)} %fusion.13), channel_id=1, source_target_pairs={{0,6},{1,7},{2,0},{3,1},{4,2},{5,3},{6,4},{7,5},{8,14},{9,15},{10,... | collective-permute-start | bytes 1228808 | tf_op jit(solution)/shard_map/ppermute | solution.py:35
  100.7 4.6 %collective-permute-done.27 = bf16[4,40,1280]{2,1,0:T(8,128)(2,1)S(1)} collective-permute-done((bf16[4,40,1280]{2,1,0:T(8,128)(2,1)S(1)}, bf16[4,40,1280]{2,1,0:T(8,128)(2,1)S(1)}, u32[]{:S(2)}, u32[]{:S(2)}) %collective-permute-start.27) | collective-permute-done | bytes 409632 | tf_op jit(solution)/shard_map/ppermute | solution.py:42
  107.0 7.2 %collective-permute-done.12 = bf16[4,40,1280]{2,1,0:T(8,128)(2,1)S(1)} collective-permute-done((bf16[4,40,1280]{2,1,0:T(8,128)(2,1)S(1)}, bf16[4,40,1280]{2,1,0:T(8,128)(2,1)S(1)}, u32[]{:S(2)}, u32[]{:S(2)}) %collective-permute-start.12) | collective-permute-done | bytes 409632 | tf_op jit(solution)/shard_map/ppermute | solution.py:42
  114.3 2.4 %collective-permute-start.13 = (bf16[4,40,1280]{2,1,0:T(8,128)(2,1)S(1)}, bf16[4,40,1280]{2,1,0:T(8,128)(2,1)S(1)}, u32[]{:S(2)}, u32[]{:S(2)}) collective-permute-start(bf16[4,40,1280]{2,1,0:T(8,128)(2,1)S(1)} %fusion.12), channel_id=1, source_target_pairs={{0,6},{1,7},{2,0},{3,1},{4,2},{5,3},{6,4},{7,5},{8,14},{9,15},{10,... | collective-permute-start | bytes 1228808 | tf_op jit(solution)/shard_map/ppermute | solution.py:35
  118.3 4.6 %collective-permute-done.29 = bf16[4,40,1280]{2,1,0:T(8,128)(2,1)S(1)} collective-permute-done((bf16[4,40,1280]{2,1,0:T(8,128)(2,1)S(1)}, bf16[4,40,1280]{2,1,0:T(8,128)(2,1)S(1)}, u32[]{:S(2)}, u32[]{:S(2)}) %collective-permute-start.29) | collective-permute-done | bytes 409632 | tf_op jit(solution)/shard_map/ppermute | solution.py:42
  123.0 8.7 %collective-permute-done.14 = bf16[4,40,1280]{2,1,0:T(8,128)(2,1)S(1)} collective-permute-done((bf16[4,40,1280]{2,1,0:T(8,128)(2,1)S(1)}, bf16[4,40,1280]{2,1,0:T(8,128)(2,1)S(1)}, u32[]{:S(2)}, u32[]{:S(2)}) %collective-permute-start.14) | collective-permute-done | bytes 409632 | tf_op jit(solution)/shard_map/ppermute | solution.py:42
  132.6 2.4 %collective-permute-start.15 = (bf16[4,40,1280]{2,1,0:T(8,128)(2,1)}, bf16[4,40,1280]{2,1,0:T(8,128)(2,1)}, u32[]{:S(2)}, u32[]{:S(2)}) collective-permute-start(bf16[4,40,1280]{2,1,0:T(8,128)(2,1)} %fusion.10), channel_id=1, source_target_pairs={{0,6},{1,7},{2,0},{3,1},{4,2},{5,3},{6,4},{7,5},{8,14},{9,15},{10,... | collective-permute-start | bytes 1228808 | tf_op jit(solution)/shard_map/ppermute | solution.py:35
  135.0 12.0 %convolution_convert_fusion.1 = bf16[4,1280,512]{2,1,0:T(8,128)(2,1)} fusion(bf16[4,320,1280]{2,1,0:T(8,128)(2,1)} %copy-done.2, f32[4,320,512]{2,1,0:T(8,128)S(1)} %fusion.31, bf16[4,320,1280]{2,1,0:T(8,128)(2,1)} %copy-done.3, bf16[4,512,1280]{2,1,0:T(8,128)(2,1)} %param.8), kind=kOutput, calls=%fused_computation.1 | convolution fusion | flops 3370516480 | bytes 19660800 | tf_op jit(solution)/shard_map/erd,erf->edf/dot_general | solution.py:126
  150.9 4.8 %convolution_convert_fusion = bf16[4,512,1280]{2,1,0:T(8,128)(2,1)} fusion(bf16[4,320,1280]{2,1,0:T(8,128)(2,1)S(1)} %copy-done.4, f32[4,320,512]{2,1,0:T(8,128)S(1)} %fusion.31), kind=kOutput, calls=%fused_computation | convolution fusion | flops 1686241280 | bytes 11141120 | tf_op jit(solution)/shard_map/erf,erd->efd/dot_general | solution.py:123
  (105 shorter events, 38.1 us)
Async XLA Ops:
  7.2 9.4 %collective-permute-start.22 = (bf16[4,10,1280]{2,1,0:T(8,128)(2,1)S(1)}, bf16[4,10,1280]{2,1,0:T(8,128)(2,1)S(1)}, u32[]{:S(2)}, u32[]{:S(2)}) collective-permute-start(bf16[4,10,1280]{2,1,0:T(8,128)(2,1)S(1)} %squeeze.39), channel_id=1, source_target_pairs={{0,24},{8,16},{16,8},{24,0},{1,25},{9,17},{17,9},{25,1},{2,26},{10... | collective-permute-start | bytes 307208 | tf_op jit(solution)/shard_map/ppermute | solution.py:47
  8.7 11.5 %collective-permute-start.21 = (bf16[4,10,1280]{2,1,0:T(8,128)(2,1)S(1)}, bf16[4,10,1280]{2,1,0:T(8,128)(2,1)S(1)}, u32[]{:S(2)}, u32[]{:S(2)}) collective-permute-start(bf16[4,10,1280]{2,1,0:T(8,128)(2,1)S(1)} %squeeze.38), channel_id=1, source_target_pairs={{0,16},{8,24},{16,0},{24,8},{1,17},{9,25},{17,1},{25,9},{2,18},{10... | collective-permute-start | bytes 307208 | tf_op jit(solution)/shard_map/ppermute | solution.py:47
  9.6 10.7 %collective-permute-start.20 = (bf16[4,10,1280]{2,1,0:T(8,128)(2,1)S(1)}, bf16[4,10,1280]{2,1,0:T(8,128)(2,1)S(1)}, u32[]{:S(2)}, u32[]{:S(2)}) collective-permute-start(bf16[4,10,1280]{2,1,0:T(8,128)(2,1)S(1)} %squeeze.37), channel_id=1, source_target_pairs={{0,8},{8,0},{16,24},{24,16},{1,9},{9,1},{17,25},{25,17},{2,10},{10... | collective-permute-start | bytes 307208 | tf_op jit(solution)/shard_map/ppermute | solution.py:47
  14.5 14.2 %collective-permute-start.4 = (bf16[4,40,1280]{2,1,0:T(8,128)(2,1)S(1)}, bf16[4,40,1280]{2,1,0:T(8,128)(2,1)S(1)}, u32[]{:S(2)}, u32[]{:S(2)}) collective-permute-start(bf16[4,40,1280]{2,1,0:T(8,128)(2,1)S(1)} %get-tuple-element.17), channel_id=1, source_target_pairs={{0,2},{1,3},{2,4},{3,5},{4,6},{5,7},{6,0},{7,1},{8,10},{9,11},{10,... | collective-permute-start | bytes 1228808 | tf_op jit(solution)/shard_map/ppermute | solution.py:35
  20.7 16.7 %collective-permute-start.24 = (bf16[4,40,1280]{2,1,0:T(8,128)(2,1)S(1)}, bf16[4,40,1280]{2,1,0:T(8,128)(2,1)S(1)}, u32[]{:S(2)}, u32[]{:S(2)}) collective-permute-start(bf16[4,40,1280]{2,1,0:T(8,128)(2,1)S(1)} %get-tuple-element.7), channel_id=1, source_target_pairs={{0,2},{1,3},{2,4},{3,5},{4,6},{5,7},{6,0},{7,1},{8,10},{9,11},{10,... | collective-permute-start | bytes 1228808 | tf_op jit(solution)/shard_map/ppermute | solution.py:35
  23.1 15.9 %collective-permute-start.3 = (bf16[4,40,1280]{2,1,0:T(8,128)(2,1)S(1)}, bf16[4,40,1280]{2,1,0:T(8,128)(2,1)S(1)}, u32[]{:S(2)}, u32[]{:S(2)}) collective-permute-start(bf16[4,40,1280]{2,1,0:T(8,128)(2,1)S(1)} %get-tuple-element.17), channel_id=1, source_target_pairs={{0,1},{1,0},{2,3},{3,2},{4,5},{5,4},{6,7},{7,6},{8,9},{9,8},{10,11... | collective-permute-start | bytes 1228808 | tf_op jit(solution)/shard_map/ppermute | solution.py:42
  24.6 19.6 %collective-permute-start.23 = (bf16[4,40,1280]{2,1,0:T(8,128)(2,1)S(1)}, bf16[4,40,1280]{2,1,0:T(8,128)(2,1)S(1)}, u32[]{:S(2)}, u32[]{:S(2)}) collective-permute-start(bf16[4,40,1280]{2,1,0:T(8,128)(2,1)S(1)} %get-tuple-element.7), channel_id=1, source_target_pairs={{0,1},{1,0},{2,3},{3,2},{4,5},{5,4},{6,7},{7,6},{8,9},{9,8},{10,11... | collective-permute-start | bytes 1228808 | tf_op jit(solution)/shard_map/ppermute | solution.py:42
  28.6 24.4 %collective-permute-start.5 = (bf16[4,40,1280]{2,1,0:T(8,128)(2,1)S(1)}, bf16[4,40,1280]{2,1,0:T(8,128)(2,1)S(1)}, u32[]{:S(2)}, u32[]{:S(2)}) collective-permute-start(bf16[4,40,1280]{2,1,0:T(8,128)(2,1)S(1)} %collective-permute-done.4), channel_id=1, source_target_pairs={{0,1},{1,0},{2,3},{3,2},{4,5},{5,4},{6,7},{7,6},{8,9},{9,8},{10,11... | collective-permute-start | bytes 1228808 | tf_op jit(solution)/shard_map/ppermute | solution.py:42
  30.2 16.0 %collective-permute-start.6 = (bf16[4,40,1280]{2,1,0:T(8,128)(2,1)S(1)}, bf16[4,40,1280]{2,1,0:T(8,128)(2,1)S(1)}, u32[]{:S(2)}, u32[]{:S(2)}) collective-permute-start(bf16[4,40,1280]{2,1,0:T(8,128)(2,1)S(1)} %collective-permute-done.4), channel_id=1, source_target_pairs={{0,2},{1,3},{2,4},{3,5},{4,6},{5,7},{6,0},{7,1},{8,10},{9,11},{10,... | collective-permute-start | bytes 1228808 | tf_op jit(solution)/shard_map/ppermute | solution.py:35
  37.4 50.5 %collective-permute-start.25 = (bf16[4,40,1280]{2,1,0:T(8,128)(2,1)S(1)}, bf16[4,40,1280]{2,1,0:T(8,128)(2,1)S(1)}, u32[]{:S(2)}, u32[]{:S(2)}) collective-permute-start(bf16[4,40,1280]{2,1,0:T(8,128)(2,1)S(1)} %collective-permute-done.24), channel_id=1, source_target_pairs={{0,1},{1,0},{2,3},{3,2},{4,5},{5,4},{6,7},{7,6},{8,9},{9,8},{10,11... | collective-permute-start | bytes 1228808 | tf_op jit(solution)/shard_map/ppermute | solution.py:42
  39.0 46.8 %collective-permute-start.26 = (bf16[4,40,1280]{2,1,0:T(8,128)(2,1)S(1)}, bf16[4,40,1280]{2,1,0:T(8,128)(2,1)S(1)}, u32[]{:S(2)}, u32[]{:S(2)}) collective-permute-start(bf16[4,40,1280]{2,1,0:T(8,128)(2,1)S(1)} %collective-permute-done.24), channel_id=1, source_target_pairs={{0,2},{1,3},{2,4},{3,5},{4,6},{5,7},{6,0},{7,1},{8,10},{9,11},{10,... | collective-permute-start | bytes 1228808 | tf_op jit(solution)/shard_map/ppermute | solution.py:35
  46.2 24.4 %collective-permute-start.7 = (bf16[4,40,1280]{2,1,0:T(8,128)(2,1)S(1)}, bf16[4,40,1280]{2,1,0:T(8,128)(2,1)S(1)}, u32[]{:S(2)}, u32[]{:S(2)}) collective-permute-start(bf16[4,40,1280]{2,1,0:T(8,128)(2,1)S(1)} %collective-permute-done.6), channel_id=1, source_target_pairs={{0,1},{1,0},{2,3},{3,2},{4,5},{5,4},{6,7},{7,6},{8,9},{9,8},{10,11... | collective-permute-start | bytes 1228808 | tf_op jit(solution)/shard_map/ppermute | solution.py:42
  47.7 15.2 %collective-permute-start.8 = (bf16[4,40,1280]{2,1,0:T(8,128)(2,1)S(1)}, bf16[4,40,1280]{2,1,0:T(8,128)(2,1)S(1)}, u32[]{:S(2)}, u32[]{:S(2)}) collective-permute-start(bf16[4,40,1280]{2,1,0:T(8,128)(2,1)S(1)} %collective-permute-done.6), channel_id=1, source_target_pairs={{0,2},{1,3},{2,4},{3,5},{4,6},{5,7},{6,0},{7,1},{8,10},{9,11},{10,... | collective-permute-start | bytes 1228808 | tf_op jit(solution)/shard_map/ppermute | solution.py:35
  62.9 15.2 %collective-permute-start.9 = (bf16[4,40,1280]{2,1,0:T(8,128)(2,1)S(1)}, bf16[4,40,1280]{2,1,0:T(8,128)(2,1)S(1)}, u32[]{:S(2)}, u32[]{:S(2)}) collective-permute-start(bf16[4,40,1280]{2,1,0:T(8,128)(2,1)S(1)} %collective-permute-done.8), channel_id=1, source_target_pairs={{0,1},{1,0},{2,3},{3,2},{4,5},{5,4},{6,7},{7,6},{8,9},{9,8},{10,11... | collective-permute-start | bytes 1228808 | tf_op jit(solution)/shard_map/ppermute | solution.py:42
  84.1 12.5 %collective-permute-start.10 = (bf16[4,40,1280]{2,1,0:T(8,128)(2,1)S(1)}, bf16[4,40,1280]{2,1,0:T(8,128)(2,1)S(1)}, u32[]{:S(2)}, u32[]{:S(2)}) collective-permute-start(bf16[4,40,1280]{2,1,0:T(8,128)(2,1)S(1)} %get-tuple-element.3), channel_id=1, source_target_pairs={{0,1},{1,0},{2,3},{3,2},{4,5},{5,4},{6,7},{7,6},{8,9},{9,8},{10,11... | collective-permute-start | bytes 1228808 | tf_op jit(solution)/shard_map/ppermute | solution.py:42
  85.7 19.6 %collective-permute-start.27 = (bf16[4,40,1280]{2,1,0:T(8,128)(2,1)S(1)}, bf16[4,40,1280]{2,1,0:T(8,128)(2,1)S(1)}, u32[]{:S(2)}, u32[]{:S(2)}) collective-permute-start(bf16[4,40,1280]{2,1,0:T(8,128)(2,1)S(1)} %collective-permute-done.26), channel_id=1, source_target_pairs={{0,1},{1,0},{2,3},{3,2},{4,5},{5,4},{6,7},{7,6},{8,9},{9,8},{10,11... | collective-permute-start | bytes 1228808 | tf_op jit(solution)/shard_map/ppermute | solution.py:42
  86.3 12.8 %collective-permute-start.28 = (bf16[4,40,1280]{2,1,0:T(8,128)(2,1)S(1)}, bf16[4,40,1280]{2,1,0:T(8,128)(2,1)S(1)}, u32[]{:S(2)}, u32[]{:S(2)}) collective-permute-start(bf16[4,40,1280]{2,1,0:T(8,128)(2,1)S(1)} %collective-permute-done.26), channel_id=1, source_target_pairs={{0,2},{1,3},{2,4},{3,5},{4,6},{5,7},{6,0},{7,1},{8,10},{9,11},{10,... | collective-permute-start | bytes 1228808 | tf_op jit(solution)/shard_map/ppermute | solution.py:35
  87.9 26.2 %collective-permute-start.12 = (bf16[4,40,1280]{2,1,0:T(8,128)(2,1)S(1)}, bf16[4,40,1280]{2,1,0:T(8,128)(2,1)S(1)}, u32[]{:S(2)}, u32[]{:S(2)}) collective-permute-start(bf16[4,40,1280]{2,1,0:T(8,128)(2,1)S(1)} %get-tuple-element.6), channel_id=1, source_target_pairs={{0,1},{1,0},{2,3},{3,2},{4,5},{5,4},{6,7},{7,6},{8,9},{9,8},{10,11... | collective-permute-start | bytes 1228808 | tf_op jit(solution)/shard_map/ppermute | solution.py:42
  96.7 17.5 %collective-permute-start.11 = (bf16[4,40,1280]{2,1,0:T(8,128)(2,1)S(1)}, bf16[4,40,1280]{2,1,0:T(8,128)(2,1)S(1)}, u32[]{:S(2)}, u32[]{:S(2)}) collective-permute-start(bf16[4,40,1280]{2,1,0:T(8,128)(2,1)S(1)} %fusion.13), channel_id=1, source_target_pairs={{0,6},{1,7},{2,0},{3,1},{4,2},{5,3},{6,4},{7,5},{8,14},{9,15},{10,... | collective-permute-start | bytes 1228808 | tf_op jit(solution)/shard_map/ppermute | solution.py:35
  99.2 23.8 %collective-permute-start.29 = (bf16[4,40,1280]{2,1,0:T(8,128)(2,1)S(1)}, bf16[4,40,1280]{2,1,0:T(8,128)(2,1)S(1)}, u32[]{:S(2)}, u32[]{:S(2)}) collective-permute-start(bf16[4,40,1280]{2,1,0:T(8,128)(2,1)S(1)} %collective-permute-done.28), channel_id=1, source_target_pairs={{0,1},{1,0},{2,3},{3,2},{4,5},{5,4},{6,7},{7,6},{8,9},{9,8},{10,11... | collective-permute-start | bytes 1228808 | tf_op jit(solution)/shard_map/ppermute | solution.py:42
  105.4 26.3 %collective-permute-start.14 = (bf16[4,40,1280]{2,1,0:T(8,128)(2,1)S(1)}, bf16[4,40,1280]{2,1,0:T(8,128)(2,1)S(1)}, u32[]{:S(2)}, u32[]{:S(2)}) collective-permute-start(bf16[4,40,1280]{2,1,0:T(8,128)(2,1)S(1)} %get-tuple-element.5), channel_id=1, source_target_pairs={{0,1},{1,0},{2,3},{3,2},{4,5},{5,4},{6,7},{7,6},{8,9},{9,8},{10,11... | collective-permute-start | bytes 1228808 | tf_op jit(solution)/shard_map/ppermute | solution.py:42
  114.3 17.4 %collective-permute-start.13 = (bf16[4,40,1280]{2,1,0:T(8,128)(2,1)S(1)}, bf16[4,40,1280]{2,1,0:T(8,128)(2,1)S(1)}, u32[]{:S(2)}, u32[]{:S(2)}) collective-permute-start(bf16[4,40,1280]{2,1,0:T(8,128)(2,1)S(1)} %fusion.12), channel_id=1, source_target_pairs={{0,6},{1,7},{2,0},{3,1},{4,2},{5,3},{6,4},{7,5},{8,14},{9,15},{10,... | collective-permute-start | bytes 1228808 | tf_op jit(solution)/shard_map/ppermute | solution.py:35
  116.8 30.2 %collective-permute-start.16 = (bf16[4,40,1280]{2,1,0:T(8,128)(2,1)S(1)}, bf16[4,40,1280]{2,1,0:T(8,128)(2,1)}, u32[]{:S(2)}, u32[]{:S(2)}) collective-permute-start(bf16[4,40,1280]{2,1,0:T(8,128)(2,1)S(1)} %get-tuple-element.4), channel_id=1, source_target_pairs={{0,1},{1,0},{2,3},{3,2},{4,5},{5,4},{6,7},{7,6},{8,9},{9,8},{10,11... | collective-permute-start | bytes 1228808 | tf_op jit(solution)/shard_map/ppermute | solution.py:42
  132.6 14.4 %collective-permute-start.15 = (bf16[4,40,1280]{2,1,0:T(8,128)(2,1)}, bf16[4,40,1280]{2,1,0:T(8,128)(2,1)}, u32[]{:S(2)}, u32[]{:S(2)}) collective-permute-start(bf16[4,40,1280]{2,1,0:T(8,128)(2,1)} %fusion.10), channel_id=1, source_target_pairs={{0,6},{1,7},{2,0},{3,1},{4,2},{5,3},{6,4},{7,5},{8,14},{9,15},{10,... | collective-permute-start | bytes 1228808 | tf_op jit(solution)/shard_map/ppermute | solution.py:35
  (15 other events, 239.6 us)

commit v2 on v1

--- a/solution.py
+++ b/solution.py
@@ -51,30 +51,49 @@
     return [packed[0]] + [swap_expert(packed[m], m) for m in range(1, packed.shape[0])]
 
 
+def after(value, *earlier):
+    return lax.optimization_barrier((value, *earlier))[0]
+
+
 def gather_dp(block):
     rows, cols = grid_of(lax.axis_size("dp"))
+    half = block.shape[0] // 2
     blocks = []
     for k in range(rows):
+        if k > 0:
+            block = ring_z(block, 1)
         line = [block]
-        for _ in range(cols - 1):
-            line.append(ring_y(line[-1], 1))
+        if cols == 2 and k > 0 and k == rows - 1 and half > 0:
+            low = ring_y(block[:half], 1)
+            high = ring_z(blocks[k - 1][1][half:], 1)
+            line.append(jnp.concatenate([low, high], axis=0))
+        else:
+            for _ in range(cols - 1):
+                line.append(ring_y(line[-1], 1))
         blocks.append(line)
-        if k < rows - 1:
-            block = ring_z(block, 1)
     return blocks
 
 
 def scatter_dp(parts):
     rows, cols = grid_of(lax.axis_size("dp"))
+    parts = [list(line) for line in parts]
+    half = parts[0][0].shape[0] // 2
+
+    def moved(ring, value):
+        return ring(value.astype(jnp.bfloat16), -1).astype(jnp.float32)
+
     total = None
     for k in reversed(range(rows)):
-        line = parts[k][cols - 1]
-        for j in reversed(range(cols - 1)):
-            line = ring_y(line.astype(jnp.bfloat16), -1).astype(jnp.float32) + parts[k][j]
-        if total is None:
-            total = line
+        if cols == 2 and k > 0 and k == rows - 1 and half > 0:
+            low = moved(ring_y, parts[k][1][:half]) + parts[k][0][:half]
+            high = moved(ring_z, parts[k][1][half:]) + parts[k - 1][1][half:]
+            line = jnp.concatenate([low, parts[k][0][half:]], axis=0)
+            parts[k - 1][1] = jnp.concatenate([parts[k - 1][1][:half], high], axis=0)
         else:
-            total = ring_z(total.astype(jnp.bfloat16), -1).astype(jnp.float32) + line
+            line = parts[k][cols - 1]
+            for j in reversed(range(cols - 1)):
+                line = moved(ring_y, line) + parts[k][j]
+        total = line if total is None else moved(ring_z, total) + line
     return total
 
 
@@ -103,11 +122,15 @@
     def rows_of(blocks):
         return jnp.concatenate([b for line in blocks for b in line], axis=1)
 
-    rows_tok = rows_of(gather_dp(dispatch(tokens)))
-    rows_grad = rows_of(gather_dp(dispatch(out_grad)))
+    blocks_tok = gather_dp(dispatch(tokens))
+    rows_tok = rows_of(blocks_tok)
+    block_grad = after(dispatch(out_grad), blocks_tok[rows - 1][0])
+    rows_grad = rows_of(gather_dp(block_grad))
 
     hidden_pre = jnp.einsum("erd,edf->erf", rows_tok, up_weight, preferred_element_type=jnp.float32)
+    hidden_pre = lax.optimization_barrier(hidden_pre)
     active = gelu_value(hidden_pre).astype(jnp.bfloat16)
+    active, slope = lax.optimization_barrier((active, gelu_slope(hidden_pre)))
     part = jnp.einsum("erf,efd->erd", active, down_weight, preferred_element_type=jnp.float32)
     part = jnp.split(part, rows * cols, axis=1)
     summed = scatter_dp([part[k * cols : (k + 1) * cols] for k in range(rows)]).astype(jnp.bfloat16)
@@ -119,7 +142,7 @@
     back_grad = jnp.einsum(
         "erd,efd->erf", rows_grad, down_weight, preferred_element_type=jnp.float32
     )
-    pre_grad = (back_grad * gelu_slope(hidden_pre)).astype(jnp.bfloat16)
+    pre_grad = lax.optimization_barrier((back_grad * slope).astype(jnp.bfloat16))
     down_part = jnp.einsum(
         "erf,erd->efd", active, rows_grad, preferred_element_type=jnp.float32
     ).astype(jnp.bfloat16)

time: 158 us -> 165 us (1.044)
  waiting for transfers between devices: 87.4 us -> 97.7 us
  starting transfers between devices: 37.8 us -> 31.3 us
  local copies, waits for them, and re-layouts: 3.93 us -> 7.29 us
  matrix products: 23.1 us -> 21.4 us
    ppermute x9 -> x12, waiting for transfers between devices: 22.4 us -> 56.5 us  [ring_z(): return lax.ppermute(value, 'dp', perm)]
    ppermute x12, waiting for transfers between devices: 56.3 us -> 27.2 us  [ring_y(): return lax.ppermute(value, 'dp', perm)]
    dot_general x1, matrix products: 12 us -> 4.65 us  [on_device(): jnp.einsum('erd,erf->edf', rows_tok, pre_grad, preferred_element_type=jnp...]
    ppermute x9, waiting for transfers between devices: 8.58 us -> 14 us  [swap_expert(): return lax.ppermute(value, 'expert', [(i, i ^ mask) for i in range(n)])]
    dot_general x1, matrix products: 1.85 us -> 5.85 us  [on_device(): jnp.einsum('erd,edf->erf', rows_tok, up_weight, preferred_element_type=jn...]
    ppermute x9 -> x12, starting transfers between devices: 12.9 us -> 9.64 us  [ring_z(): return lax.ppermute(value, 'dp', perm)]
    unnamed x30 -> x22, local copies, waits for them, and re-layouts: 2.26 us -> 4.87 us
    ppermute x12, starting transfers between devices: 16.7 us -> 14.5 us  [ring_y(): return lax.ppermute(value, 'dp', perm)]
  transfers between devices with their start and end apart: 30 -> 33, of which waited for: 17 -> 14; matrix products, arithmetic and copies ran while one was open for 16% -> 18% of each run, Pallas kernels for 0% -> 0%
where the time goes in v2:
time: 165 us; the launch traced here: 164 us
  waiting for transfers between devices  97.7 us (59%)
  starting transfers between devices  31.3 us (19%)
  matrix products  21.4 us (13%)
  local copies, waits for them, and re-layouts  7.29 us (4%)
  other arithmetic  5.1 us (3%)
    ppermute x12, waiting for transfers between devices, ring_z(): return lax.ppermute(value, 'dp', perm)  56.5 us
    ppermute x12, waiting for transfers between devices, ring_y(): return lax.ppermute(value, 'dp', perm)  27.2 us
    ppermute x12, starting transfers between devices, ring_y(): return lax.ppermute(value, 'dp', perm)  14.5 us
    ppermute x9, waiting for transfers between devices, swap_expert(): return lax.ppermute(value, 'expert', [(i, i ^ mask) for i in range(n)])  14 us
    ppermute x12, starting transfers between devices, ring_z(): return lax.ppermute(value, 'dp', perm)  9.64 us
    ppermute x9, starting transfers between devices, swap_expert(): return lax.ppermute(value, 'expert', [(i, i ^ mask) for i in range(n)])  7.24 us
    dot_general x1, matrix products, on_device(): jnp.einsum('erd,edf->erf', rows_tok, up_weight, preferred_element_type=jn...  5.85 us
    unnamed x22, local copies, waits for them, and re-layouts  4.87 us
  transfers between devices with their start and end apart: 33, of which 14 were waited for; matrix products, arithmetic and copies ran while one was open for 18% of the time, Pallas kernels for 0%

profile of v2, /device:TPU:0, one launch (start us, length us, event | category | flops | bytes accessed | tf_op | source)
XLA Modules:
  0.0 163.9 jit_solution(5201456884555684087)
XLA Ops:
  2.5 2.4 %collective-permute-start.2 = (bf16[4,10,1280]{2,1,0:T(8,128)(2,1)S(1)}, bf16[4,10,1280]{2,1,0:T(8,128)(2,1)S(1)}, u32[]{:S(2)}, u32[]{:S(2)}) collective-permute-start(bf16[4,10,1280]{2,1,0:T(8,128)(2,1)S(1)} %squeeze.32), channel_id=1, source_target_pairs={{0,24},{8,16},{16,8},{24,0},{1,25},{9,17},{17,9},{25,1},{2,26},{10... | collective-permute-start | bytes 307208 | tf_op jit(solution)/shard_map/ppermute | solution.py:47
  7.1 2.4 %collective-permute-done.2 = bf16[4,10,1280]{2,1,0:T(8,128)(2,1)S(1)} collective-permute-done((bf16[4,10,1280]{2,1,0:T(8,128)(2,1)S(1)}, bf16[4,10,1280]{2,1,0:T(8,128)(2,1)S(1)}, u32[]{:S(2)}, u32[]{:S(2)}) %collective-permute-start.2) | collective-permute-done | bytes 102432 | tf_op jit(solution)/shard_map/ppermute | solution.py:47
  9.5 3.7 %collective-permute-done.1 = bf16[4,10,1280]{2,1,0:T(8,128)(2,1)S(1)} collective-permute-done((bf16[4,10,1280]{2,1,0:T(8,128)(2,1)S(1)}, bf16[4,10,1280]{2,1,0:T(8,128)(2,1)S(1)}, u32[]{:S(2)}, u32[]{:S(2)}) %collective-permute-start.1) | collective-permute-done | bytes 102432 | tf_op jit(solution)/shard_map/ppermute | solution.py:47
  14.4 2.3 %collective-permute-start.3 = (bf16[4,40,1280]{2,1,0:T(8,128)(2,1)S(1)}, bf16[4,40,1280]{2,1,0:T(8,128)(2,1)S(1)}, u32[]{:S(2)}, u32[]{:S(2)}) collective-permute-start(bf16[4,40,1280]{2,1,0:T(8,128)(2,1)S(1)} %get-tuple-element.29), channel_id=1, source_target_pairs={{0,1},{1,0},{2,3},{3,2},{4,5},{5,4},{6,7},{7,6},{8,9},{9,8},{10,11... | collective-permute-start | bytes 1228808 | tf_op jit(solution)/shard_map/ppermute | solution.py:42
  20.6 4.3 %collective-permute-done.24 = bf16[4,10,1280]{2,1,0:T(8,128)(2,1)S(1)} collective-permute-done((bf16[4,10,1280]{2,1,0:T(8,128)(2,1)S(1)}, bf16[4,10,1280]{2,1,0:T(8,128)(2,1)S(1)}, u32[]{:S(2)}, u32[]{:S(2)}) %collective-permute-start.24) | collective-permute-done | bytes 102432 | tf_op jit(solution)/shard_map/ppermute | solution.py:47
  24.9 3.6 %collective-permute-done.23 = bf16[4,10,1280]{2,1,0:T(8,128)(2,1)S(1)} collective-permute-done((bf16[4,10,1280]{2,1,0:T(8,128)(2,1)S(1)}, bf16[4,10,1280]{2,1,0:T(8,128)(2,1)S(1)}, u32[]{:S(2)}, u32[]{:S(2)}) %collective-permute-start.23) | collective-permute-done | bytes 102432 | tf_op jit(solution)/shard_map/ppermute | solution.py:47
  32.5 9.8 %collective-permute-done.6 = bf16[4,40,1280]{2,1,0:T(8,128)(2,1)S(1)} collective-permute-done((bf16[4,40,1280]{2,1,0:T(8,128)(2,1)S(1)}, bf16[4,40,1280]{2,1,0:T(8,128)(2,1)S(1)}, u32[]{:S(2)}, u32[]{:S(2)}) %collective-permute-start.6) | collective-permute-done | bytes 409632 | tf_op jit(solution)/shard_map/ppermute | solution.py:35
  45.4 9.3 %collective-permute-done.8 = bf16[4,40,1280]{2,1,0:T(8,128)(2,1)S(1)} collective-permute-done((bf16[4,40,1280]{2,1,0:T(8,128)(2,1)S(1)}, bf16[4,40,1280]{2,1,0:T(8,128)(2,1)S(1)}, u32[]{:S(2)}, u32[]{:S(2)}) %collective-permute-start.8) | collective-permute-done | bytes 409632 | tf_op jit(solution)/shard_map/ppermute | solution.py:35
  55.9 1.6 collective-permute-start.9
  59.1 10.4 %collective-permute-done.10 = bf16[2,40,1280]{2,1,0:T(8,128)(2,1)S(1)} collective-permute-done((bf16[2,40,1280]{2,1,0:T(8,128)(2,1)S(1)}, bf16[2,40,1280]{2,1,0:T(8,128)(2,1)S(1)}, u32[]{:S(2)}, u32[]{:S(2)}) %collective-permute-start.10) | collective-permute-done | bytes 204832 | tf_op jit(solution)/shard_map/ppermute | solution.py:35
  70.3 5.8 %fusion.25 = f32[4,320,512]{2,1,0:T(8,128)S(1)} fusion(bf16[4,320,1280]{2,1,0:T(8,128)(2,1)} %maximum_dynamic-update-slice_fusion, bf16[4,1280,512]{2,1,0:T(8,128)(2,1)} %param.7), kind=kOutput, calls=%fused_computation.73 | convolution fusion | flops 1677721600 | bytes 11141120 | tf_op jit(solution)/shard_map/erd,edf->erf/dot_general | solution.py:130
  76.2 1.7 %fusion.4 = (f32[4,320,512]{2,1,0:T(8,128)S(1)}, bf16[4,320,512]{2,1,0:T(8,128)(2,1)S(1)}) fusion(f32[4,320,512]{2,1,0:T(8,128)S(1)} %fusion.25), kind=kLoop, calls=%fused_computation.8 | loop fusion | flops 12451840 | bytes 6553600 | tf_op jit(solution)/shard_map/add | solution.py:19
  77.9 1.9 %fusion.24 = (bf16[4,320,1280]{2,1,0:T(8,128)(2,1)S(1)}, f32[4,320,1280]{2,1,0:T(8,128)S(1)}) fusion(bf16[4,320,512]{2,1,0:T(8,128)(2,1)S(1)} %get-tuple-element.6, bf16[4,512,1280]{2,1,0:T(8,128)(2,1)S(1)} %bitcast.33), kind=kOutput, calls=%fused_computation.72 | convolution fusion | flops 1679360000 | bytes 16384000 | tf_op jit(solution)/shard_map/erf,efd->erd/dot_general | solution.py:134
  82.1 5.9 %collective-permute-done.11 = bf16[2,40,1280]{2,1,0:T(8,128)(2,1)S(1)} collective-permute-done((bf16[2,40,1280]{2,1,0:T(8,128)(2,1)S(1)}, bf16[2,40,1280]{2,1,0:T(8,128)(2,1)S(1)}, u32[]{:S(2)}, u32[]{:S(2)}) %collective-permute-start.11) | collective-permute-done | bytes 204832 | tf_op jit(solution)/shard_map/ppermute | solution.py:42
  91.9 21.4 %collective-permute-done.14 = bf16[4,40,1280]{2,1,0:T(8,128)(2,1)S(1)} collective-permute-done((bf16[4,40,1280]{2,1,0:T(8,128)(2,1)S(1)}, bf16[4,40,1280]{2,1,0:T(8,128)(2,1)S(1)}, u32[]{:S(2)}, u32[]{:S(2)}) %collective-permute-start.14) | collective-permute-done | bytes 409632 | tf_op jit(solution)/shard_map/ppermute | solution.py:42
  113.7 3.6 %collective-permute-start.15 = (bf16[4,40,1280]{2,1,0:T(8,128)(2,1)S(1)}, bf16[4,40,1280]{2,1,0:T(8,128)(2,1)S(1)}, u32[]{:S(2)}, u32[]{:S(2)}) collective-permute-start(bf16[4,40,1280]{2,1,0:T(8,128)(2,1)S(1)} %fusion.10), channel_id=1, source_target_pairs={{0,6},{1,7},{2,0},{3,1},{4,2},{5,3},{6,4},{7,5},{8,14},{9,15},{10,... | collective-permute-start | bytes 1228808 | tf_op jit(solution)/shard_map/ppermute | solution.py:35
  117.3 10.1 %collective-permute-done.28 = bf16[4,40,1280]{2,1,0:T(8,128)(2,1)S(1)} collective-permute-done((bf16[4,40,1280]{2,1,0:T(8,128)(2,1)S(1)}, bf16[4,40,1280]{2,1,0:T(8,128)(2,1)S(1)}, u32[]{:S(2)}, u32[]{:S(2)}) %collective-permute-start.28) | collective-permute-done | bytes 409632 | tf_op jit(solution)/shard_map/ppermute | solution.py:35
  129.0 5.0 %collective-permute-done.15 = bf16[4,40,1280]{2,1,0:T(8,128)(2,1)S(1)} collective-permute-done((bf16[4,40,1280]{2,1,0:T(8,128)(2,1)S(1)}, bf16[4,40,1280]{2,1,0:T(8,128)(2,1)S(1)}, u32[]{:S(2)}, u32[]{:S(2)}) %collective-permute-start.15) | collective-permute-done | bytes 409632 | tf_op jit(solution)/shard_map/ppermute | solution.py:35
  134.1 2.7 %collective-permute-start.17 = (bf16[4,40,1280]{2,1,0:T(8,128)(2,1)S(1)}, bf16[4,40,1280]{2,1,0:T(8,128)(2,1)S(1)}, u32[]{:S(2)}, u32[]{:S(2)}) collective-permute-start(bf16[4,40,1280]{2,1,0:T(8,128)(2,1)S(1)} %fusion.8), channel_id=1, source_target_pairs={{0,6},{1,7},{2,0},{3,1},{4,2},{5,3},{6,4},{7,5},{8,14},{9,15},{10,... | collective-permute-start | bytes 1228808 | tf_op jit(solution)/shard_map/ppermute | solution.py:35
  137.1 5.1 %collective-permute-done.30 = bf16[4,40,1280]{2,1,0:T(8,128)(2,1)S(1)} collective-permute-done((bf16[4,40,1280]{2,1,0:T(8,128)(2,1)S(1)}, bf16[4,40,1280]{2,1,0:T(8,128)(2,1)S(1)}, u32[]{:S(2)}, u32[]{:S(2)}) %collective-permute-start.30) | collective-permute-done | bytes 409632 | tf_op jit(solution)/shard_map/ppermute | solution.py:35
  143.0 5.7 %collective-permute-done.32 = bf16[2,40,1280]{2,1,0:T(8,128)(2,1)S(1)} collective-permute-done((bf16[2,40,1280]{2,1,0:T(8,128)(2,1)S(1)}, bf16[2,40,1280]{2,1,0:T(8,128)(2,1)S(1)}, u32[]{:S(2)}, u32[]{:S(2)}) %collective-permute-start.32) | collective-permute-done | bytes 204832 | tf_op jit(solution)/shard_map/ppermute | solution.py:35
  148.7 1.9 %multiply_convert_fusion = bf16[4,320,512]{2,1,0:T(8,128)(2,1)S(1)} fusion(f32[4,320,512]{2,1,0:T(8,128)S(1)} %get-tuple-element.8, bf16[4,320,1280]{2,1,0:T(8,128)(2,1)S(1)} %maximum_dynamic-update-slice_fusion.1, bf16[4,512,1280]{2,1,0:T(8,128)(2,1)S(1)} %bitcast.33), kind=kOutput, calls=%fused_computation.9 | convolution fusion | flops 1679032320 | bytes 12451840 | tf_op jit(solution)/shard_map/erd,efd->erf/dot_general | solution.py:142
  150.6 4.7 %convolution_convert_fusion = bf16[4,512,1280]{2,1,0:T(8,128)(2,1)} fusion(bf16[4,320,512]{2,1,0:T(8,128)(2,1)S(1)} %get-tuple-element.6, bf16[4,320,1280]{2,1,0:T(8,128)(2,1)S(1)} %maximum_dynamic-update-slice_fusion.1), kind=kOutput, calls=%fused_computation | convolution fusion | flops 1680343040 | bytes 9830400 | tf_op jit(solution)/shard_map/erf,erd->efd/dot_general | solution.py:146
  157.7 4.6 %convolution_convert_fusion.1 = bf16[4,1280,512]{2,1,0:T(8,128)(2,1)} fusion(bf16[4,320,1280]{2,1,0:T(8,128)(2,1)S(1)} %copy-done.2, bf16[4,320,512]{2,1,0:T(8,128)(2,1)S(1)} %multiply_convert_fusion), kind=kOutput, calls=%fused_computation.1 | convolution fusion | flops 1680343040 | bytes 9830400 | tf_op jit(solution)/shard_map/erd,erf->edf/dot_general | solution.py:149
  (111 shorter events, 32.8 us)
Async XLA Ops:
  5.0 8.2 %collective-permute-start.1 = (bf16[4,10,1280]{2,1,0:T(8,128)(2,1)S(1)}, bf16[4,10,1280]{2,1,0:T(8,128)(2,1)S(1)}, u32[]{:S(2)}, u32[]{:S(2)}) collective-permute-start(bf16[4,10,1280]{2,1,0:T(8,128)(2,1)S(1)} %squeeze.31), channel_id=1, source_target_pairs={{0,16},{8,24},{16,0},{24,8},{1,17},{9,25},{17,1},{25,9},{2,18},{10... | collective-permute-start | bytes 307208 | tf_op jit(solution)/shard_map/ppermute | solution.py:47
  14.4 16.6 %collective-permute-start.3 = (bf16[4,40,1280]{2,1,0:T(8,128)(2,1)S(1)}, bf16[4,40,1280]{2,1,0:T(8,128)(2,1)S(1)}, u32[]{:S(2)}, u32[]{:S(2)}) collective-permute-start(bf16[4,40,1280]{2,1,0:T(8,128)(2,1)S(1)} %get-tuple-element.29), channel_id=1, source_target_pairs={{0,1},{1,0},{2,3},{3,2},{4,5},{5,4},{6,7},{7,6},{8,9},{9,8},{10,11... | collective-permute-start | bytes 1228808 | tf_op jit(solution)/shard_map/ppermute | solution.py:42
  16.7 13.0 %collective-permute-start.4 = (bf16[4,40,1280]{2,1,0:T(8,128)(2,1)S(1)}, bf16[4,40,1280]{2,1,0:T(8,128)(2,1)S(1)}, u32[]{:S(2)}, u32[]{:S(2)}) collective-permute-start(bf16[4,40,1280]{2,1,0:T(8,128)(2,1)S(1)} %get-tuple-element.29), channel_id=1, source_target_pairs={{0,2},{1,3},{2,4},{3,5},{4,6},{5,7},{6,0},{7,1},{8,10},{9,11},{10,... | collective-permute-start | bytes 1228808 | tf_op jit(solution)/shard_map/ppermute | solution.py:35
  19.1 9.3 %collective-permute-start.23 = (bf16[4,10,1280]{2,1,0:T(8,128)(2,1)S(1)}, bf16[4,10,1280]{2,1,0:T(8,128)(2,1)S(1)}, u32[]{:S(2)}, u32[]{:S(2)}) collective-permute-start(bf16[4,10,1280]{2,1,0:T(8,128)(2,1)S(1)} %squeeze.38), channel_id=1, source_target_pairs={{0,16},{8,24},{16,0},{24,8},{1,17},{9,25},{17,1},{25,9},{2,18},{10... | collective-permute-start | bytes 307208 | tf_op jit(solution)/shard_map/ppermute | solution.py:47
  20.1 8.4 %collective-permute-start.22 = (bf16[4,10,1280]{2,1,0:T(8,128)(2,1)S(1)}, bf16[4,10,1280]{2,1,0:T(8,128)(2,1)S(1)}, u32[]{:S(2)}, u32[]{:S(2)}) collective-permute-start(bf16[4,10,1280]{2,1,0:T(8,128)(2,1)S(1)} %squeeze.37), channel_id=1, source_target_pairs={{0,8},{8,0},{16,24},{24,16},{1,9},{9,1},{17,25},{25,17},{2,10},{10... | collective-permute-start | bytes 307208 | tf_op jit(solution)/shard_map/ppermute | solution.py:47
  29.7 14.1 %collective-permute-start.5 = (bf16[4,40,1280]{2,1,0:T(8,128)(2,1)S(1)}, bf16[4,40,1280]{2,1,0:T(8,128)(2,1)S(1)}, u32[]{:S(2)}, u32[]{:S(2)}) collective-permute-start(bf16[4,40,1280]{2,1,0:T(8,128)(2,1)S(1)} %collective-permute-done.4), channel_id=1, source_target_pairs={{0,1},{1,0},{2,3},{3,2},{4,5},{5,4},{6,7},{7,6},{8,9},{9,8},{10,11... | collective-permute-start | bytes 1228808 | tf_op jit(solution)/shard_map/ppermute | solution.py:42
  30.2 12.1 %collective-permute-start.6 = (bf16[4,40,1280]{2,1,0:T(8,128)(2,1)S(1)}, bf16[4,40,1280]{2,1,0:T(8,128)(2,1)S(1)}, u32[]{:S(2)}, u32[]{:S(2)}) collective-permute-start(bf16[4,40,1280]{2,1,0:T(8,128)(2,1)S(1)} %collective-permute-done.4), channel_id=1, source_target_pairs={{0,2},{1,3},{2,4},{3,5},{4,6},{5,7},{6,0},{7,1},{8,10},{9,11},{10,... | collective-permute-start | bytes 1228808 | tf_op jit(solution)/shard_map/ppermute | solution.py:35
  42.4 13.1 %collective-permute-start.7 = (bf16[4,40,1280]{2,1,0:T(8,128)(2,1)S(1)}, bf16[4,40,1280]{2,1,0:T(8,128)(2,1)S(1)}, u32[]{:S(2)}, u32[]{:S(2)}) collective-permute-start(bf16[4,40,1280]{2,1,0:T(8,128)(2,1)S(1)} %collective-permute-done.6), channel_id=1, source_target_pairs={{0,1},{1,0},{2,3},{3,2},{4,5},{5,4},{6,7},{7,6},{8,9},{9,8},{10,11... | collective-permute-start | bytes 1228808 | tf_op jit(solution)/shard_map/ppermute | solution.py:42
  43.9 10.9 %collective-permute-start.8 = (bf16[4,40,1280]{2,1,0:T(8,128)(2,1)S(1)}, bf16[4,40,1280]{2,1,0:T(8,128)(2,1)S(1)}, u32[]{:S(2)}, u32[]{:S(2)}) collective-permute-start(bf16[4,40,1280]{2,1,0:T(8,128)(2,1)S(1)} %collective-permute-done.6), channel_id=1, source_target_pairs={{0,2},{1,3},{2,4},{3,5},{4,6},{5,7},{6,0},{7,1},{8,10},{9,11},{10,... | collective-permute-start | bytes 1228808 | tf_op jit(solution)/shard_map/ppermute | solution.py:35
  54.8 35.4 %collective-permute-start.25 = (bf16[4,40,1280]{2,1,0:T(8,128)(2,1)S(1)}, bf16[4,40,1280]{2,1,0:T(8,128)(2,1)S(1)}, u32[]{:S(2)}, u32[]{:S(2)}) collective-permute-start(bf16[4,40,1280]{2,1,0:T(8,128)(2,1)S(1)} %get-tuple-element.19), channel_id=1, source_target_pairs={{0,1},{1,0},{2,3},{3,2},{4,5},{5,4},{6,7},{7,6},{8,9},{9,8},{10,11... | collective-permute-start | bytes 1228808 | tf_op jit(solution)/shard_map/ppermute | solution.py:42
  55.4 34.9 %collective-permute-start.26 = (bf16[4,40,1280]{2,1,0:T(8,128)(2,1)S(1)}, bf16[4,40,1280]{2,1,0:T(8,128)(2,1)S(1)}, u32[]{:S(2)}, u32[]{:S(2)}) collective-permute-start(bf16[4,40,1280]{2,1,0:T(8,128)(2,1)S(1)} %get-tuple-element.19), channel_id=1, source_target_pairs={{0,2},{1,3},{2,4},{3,5},{4,6},{5,7},{6,0},{7,1},{8,10},{9,11},{10,... | collective-permute-start | bytes 1228808 | tf_op jit(solution)/shard_map/ppermute | solution.py:35
  55.4 14.1 %collective-permute-start.10 = (bf16[2,40,1280]{2,1,0:T(8,128)(2,1)S(1)}, bf16[2,40,1280]{2,1,0:T(8,128)(2,1)S(1)}, u32[]{:S(2)}, u32[]{:S(2)}) collective-permute-start(bf16[2,40,1280]{2,1,0:T(8,128)(2,1)S(1)} %slice.111), channel_id=1, source_target_pairs={{0,2},{1,3},{2,4},{3,5},{4,6},{5,7},{6,0},{7,1},{8,10},{9,11},{10,... | collective-permute-start | bytes 614408 | tf_op jit(solution)/shard_map/ppermute | solution.py:35
  55.9 13.6 %collective-permute-start.9 = (bf16[2,40,1280]{2,1,0:T(8,128)(2,1)S(1)}, bf16[2,40,1280]{2,1,0:T(8,128)(2,1)S(1)}, u32[]{:S(2)}, u32[]{:S(2)}) collective-permute-start(bf16[2,40,1280]{2,1,0:T(8,128)(2,1)S(1)} %slice.110), channel_id=1, source_target_pairs={{0,1},{1,0},{2,3},{3,2},{4,5},{5,4},{6,7},{7,6},{8,9},{9,8},{10,11... | collective-permute-start | bytes 614408 | tf_op jit(solution)/shard_map/ppermute | solution.py:42
  81.5 73.8 %collective-permute-start.18 = (bf16[4,40,1280]{2,1,0:T(8,128)(2,1)S(1)}, bf16[4,40,1280]{2,1,0:T(8,128)(2,1)S(1)}, u32[]{:S(2)}, u32[]{:S(2)}) collective-permute-start(bf16[4,40,1280]{2,1,0:T(8,128)(2,1)S(1)} %get-tuple-element.16), channel_id=1, source_target_pairs={{0,1},{1,0},{2,3},{3,2},{4,5},{5,4},{6,7},{7,6},{8,9},{9,8},{10,11... | collective-permute-start | bytes 1228808 | tf_op jit(solution)/shard_map/ppermute | solution.py:42
  88.0 41.0 %collective-permute-start.16 = (bf16[4,40,1280]{2,1,0:T(8,128)(2,1)S(1)}, bf16[4,40,1280]{2,1,0:T(8,128)(2,1)S(1)}, u32[]{:S(2)}, u32[]{:S(2)}) collective-permute-start(bf16[4,40,1280]{2,1,0:T(8,128)(2,1)S(1)} %get-tuple-element.15), channel_id=1, source_target_pairs={{0,1},{1,0},{2,3},{3,2},{4,5},{5,4},{6,7},{7,6},{8,9},{9,8},{10,11... | collective-permute-start | bytes 1228808 | tf_op jit(solution)/shard_map/ppermute | solution.py:42
  89.6 23.7 %collective-permute-start.14 = (bf16[4,40,1280]{2,1,0:T(8,128)(2,1)S(1)}, bf16[4,40,1280]{2,1,0:T(8,128)(2,1)S(1)}, u32[]{:S(2)}, u32[]{:S(2)}) collective-permute-start(bf16[4,40,1280]{2,1,0:T(8,128)(2,1)S(1)} %pad_maximum_fusion.3), channel_id=1, source_target_pairs={{0,1},{1,0},{2,3},{3,2},{4,5},{5,4},{6,7},{7,6},{8,9},{9,8},{10,11... | collective-permute-start | bytes 1228808 | tf_op jit(solution)/shard_map/ppermute | solution.py:42
  90.2 23.3 %collective-permute-start.12 = (bf16[4,40,1280]{2,1,0:T(8,128)(2,1)S(1)}, bf16[4,40,1280]{2,1,0:T(8,128)(2,1)S(1)}, u32[]{:S(2)}, u32[]{:S(2)}) collective-permute-start(bf16[4,40,1280]{2,1,0:T(8,128)(2,1)S(1)} %pad_maximum_fusion.2), channel_id=1, source_target_pairs={{0,6},{1,7},{2,0},{3,1},{4,2},{5,3},{6,4},{7,5},{8,14},{9,15},{10,... | collective-permute-start | bytes 1228808 | tf_op jit(solution)/shard_map/ppermute | solution.py:35
  90.3 38.6 %collective-permute-start.27 = (bf16[4,40,1280]{2,1,0:T(8,128)(2,1)S(1)}, bf16[4,40,1280]{2,1,0:T(8,128)(2,1)S(1)}, u32[]{:S(2)}, u32[]{:S(2)}) collective-permute-start(bf16[4,40,1280]{2,1,0:T(8,128)(2,1)S(1)} %collective-permute-done.26), channel_id=1, source_target_pairs={{0,1},{1,0},{2,3},{3,2},{4,5},{5,4},{6,7},{7,6},{8,9},{9,8},{10,11... | collective-permute-start | bytes 1228808 | tf_op jit(solution)/shard_map/ppermute | solution.py:42
  113.3 14.2 %collective-permute-start.28 = (bf16[4,40,1280]{2,1,0:T(8,128)(2,1)S(1)}, bf16[4,40,1280]{2,1,0:T(8,128)(2,1)S(1)}, u32[]{:S(2)}, u32[]{:S(2)}) collective-permute-start(bf16[4,40,1280]{2,1,0:T(8,128)(2,1)S(1)} %collective-permute-done.26), channel_id=1, source_target_pairs={{0,2},{1,3},{2,4},{3,5},{4,6},{5,7},{6,0},{7,1},{8,10},{9,11},{10,... | collective-permute-start | bytes 1228808 | tf_op jit(solution)/shard_map/ppermute | solution.py:35
  113.7 20.4 %collective-permute-start.15 = (bf16[4,40,1280]{2,1,0:T(8,128)(2,1)S(1)}, bf16[4,40,1280]{2,1,0:T(8,128)(2,1)S(1)}, u32[]{:S(2)}, u32[]{:S(2)}) collective-permute-start(bf16[4,40,1280]{2,1,0:T(8,128)(2,1)S(1)} %fusion.10), channel_id=1, source_target_pairs={{0,6},{1,7},{2,0},{3,1},{4,2},{5,3},{6,4},{7,5},{8,14},{9,15},{10,... | collective-permute-start | bytes 1228808 | tf_op jit(solution)/shard_map/ppermute | solution.py:35
  127.4 9.4 %collective-permute-start.29 = (bf16[4,40,1280]{2,1,0:T(8,128)(2,1)S(1)}, bf16[4,40,1280]{2,1,0:T(8,128)(2,1)S(1)}, u32[]{:S(2)}, u32[]{:S(2)}) collective-permute-start(bf16[4,40,1280]{2,1,0:T(8,128)(2,1)S(1)} %collective-permute-done.28), channel_id=1, source_target_pairs={{0,1},{1,0},{2,3},{3,2},{4,5},{5,4},{6,7},{7,6},{8,9},{9,8},{10,11... | collective-permute-start | bytes 1228808 | tf_op jit(solution)/shard_map/ppermute | solution.py:42
  128.9 13.3 %collective-permute-start.30 = (bf16[4,40,1280]{2,1,0:T(8,128)(2,1)S(1)}, bf16[4,40,1280]{2,1,0:T(8,128)(2,1)S(1)}, u32[]{:S(2)}, u32[]{:S(2)}) collective-permute-start(bf16[4,40,1280]{2,1,0:T(8,128)(2,1)S(1)} %collective-permute-done.28), channel_id=1, source_target_pairs={{0,2},{1,3},{2,4},{3,5},{4,6},{5,7},{6,0},{7,1},{8,10},{9,11},{10,... | collective-permute-start | bytes 1228808 | tf_op jit(solution)/shard_map/ppermute | solution.py:35
  134.1 21.1 %collective-permute-start.17 = (bf16[4,40,1280]{2,1,0:T(8,128)(2,1)S(1)}, bf16[4,40,1280]{2,1,0:T(8,128)(2,1)S(1)}, u32[]{:S(2)}, u32[]{:S(2)}) collective-permute-start(bf16[4,40,1280]{2,1,0:T(8,128)(2,1)S(1)} %fusion.8), channel_id=1, source_target_pairs={{0,6},{1,7},{2,0},{3,1},{4,2},{5,3},{6,4},{7,5},{8,14},{9,15},{10,... | collective-permute-start | bytes 1228808 | tf_op jit(solution)/shard_map/ppermute | solution.py:35
  136.9 11.8 %collective-permute-start.32 = (bf16[2,40,1280]{2,1,0:T(8,128)(2,1)S(1)}, bf16[2,40,1280]{2,1,0:T(8,128)(2,1)S(1)}, u32[]{:S(2)}, u32[]{:S(2)}) collective-permute-start(bf16[2,40,1280]{2,1,0:T(8,128)(2,1)S(1)} %slice.127), channel_id=1, source_target_pairs={{0,2},{1,3},{2,4},{3,5},{4,6},{5,7},{6,0},{7,1},{8,10},{9,11},{10,... | collective-permute-start | bytes 614408 | tf_op jit(solution)/shard_map/ppermute | solution.py:35
  (14 other events, 88.8 us)

commit v3 on v2

--- a/solution.py
+++ b/solution.py
@@ -49,10 +49,6 @@
 
 def exchange(packed):
     return [packed[0]] + [swap_expert(packed[m], m) for m in range(1, packed.shape[0])]
-
-
-def after(value, *earlier):
-    return lax.optimization_barrier((value, *earlier))[0]
 
 
 def gather_dp(block):
@@ -124,8 +120,7 @@
 
     blocks_tok = gather_dp(dispatch(tokens))
     rows_tok = rows_of(blocks_tok)
-    block_grad = after(dispatch(out_grad), blocks_tok[rows - 1][0])
-    rows_grad = rows_of(gather_dp(block_grad))
+    rows_grad = rows_of(gather_dp(dispatch(out_grad)))
 
     hidden_pre = jnp.einsum("erd,edf->erf", rows_tok, up_weight, preferred_element_type=jnp.float32)
     hidden_pre = lax.optimization_barrier(hidden_pre)
@@ -133,9 +128,15 @@
     active, slope = lax.optimization_barrier((active, gelu_slope(hidden_pre)))
     part = jnp.einsum("erf,efd->erd", active, down_weight, preferred_element_type=jnp.float32)
     part = jnp.split(part, rows * cols, axis=1)
-    summed = scatter_dp([part[k * cols : (k + 1) * cols] for k in range(rows)]).astype(jnp.bfloat16)
-    summed = summed.reshape(local_experts, owners, capacity, width).transpose(1, 0, 2, 3)
-    returned = jnp.concatenate(exchange(summed), axis=0).reshape(slots, width)
+    halves = 2 if local_experts % 2 == 0 else 1
+    count = local_experts // halves
+    returned = []
+    for first in range(0, local_experts, count):
+        piece = [p[first : first + count] for p in part]
+        summed = scatter_dp([piece[k * cols : (k + 1) * cols] for k in range(rows)])
+        summed = summed.astype(jnp.bfloat16).reshape(count, owners, capacity, width)
+        returned.append(jnp.stack(exchange(summed.transpose(1, 0, 2, 3))))
+    returned = jnp.concatenate(returned, axis=1).reshape(slots, width)
     combined = jnp.einsum("rt,rd->td", place, returned, preferred_element_type=jnp.float32)
     combined = combined.astype(jnp.bfloat16)
 

time: 165 us -> 146 us (0.88)
  waiting for transfers between devices: 97.7 us -> 67.8 us
  starting transfers between devices: 31.3 us -> 51.5 us
  local copies, waits for them, and re-layouts: 7.29 us -> 2.29 us
  matrix products: 21.4 us -> 17.5 us
    ppermute x12 -> x16, waiting for transfers between devices: 56.5 us -> 20.6 us  [ring_z(): return lax.ppermute(value, 'dp', perm)]
    ppermute x12 -> x16, starting transfers between devices: 9.64 us -> 22.6 us  [ring_z(): return lax.ppermute(value, 'dp', perm)]
    ppermute x12 -> x16, waiting for transfers between devices: 27.2 us -> 39.4 us  [ring_y(): return lax.ppermute(value, 'dp', perm)]
    ppermute x9 -> x12, waiting for transfers between devices: 14 us -> 7.85 us  [swap_expert(): return lax.ppermute(value, 'expert', [(i, i ^ mask) for i in range(n)])]
    unnamed x22 -> x24, local copies, waits for them, and re-layouts: 4.87 us -> 0.38 us
    ppermute x12 -> x16, starting transfers between devices: 14.5 us -> 18.8 us  [ring_y(): return lax.ppermute(value, 'dp', perm)]
    dot_general x1, matrix products: 5.85 us -> 1.85 us  [on_device(): jnp.einsum('erd,edf->erf', rows_tok, up_weight, preferred_element_type=jn...]
    ppermute x9 -> x12, starting transfers between devices: 7.24 us -> 10.1 us  [swap_expert(): return lax.ppermute(value, 'expert', [(i, i ^ mask) for i in range(n)])]
  transfers between devices with their start and end apart: 33 -> 44, of which waited for: 14 -> 18; matrix products, arithmetic and copies ran while one was open for 18% -> 14% of each run, Pallas kernels for 0% -> 0%
where the time goes in v3:
time: 146 us; the launch traced here: 145 us
  waiting for transfers between devices  67.8 us (46%)
  starting transfers between devices  51.5 us (35%)
  matrix products  17.5 us (12%)
  other arithmetic  4.55 us (3%)
  local copies, waits for them, and re-layouts  2.29 us (2%)
    ppermute x16, waiting for transfers between devices, ring_y(): return lax.ppermute(value, 'dp', perm)  39.4 us
    ppermute x16, starting transfers between devices, ring_z(): return lax.ppermute(value, 'dp', perm)  22.6 us
    ppermute x16, waiting for transfers between devices, ring_z(): return lax.ppermute(value, 'dp', perm)  20.6 us
    ppermute x16, starting transfers between devices, ring_y(): return lax.ppermute(value, 'dp', perm)  18.8 us
    ppermute x12, starting transfers between devices, swap_expert(): return lax.ppermute(value, 'expert', [(i, i ^ mask) for i in range(n)])  10.1 us
    ppermute x12, waiting for transfers between devices, swap_expert(): return lax.ppermute(value, 'expert', [(i, i ^ mask) for i in range(n)])  7.85 us
    dot_general x1, matrix products, on_device(): jnp.einsum('erf,erd->efd', active, rows_grad, preferred_element_type=jnp....  4.69 us
    dot_general x1, matrix products, on_device(): jnp.einsum('erd,erf->edf', rows_tok, pre_grad, preferred_element_type=jnp...  4.66 us
  transfers between devices with their start and end apart: 44, of which 18 were waited for; matrix products, arithmetic and copies ran while one was open for 14% of the time, Pallas kernels for 0%

profile of v3, /device:TPU:0, one launch (start us, length us, event | category | flops | bytes accessed | tf_op | source)
XLA Modules:
  0.0 144.8 jit_solution(9528072980313228943)
XLA Ops:
  2.5 2.4 %collective-permute-start.2 = (bf16[4,10,1280]{2,1,0:T(8,128)(2,1)S(1)}, bf16[4,10,1280]{2,1,0:T(8,128)(2,1)S(1)}, u32[]{:S(2)}, u32[]{:S(2)}) collective-permute-start(bf16[4,10,1280]{2,1,0:T(8,128)(2,1)S(1)} %squeeze.38), channel_id=1, source_target_pairs={{0,24},{8,16},{16,8},{24,0},{1,25},{9,17},{17,9},{25,1},{2,26},{10... | collective-permute-start | bytes 307208 | tf_op jit(solution)/shard_map/ppermute | solution.py:47
  10.4 3.7 %collective-permute-done.1 = bf16[4,10,1280]{2,1,0:T(8,128)(2,1)S(1)} collective-permute-done((bf16[4,10,1280]{2,1,0:T(8,128)(2,1)S(1)}, bf16[4,10,1280]{2,1,0:T(8,128)(2,1)S(1)}, u32[]{:S(2)}, u32[]{:S(2)}) %collective-permute-start.1) | collective-permute-done | bytes 102432 | tf_op jit(solution)/shard_map/ppermute | solution.py:47
  16.6 3.7 %collective-permute-done.34 = bf16[4,10,1280]{2,1,0:T(8,128)(2,1)S(1)} collective-permute-done((bf16[4,10,1280]{2,1,0:T(8,128)(2,1)S(1)}, bf16[4,10,1280]{2,1,0:T(8,128)(2,1)S(1)}, u32[]{:S(2)}, u32[]{:S(2)}) %collective-permute-start.34) | collective-permute-done | bytes 102432 | tf_op jit(solution)/shard_map/ppermute | solution.py:47
  20.7 2.4 %collective-permute-start.37 = (bf16[4,40,1280]{2,1,0:T(8,128)(2,1)S(1)}, bf16[4,40,1280]{2,1,0:T(8,128)(2,1)S(1)}, u32[]{:S(2)}, u32[]{:S(2)}) collective-permute-start(bf16[4,40,1280]{2,1,0:T(8,128)(2,1)S(1)} %get-tuple-element.31), channel_id=1, source_target_pairs={{0,2},{1,3},{2,4},{3,5},{4,6},{5,7},{6,0},{7,1},{8,10},{9,11},{10,... | collective-permute-start | bytes 1228808 | tf_op jit(solution)/shard_map/ppermute | solution.py:35
  25.1 3.5 %collective-permute-done.4 = bf16[4,40,1280]{2,1,0:T(8,128)(2,1)S(1)} collective-permute-done((bf16[4,40,1280]{2,1,0:T(8,128)(2,1)S(1)}, bf16[4,40,1280]{2,1,0:T(8,128)(2,1)S(1)}, u32[]{:S(2)}, u32[]{:S(2)}) %collective-permute-start.4) | collective-permute-done | bytes 409632 | tf_op jit(solution)/shard_map/ppermute | solution.py:35
  30.2 7.2 %collective-permute-done.37 = bf16[4,40,1280]{2,1,0:T(8,128)(2,1)S(1)} collective-permute-done((bf16[4,40,1280]{2,1,0:T(8,128)(2,1)S(1)}, bf16[4,40,1280]{2,1,0:T(8,128)(2,1)S(1)}, u32[]{:S(2)}, u32[]{:S(2)}) %collective-permute-start.37) | collective-permute-done | bytes 409632 | tf_op jit(solution)/shard_map/ppermute | solution.py:35
  39.0 5.2 %collective-permute-done.36 = bf16[4,40,1280]{2,1,0:T(8,128)(2,1)S(1)} collective-permute-done((bf16[4,40,1280]{2,1,0:T(8,128)(2,1)S(1)}, bf16[4,40,1280]{2,1,0:T(8,128)(2,1)S(1)}, u32[]{:S(2)}, u32[]{:S(2)}) %collective-permute-start.36) | collective-permute-done | bytes 409632 | tf_op jit(solution)/shard_map/ppermute | solution.py:42
  44.3 1.9 %collective-permute-done.6 = bf16[4,40,1280]{2,1,0:T(8,128)(2,1)S(1)} collective-permute-done((bf16[4,40,1280]{2,1,0:T(8,128)(2,1)S(1)}, bf16[4,40,1280]{2,1,0:T(8,128)(2,1)S(1)}, u32[]{:S(2)}, u32[]{:S(2)}) %collective-permute-start.6) | collective-permute-done | bytes 409632 | tf_op jit(solution)/shard_map/ppermute | solution.py:35
  47.7 7.2 %collective-permute-done.39 = bf16[4,40,1280]{2,1,0:T(8,128)(2,1)S(1)} collective-permute-done((bf16[4,40,1280]{2,1,0:T(8,128)(2,1)S(1)}, bf16[4,40,1280]{2,1,0:T(8,128)(2,1)S(1)}, u32[]{:S(2)}, u32[]{:S(2)}) %collective-permute-start.39) | collective-permute-done | bytes 409632 | tf_op jit(solution)/shard_map/ppermute | solution.py:35
  56.6 5.2 %collective-permute-done.38 = bf16[4,40,1280]{2,1,0:T(8,128)(2,1)S(1)} collective-permute-done((bf16[4,40,1280]{2,1,0:T(8,128)(2,1)S(1)}, bf16[4,40,1280]{2,1,0:T(8,128)(2,1)S(1)}, u32[]{:S(2)}, u32[]{:S(2)}) %collective-permute-start.38) | collective-permute-done | bytes 409632 | tf_op jit(solution)/shard_map/ppermute | solution.py:42
  61.9 8.7 %collective-permute-done.7 = bf16[4,40,1280]{2,1,0:T(8,128)(2,1)S(1)} collective-permute-done((bf16[4,40,1280]{2,1,0:T(8,128)(2,1)S(1)}, bf16[4,40,1280]{2,1,0:T(8,128)(2,1)S(1)}, u32[]{:S(2)}, u32[]{:S(2)}) %collective-permute-start.7) | collective-permute-done | bytes 409632 | tf_op jit(solution)/shard_map/ppermute | solution.py:42
  73.8 5.5 %collective-permute-done.40 = bf16[4,40,1280]{2,1,0:T(8,128)(2,1)S(1)} collective-permute-done((bf16[4,40,1280]{2,1,0:T(8,128)(2,1)S(1)}, bf16[4,40,1280]{2,1,0:T(8,128)(2,1)S(1)}, u32[]{:S(2)}, u32[]{:S(2)}) %collective-permute-start.40) | collective-permute-done | bytes 409632 | tf_op jit(solution)/shard_map/ppermute | solution.py:42
  82.6 1.8 %fusion.35 = f32[4,320,512]{2,1,0:T(8,128)S(1)} fusion(bf16[4,320,1280]{2,1,0:T(8,128)(2,1)S(1)} %maximum_dynamic-update-slice_fusion, bf16[4,1280,512]{2,1,0:T(8,128)(2,1)S(1)} %bitcast.64), kind=kOutput, calls=%fused_computation.92 | convolution fusion | flops 1677721600 | bytes 11141120 | tf_op jit(solution)/shard_map/erd,edf->erf/dot_general | solution.py:125
  84.5 1.7 %fusion.4 = (f32[4,320,512]{2,1,0:T(8,128)S(1)}, bf16[4,320,512]{2,1,0:T(8,128)(2,1)S(1)}) fusion(f32[4,320,512]{2,1,0:T(8,128)S(1)} %fusion.35), kind=kLoop, calls=%fused_computation.8 | loop fusion | flops 12451840 | bytes 6553600 | tf_op jit(solution)/shard_map/add | solution.py:19
  86.2 1.9 %fusion.34 = (bf16[4,320,1280]{2,1,0:T(8,128)(2,1)S(1)}, f32[4,320,1280]{2,1,0:T(8,128)S(1)}) fusion(bf16[4,320,512]{2,1,0:T(8,128)(2,1)S(1)} %get-tuple-element.5, bf16[4,512,1280]{2,1,0:T(8,128)(2,1)S(1)} %bitcast.46), kind=kOutput, calls=%fused_computation.91 | convolution fusion | flops 1679360000 | bytes 16384000 | tf_op jit(solution)/shard_map/erf,efd->erd/dot_general | solution.py:129
  89.8 2.4 %collective-permute-start.24 = (bf16[1,40,1280]{2,1,0:T(8,128)(2,1)S(1)}, bf16[1,40,1280]{2,1,0:T(8,128)(2,1)S(1)}, u32[]{:S(2)}, u32[]{:S(2)}) collective-permute-start(bf16[1,40,1280]{2,1,0:T(8,128)(2,1)S(1)} %get-tuple-element.18), channel_id=1, source_target_pairs={{0,6},{1,7},{2,0},{3,1},{4,2},{5,3},{6,4},{7,5},{8,14},{9,15},{10,... | collective-permute-start | bytes 307208 | tf_op jit(solution)/shard_map/ppermute | solution.py:35
  99.0 3.5 %collective-permute-start.12 = (bf16[2,40,1280]{2,1,0:T(8,128)(2,1)S(1)}, bf16[2,40,1280]{2,1,0:T(8,128)(2,1)S(1)}, u32[]{:S(2)}, u32[]{:S(2)}) collective-permute-start(bf16[2,40,1280]{2,1,0:T(8,128)(2,1)S(1)} %pad_maximum_fusion.2), channel_id=1, source_target_pairs={{0,6},{1,7},{2,0},{3,1},{4,2},{5,3},{6,4},{7,5},{8,14},{9,15},{10,... | collective-permute-start | bytes 614408 | tf_op jit(solution)/shard_map/ppermute | solution.py:35
  104.1 7.2 %collective-permute-done.14 = bf16[2,40,1280]{2,1,0:T(8,128)(2,1)S(1)} collective-permute-done((bf16[2,40,1280]{2,1,0:T(8,128)(2,1)S(1)}, bf16[2,40,1280]{2,1,0:T(8,128)(2,1)S(1)}, u32[]{:S(2)}, u32[]{:S(2)}) %collective-permute-start.14) | collective-permute-done | bytes 204832 | tf_op jit(solution)/shard_map/ppermute | solution.py:42
  113.3 2.4 %collective-permute-done.25 = bf16[2,40,1280]{2,1,0:T(8,128)(2,1)S(1)} collective-permute-done((bf16[2,40,1280]{2,1,0:T(8,128)(2,1)S(1)}, bf16[2,40,1280]{2,1,0:T(8,128)(2,1)S(1)}, u32[]{:S(2)}, u32[]{:S(2)}) %collective-permute-start.25) | collective-permute-done | bytes 204832 | tf_op jit(solution)/shard_map/ppermute | solution.py:42
  118.8 1.9 %multiply_convert_fusion = bf16[4,320,512]{2,1,0:T(8,128)(2,1)S(1)} fusion(f32[4,320,512]{2,1,0:T(8,128)S(1)} %get-tuple-element.6, bf16[4,320,1280]{2,1,0:T(8,128)(2,1)S(1)} %maximum_dynamic-update-slice_fusion.1, bf16[4,512,1280]{2,1,0:T(8,128)(2,1)S(1)} %bitcast.46), kind=kOutput, calls=%fused_computation.9 | convolution fusion | flops 1679032320 | bytes 12451840 | tf_op jit(solution)/shard_map/erd,efd->erf/dot_general | solution.py:143
  122.0 2.4 %collective-permute-done.27 = bf16[2,40,1280]{2,1,0:T(8,128)(2,1)S(1)} collective-permute-done((bf16[2,40,1280]{2,1,0:T(8,128)(2,1)S(1)}, bf16[2,40,1280]{2,1,0:T(8,128)(2,1)S(1)}, u32[]{:S(2)}, u32[]{:S(2)}) %collective-permute-start.27) | collective-permute-done | bytes 204832 | tf_op jit(solution)/shard_map/ppermute | solution.py:42
  124.6 3.4 %collective-permute-start.17 = (bf16[2,40,1280]{2,1,0:T(8,128)(2,1)S(1)}, bf16[2,40,1280]{2,1,0:T(8,128)(2,1)S(1)}, u32[]{:S(2)}, u32[]{:S(2)}) collective-permute-start(bf16[2,40,1280]{2,1,0:T(8,128)(2,1)S(1)} %get-tuple-element.9), channel_id=1, source_target_pairs={{0,6},{1,7},{2,0},{3,1},{4,2},{5,3},{6,4},{7,5},{8,14},{9,15},{10,... | collective-permute-start | bytes 614408 | tf_op jit(solution)/shard_map/ppermute | solution.py:35
  128.5 4.7 %convolution_convert_fusion = bf16[4,512,1280]{2,1,0:T(8,128)(2,1)} fusion(bf16[4,320,512]{2,1,0:T(8,128)(2,1)S(1)} %get-tuple-element.5, bf16[4,320,1280]{2,1,0:T(8,128)(2,1)S(1)} %maximum_dynamic-update-slice_fusion.1), kind=kOutput, calls=%fused_computation | convolution fusion | flops 1680343040 | bytes 9830400 | tf_op jit(solution)/shard_map/erf,erd->efd/dot_general | solution.py:147
  138.5 4.7 %convolution_convert_fusion.1 = bf16[4,1280,512]{2,1,0:T(8,128)(2,1)} fusion(bf16[4,320,1280]{2,1,0:T(8,128)(2,1)S(1)} %maximum_dynamic-update-slice_fusion, bf16[4,320,512]{2,1,0:T(8,128)(2,1)S(1)} %multiply_convert_fusion), kind=kOutput, calls=%fused_computation.1 | convolution fusion | flops 1680343040 | bytes 9830400 | tf_op jit(solution)/shard_map/erd,erf->edf/dot_general | solution.py:150
  (140 shorter events, 48.9 us)
Async XLA Ops:
  8.7 11.5 %collective-permute-start.34 = (bf16[4,10,1280]{2,1,0:T(8,128)(2,1)S(1)}, bf16[4,10,1280]{2,1,0:T(8,128)(2,1)S(1)}, u32[]{:S(2)}, u32[]{:S(2)}) collective-permute-start(bf16[4,10,1280]{2,1,0:T(8,128)(2,1)S(1)} %squeeze.46), channel_id=1, source_target_pairs={{0,16},{8,24},{16,0},{24,8},{1,17},{9,25},{17,1},{25,9},{2,18},{10... | collective-permute-start | bytes 307208 | tf_op jit(solution)/shard_map/ppermute | solution.py:47
  9.5 10.7 %collective-permute-start.33 = (bf16[4,10,1280]{2,1,0:T(8,128)(2,1)S(1)}, bf16[4,10,1280]{2,1,0:T(8,128)(2,1)S(1)}, u32[]{:S(2)}, u32[]{:S(2)}) collective-permute-start(bf16[4,10,1280]{2,1,0:T(8,128)(2,1)S(1)} %squeeze.45), channel_id=1, source_target_pairs={{0,8},{8,0},{16,24},{24,16},{1,9},{9,1},{17,25},{25,17},{2,10},{10... | collective-permute-start | bytes 307208 | tf_op jit(solution)/shard_map/ppermute | solution.py:47
  14.5 14.2 %collective-permute-start.4 = (bf16[4,40,1280]{2,1,0:T(8,128)(2,1)S(1)}, bf16[4,40,1280]{2,1,0:T(8,128)(2,1)S(1)}, u32[]{:S(2)}, u32[]{:S(2)}) collective-permute-start(bf16[4,40,1280]{2,1,0:T(8,128)(2,1)S(1)} %get-tuple-element.37), channel_id=1, source_target_pairs={{0,2},{1,3},{2,4},{3,5},{4,6},{5,7},{6,0},{7,1},{8,10},{9,11},{10,... | collective-permute-start | bytes 1228808 | tf_op jit(solution)/shard_map/ppermute | solution.py:35
  20.7 16.7 %collective-permute-start.37 = (bf16[4,40,1280]{2,1,0:T(8,128)(2,1)S(1)}, bf16[4,40,1280]{2,1,0:T(8,128)(2,1)S(1)}, u32[]{:S(2)}, u32[]{:S(2)}) collective-permute-start(bf16[4,40,1280]{2,1,0:T(8,128)(2,1)S(1)} %get-tuple-element.31), channel_id=1, source_target_pairs={{0,2},{1,3},{2,4},{3,5},{4,6},{5,7},{6,0},{7,1},{8,10},{9,11},{10,... | collective-permute-start | bytes 1228808 | tf_op jit(solution)/shard_map/ppermute | solution.py:35
  23.1 15.8 %collective-permute-start.3 = (bf16[4,40,1280]{2,1,0:T(8,128)(2,1)S(1)}, bf16[4,40,1280]{2,1,0:T(8,128)(2,1)S(1)}, u32[]{:S(2)}, u32[]{:S(2)}) collective-permute-start(bf16[4,40,1280]{2,1,0:T(8,128)(2,1)S(1)} %get-tuple-element.37), channel_id=1, source_target_pairs={{0,1},{1,0},{2,3},{3,2},{4,5},{5,4},{6,7},{7,6},{8,9},{9,8},{10,11... | collective-permute-start | bytes 1228808 | tf_op jit(solution)/shard_map/ppermute | solution.py:42
  24.6 19.6 %collective-permute-start.36 = (bf16[4,40,1280]{2,1,0:T(8,128)(2,1)S(1)}, bf16[4,40,1280]{2,1,0:T(8,128)(2,1)S(1)}, u32[]{:S(2)}, u32[]{:S(2)}) collective-permute-start(bf16[4,40,1280]{2,1,0:T(8,128)(2,1)S(1)} %get-tuple-element.31), channel_id=1, source_target_pairs={{0,1},{1,0},{2,3},{3,2},{4,5},{5,4},{6,7},{7,6},{8,9},{9,8},{10,11... | collective-permute-start | bytes 1228808 | tf_op jit(solution)/shard_map/ppermute | solution.py:42
  28.6 27.9 %collective-permute-start.5 = (bf16[4,40,1280]{2,1,0:T(8,128)(2,1)S(1)}, bf16[4,40,1280]{2,1,0:T(8,128)(2,1)S(1)}, u32[]{:S(2)}, u32[]{:S(2)}) collective-permute-start(bf16[4,40,1280]{2,1,0:T(8,128)(2,1)S(1)} %collective-permute-done.4), channel_id=1, source_target_pairs={{0,1},{1,0},{2,3},{3,2},{4,5},{5,4},{6,7},{7,6},{8,9},{9,8},{10,11... | collective-permute-start | bytes 1228808 | tf_op jit(solution)/shard_map/ppermute | solution.py:42
  30.2 16.0 %collective-permute-start.6 = (bf16[4,40,1280]{2,1,0:T(8,128)(2,1)S(1)}, bf16[4,40,1280]{2,1,0:T(8,128)(2,1)S(1)}, u32[]{:S(2)}, u32[]{:S(2)}) collective-permute-start(bf16[4,40,1280]{2,1,0:T(8,128)(2,1)S(1)} %collective-permute-done.4), channel_id=1, source_target_pairs={{0,2},{1,3},{2,4},{3,5},{4,6},{5,7},{6,0},{7,1},{8,10},{9,11},{10,... | collective-permute-start | bytes 1228808 | tf_op jit(solution)/shard_map/ppermute | solution.py:35
  37.4 24.4 %collective-permute-start.38 = (bf16[4,40,1280]{2,1,0:T(8,128)(2,1)S(1)}, bf16[4,40,1280]{2,1,0:T(8,128)(2,1)S(1)}, u32[]{:S(2)}, u32[]{:S(2)}) collective-permute-start(bf16[4,40,1280]{2,1,0:T(8,128)(2,1)S(1)} %collective-permute-done.37), channel_id=1, source_target_pairs={{0,1},{1,0},{2,3},{3,2},{4,5},{5,4},{6,7},{7,6},{8,9},{9,8},{10,11... | collective-permute-start | bytes 1228808 | tf_op jit(solution)/shard_map/ppermute | solution.py:42
  39.0 16.0 %collective-permute-start.39 = (bf16[4,40,1280]{2,1,0:T(8,128)(2,1)S(1)}, bf16[4,40,1280]{2,1,0:T(8,128)(2,1)S(1)}, u32[]{:S(2)}, u32[]{:S(2)}) collective-permute-start(bf16[4,40,1280]{2,1,0:T(8,128)(2,1)S(1)} %collective-permute-done.37), channel_id=1, source_target_pairs={{0,2},{1,3},{2,4},{3,5},{4,6},{5,7},{6,0},{7,1},{8,10},{9,11},{10,... | collective-permute-start | bytes 1228808 | tf_op jit(solution)/shard_map/ppermute | solution.py:35
  46.2 24.4 %collective-permute-start.7 = (bf16[4,40,1280]{2,1,0:T(8,128)(2,1)S(1)}, bf16[4,40,1280]{2,1,0:T(8,128)(2,1)S(1)}, u32[]{:S(2)}, u32[]{:S(2)}) collective-permute-start(bf16[4,40,1280]{2,1,0:T(8,128)(2,1)S(1)} %collective-permute-done.6), channel_id=1, source_target_pairs={{0,1},{1,0},{2,3},{3,2},{4,5},{5,4},{6,7},{7,6},{8,9},{9,8},{10,11... | collective-permute-start | bytes 1228808 | tf_op jit(solution)/shard_map/ppermute | solution.py:42
  47.7 24.5 %collective-permute-start.8 = (bf16[4,40,1280]{2,1,0:T(8,128)(2,1)S(1)}, bf16[4,40,1280]{2,1,0:T(8,128)(2,1)S(1)}, u32[]{:S(2)}, u32[]{:S(2)}) collective-permute-start(bf16[4,40,1280]{2,1,0:T(8,128)(2,1)S(1)} %collective-permute-done.6), channel_id=1, source_target_pairs={{0,2},{1,3},{2,4},{3,5},{4,6},{5,7},{6,0},{7,1},{8,10},{9,11},{10,... | collective-permute-start | bytes 1228808 | tf_op jit(solution)/shard_map/ppermute | solution.py:35
  55.0 24.4 %collective-permute-start.40 = (bf16[4,40,1280]{2,1,0:T(8,128)(2,1)S(1)}, bf16[4,40,1280]{2,1,0:T(8,128)(2,1)S(1)}, u32[]{:S(2)}, u32[]{:S(2)}) collective-permute-start(bf16[4,40,1280]{2,1,0:T(8,128)(2,1)S(1)} %collective-permute-done.39), channel_id=1, source_target_pairs={{0,1},{1,0},{2,3},{3,2},{4,5},{5,4},{6,7},{7,6},{8,9},{9,8},{10,11... | collective-permute-start | bytes 1228808 | tf_op jit(solution)/shard_map/ppermute | solution.py:42
  56.5 24.6 %collective-permute-start.41 = (bf16[4,40,1280]{2,1,0:T(8,128)(2,1)S(1)}, bf16[4,40,1280]{2,1,0:T(8,128)(2,1)S(1)}, u32[]{:S(2)}, u32[]{:S(2)}) collective-permute-start(bf16[4,40,1280]{2,1,0:T(8,128)(2,1)S(1)} %collective-permute-done.39), channel_id=1, source_target_pairs={{0,2},{1,3},{2,4},{3,5},{4,6},{5,7},{6,0},{7,1},{8,10},{9,11},{10,... | collective-permute-start | bytes 1228808 | tf_op jit(solution)/shard_map/ppermute | solution.py:35
  70.6 10.6 %collective-permute-start.10 = (bf16[2,40,1280]{2,1,0:T(8,128)(2,1)S(1)}, bf16[2,40,1280]{2,1,0:T(8,128)(2,1)S(1)}, u32[]{:S(2)}, u32[]{:S(2)}) collective-permute-start(bf16[2,40,1280]{2,1,0:T(8,128)(2,1)S(1)} %slice.227), channel_id=1, source_target_pairs={{0,2},{1,3},{2,4},{3,5},{4,6},{5,7},{6,0},{7,1},{8,10},{9,11},{10,... | collective-permute-start | bytes 614408 | tf_op jit(solution)/shard_map/ppermute | solution.py:35
  72.2 10.3 %collective-permute-start.9 = (bf16[2,40,1280]{2,1,0:T(8,128)(2,1)S(1)}, bf16[2,40,1280]{2,1,0:T(8,128)(2,1)S(1)}, u32[]{:S(2)}, u32[]{:S(2)}) collective-permute-start(bf16[2,40,1280]{2,1,0:T(8,128)(2,1)S(1)} %slice.226), channel_id=1, source_target_pairs={{0,1},{1,0},{2,3},{3,2},{4,5},{5,4},{6,7},{7,6},{8,9},{9,8},{10,11... | collective-permute-start | bytes 614408 | tf_op jit(solution)/shard_map/ppermute | solution.py:42
  79.4 23.2 %collective-permute-start.43 = (bf16[2,40,1280]{2,1,0:T(8,128)(2,1)S(1)}, bf16[2,40,1280]{2,1,0:T(8,128)(2,1)S(1)}, u32[]{:S(2)}, u32[]{:S(2)}) collective-permute-start(bf16[2,40,1280]{2,1,0:T(8,128)(2,1)S(1)} %slice.263), channel_id=1, source_target_pairs={{0,2},{1,3},{2,4},{3,5},{4,6},{5,7},{6,0},{7,1},{8,10},{9,11},{10,... | collective-permute-start | bytes 614408 | tf_op jit(solution)/shard_map/ppermute | solution.py:35
  96.0 37.2 %collective-permute-start.18 = (bf16[2,40,1280]{2,1,0:T(8,128)(2,1)S(1)}, bf16[2,40,1280]{2,1,0:T(8,128)(2,1)S(1)}, u32[]{:S(2)}, u32[]{:S(2)}) collective-permute-start(bf16[2,40,1280]{2,1,0:T(8,128)(2,1)S(1)} %get-tuple-element.28), channel_id=1, source_target_pairs={{0,1},{1,0},{2,3},{3,2},{4,5},{5,4},{6,7},{7,6},{8,9},{9,8},{10,11... | collective-permute-start | bytes 614408 | tf_op jit(solution)/shard_map/ppermute | solution.py:42
  98.0 13.2 %collective-permute-start.14 = (bf16[2,40,1280]{2,1,0:T(8,128)(2,1)S(1)}, bf16[2,40,1280]{2,1,0:T(8,128)(2,1)S(1)}, u32[]{:S(2)}, u32[]{:S(2)}) collective-permute-start(bf16[2,40,1280]{2,1,0:T(8,128)(2,1)S(1)} %pad_maximum_fusion.3), channel_id=1, source_target_pairs={{0,1},{1,0},{2,3},{3,2},{4,5},{5,4},{6,7},{7,6},{8,9},{9,8},{10,11... | collective-permute-start | bytes 614408 | tf_op jit(solution)/shard_map/ppermute | solution.py:42
  99.0 13.7 %collective-permute-start.12 = (bf16[2,40,1280]{2,1,0:T(8,128)(2,1)S(1)}, bf16[2,40,1280]{2,1,0:T(8,128)(2,1)S(1)}, u32[]{:S(2)}, u32[]{:S(2)}) collective-permute-start(bf16[2,40,1280]{2,1,0:T(8,128)(2,1)S(1)} %pad_maximum_fusion.2), channel_id=1, source_target_pairs={{0,6},{1,7},{2,0},{3,1},{4,2},{5,3},{6,4},{7,5},{8,14},{9,15},{10,... | collective-permute-start | bytes 614408 | tf_op jit(solution)/shard_map/ppermute | solution.py:35
  102.6 13.0 %collective-permute-start.25 = (bf16[2,40,1280]{2,1,0:T(8,128)(2,1)S(1)}, bf16[2,40,1280]{2,1,0:T(8,128)(2,1)S(1)}, u32[]{:S(2)}, u32[]{:S(2)}) collective-permute-start(bf16[2,40,1280]{2,1,0:T(8,128)(2,1)S(1)} %pad_maximum_fusion.5), channel_id=1, source_target_pairs={{0,1},{1,0},{2,3},{3,2},{4,5},{5,4},{6,7},{7,6},{8,9},{9,8},{10,11... | collective-permute-start | bytes 614408 | tf_op jit(solution)/shard_map/ppermute | solution.py:42
  103.2 12.4 %collective-permute-start.23 = (bf16[2,40,1280]{2,1,0:T(8,128)(2,1)S(1)}, bf16[2,40,1280]{2,1,0:T(8,128)(2,1)S(1)}, u32[]{:S(2)}, u32[]{:S(2)}) collective-permute-start(bf16[2,40,1280]{2,1,0:T(8,128)(2,1)S(1)} %pad_maximum_fusion.4), channel_id=1, source_target_pairs={{0,6},{1,7},{2,0},{3,1},{4,2},{5,3},{6,4},{7,5},{8,14},{9,15},{10,... | collective-permute-start | bytes 614408 | tf_op jit(solution)/shard_map/ppermute | solution.py:35
  112.8 11.6 %collective-permute-start.27 = (bf16[2,40,1280]{2,1,0:T(8,128)(2,1)S(1)}, bf16[2,40,1280]{2,1,0:T(8,128)(2,1)S(1)}, u32[]{:S(2)}, u32[]{:S(2)}) collective-permute-start(bf16[2,40,1280]{2,1,0:T(8,128)(2,1)S(1)} %get-tuple-element.27), channel_id=1, source_target_pairs={{0,1},{1,0},{2,3},{3,2},{4,5},{5,4},{6,7},{7,6},{8,9},{9,8},{10,11... | collective-permute-start | bytes 614408 | tf_op jit(solution)/shard_map/ppermute | solution.py:42
  120.7 12.4 %collective-permute-start.29 = (bf16[2,40,1280]{2,1,0:T(8,128)(2,1)S(1)}, bf16[2,40,1280]{2,1,0:T(8,128)(2,1)S(1)}, u32[]{:S(2)}, u32[]{:S(2)}) collective-permute-start(bf16[2,40,1280]{2,1,0:T(8,128)(2,1)S(1)} %get-tuple-element.26), channel_id=1, source_target_pairs={{0,1},{1,0},{2,3},{3,2},{4,5},{5,4},{6,7},{7,6},{8,9},{9,8},{10,11... | collective-permute-start | bytes 614408 | tf_op jit(solution)/shard_map/ppermute | solution.py:42
  (26 other events, 246.1 us)

commit v4 on v1

v4 whole, which is shorter than its diff:
```python
import math

import jax
import jax.numpy as jnp
from jax import lax
from jax.sharding import PartitionSpec as P

gelu_scale = math.sqrt(2.0 / math.pi)
cubic_term = 0.044715


def gelu_value(values):
    inner_arg = gelu_scale * (values + cubic_term * values * values * values)
    return 0.5 * values * (1.0 + jnp.tanh(inner_arg))


def gelu_slope(values):
    tangent = jnp.tanh(gelu_scale * (values + cubic_term * values * values * values))
    return 0.5 * (1.0 + tangent) + 0.5 * values * (1.0 - tangent * tangent) * gelu_scale * (
        1.0 + 3.0 * cubic_term * values * values
    )


def after(value, *earlier):
    return lax.optimization_barrier((value, *earlier))[0]


def grid_of(n):
    cols = 1
    while cols * cols * 4 <= n and n % (cols * 2) == 0:
        cols *= 2
    return n // cols, cols


def ring_z(value, step, name="z"):
    n = lax.axis_size("dp")
    rows, cols = grid_of(n)
    perm = [(i, ((i // cols + step) % rows) * cols + i % cols) for i in range(n)]
    with jax.named_scope(name):
        return lax.ppermute(value, "dp", perm)


def ring_y(value, step, name="y"):
    n = lax.axis_size("dp")
    cols = grid_of(n)[1]
    perm = [(i, i // cols * cols + (i % cols + step) % cols) for i in range(n)]
    with jax.named_scope(name):
        return lax.ppermute(value, "dp", perm)


def swap_expert(value, mask, name="swap"):
    n = lax.axis_size("expert")
    with jax.named_scope(f"{name}_x{mask}"):
        return lax.ppermute(value, "expert", [(i, i ^ mask) for i in range(n)])


def exchange(packed, name):
    return [packed[0]] + [swap_expert(packed[m], m, name) for m in range(1, packed.shape[0])]


def gather_step(blocks, k, name, hold=(), last_over_z=False):
    rows, cols = grid_of(lax.axis_size("dp"))
    size = blocks[0][0].shape[0]
    half = size // 32 * 16 if size % 8 == 0 and size >= 32 else size // 2
    here = blocks[k][0]
    beyond = blocks[max(k, 1) - 1][-1][half:]
    wait = (*hold, *([blocks[k - 1][-1]] if k > 0 else []))
    if wait:
        here, beyond, *_ = lax.optimization_barrier((here, beyond, *wait))
    if cols == 2 and k > 0 and k == rows - 1 and half > 0:
        if last_over_z:
            blocks[k].append(ring_z(after(blocks[k - 1][1], *hold), 1, f"{name}_z{k + 1}"))
            return blocks[k][1:]
        low = ring_y(here[:half], 1, f"{name}_y{k}")
        high = ring_z(beyond, 1, f"{name}_z{k + 1}")
        blocks[k].append(jnp.concatenate([low, high], axis=0))
        return [low, high]
    if k < rows - 1:
        blocks.append([ring_z(here, 1, f"{name}_z{k + 1}")])
    for j in range(cols - 1):
        blocks[k].append(ring_y(here if j == 0 else blocks[k][j], 1, f"{name}_y{k}"))
    return [blocks[k][-1], *(line[0] for line in blocks[k + 1 : k + 2])]


def cross(chunks, name, hold=()):
    if hold:
        chunks = after(chunks, *hold)
    pairs = chunks.shape[0] // 2
    return [chunks[:2]] + [
        swap_expert(chunks[2 * q : 2 * q + 2], 2 * q, name) for q in range(1, pairs)
    ]


def settle(got, name, hold=()):
    if hold:
        got = lax.optimization_barrier((*got, *hold))[: len(got)]
    back = swap_expert(jnp.stack([g[1] for g in got]), 1, name)
    return [c for q in range(len(got)) for c in (got[q][0], back[q])], back


def on_device(tokens, expert_ids, up_weight, down_weight, out_grad):
    owners = lax.axis_size("expert")
    rows, cols = grid_of(lax.axis_size("dp"))
    local_experts = up_weight.shape[0]
    all_experts = owners * local_experts
    tok_rows, width = tokens.shape
    capacity = 5 * tok_rows // (4 * all_experts)
    slots = all_experts * capacity
    me = lax.axis_index("expert")
    index = jnp.arange(tok_rows, dtype=jnp.int32)
    earlier = (expert_ids[:, None] == expert_ids[None, :]) & (index[:, None] < index[None, :])
    slot_index = jnp.sum(earlier.astype(jnp.int32), axis=0)
    owner_id = expert_ids // local_experts
    local_id = expert_ids % local_experts
    target = ((owner_id ^ me) * local_experts + local_id) * capacity + slot_index
    place = (target[None, :] == jnp.arange(slots, dtype=jnp.int32)[:, None]).astype(jnp.bfloat16)

    def pack(values):
        packed = jnp.dot(place, values, preferred_element_type=jnp.float32).astype(values.dtype)
        return packed.reshape(owners, local_experts, capacity, width)

    def block_of(got):
        return jnp.stack(got, axis=1).reshape(local_experts, owners * capacity, width)

    slot_iota = jnp.arange(slots, dtype=jnp.int32)
    row_of_slot = (
        (slot_iota // capacity % local_experts) * owners + slot_iota // (local_experts * capacity)
    ) * capacity + slot_iota % capacity
    reorder = (row_of_slot[:, None] == slot_iota[None, :]).astype(jnp.bfloat16)

    def pick(spec, onehot, values):
        found = jnp.einsum(spec, onehot, values, preferred_element_type=jnp.float32)
        return found.astype(jnp.bfloat16)

    def in_chunks(line):
        shape = (owners, local_experts * capacity, width)
        return jnp.stack([v.reshape(shape) for v in line], axis=1)

    def by_column(got):
        return [jnp.concatenate([g[j] for g in got], axis=0) for j in range(cols)]

    digits = jnp.stack([target // 256, target % 256]).astype(jnp.bfloat16)
    digits = jnp.pad(digits, ((0, 6), (0, width - tok_rows)))
    blocks_tok = [[jnp.concatenate([tokens, digits], axis=0)]]
    packed_grad = pack(out_grad)
    came, crossed_tok = [], []
    for k in range(rows):
        came.append(gather_step(blocks_tok, k, "tok", came[-1] if came else ()))
        if k == 0:
            got_grad = exchange(packed_grad, "grad")
            got_grad = lax.optimization_barrier((*got_grad, *came[k]))[: len(got_grad)]
            blocks_grad = [[block_of(got_grad)]]
        gather_step(blocks_grad, k, "grad", came[k], True)
    for k in range(rows):
        line = []
        for block in blocks_tok[k]:
            at = block[tok_rows : tok_rows + 2, :tok_rows].astype(jnp.int32)
            at = at[0] * 256 + at[1]
            at = (at[None, :] == slot_iota[:, None]).astype(jnp.bfloat16)
            line.append(pick("rt,td->rd", at, block[:tok_rows]))
        crossed_tok.append(cross(in_chunks(line), f"tok{k}"))

    rows_tok, active, slope, parts = [], [], [], []
    for k in range(rows):
        got, settled = settle(crossed_tok[k], f"tok{k}", came[k + 1] if k + 1 < rows else ())
        rows_k = [
            pick("cr,cd->rd", reorder, v).reshape(local_experts, owners * capacity, width)
            for v in by_column(got)
        ]
        rows_k = jnp.concatenate(rows_k, axis=1)
        hidden_k = jnp.einsum(
            "erd,edf->erf", rows_k, up_weight, preferred_element_type=jnp.float32
        )
        hidden_k = lax.optimization_barrier(hidden_k)
        active_k, slope_k = lax.optimization_barrier(
            (gelu_value(hidden_k).astype(jnp.bfloat16), gelu_slope(hidden_k))
        )
        part_k = jnp.einsum(
            "erf,efd->erd", active_k, down_weight, preferred_element_type=jnp.float32
        )
        parts.append(part_k.reshape(local_experts, cols, owners * capacity, width))
        rows_tok.append(rows_k)
        active.append(active_k)
        slope.append(slope_k)

    over_y = []

    def column_sum(k):
        total = parts[k][:, cols - 1].astype(jnp.bfloat16)
        if k == 0 and over_y:
            total = after(total, over_y[-1])
        for j in reversed(range(cols - 1)):
            over_y.append(ring_y(total, -1, f"out_y{k}"))
            total = over_y[-1].astype(jnp.float32) + parts[k][:, j]
            if j > 0:
                total = total.astype(jnp.bfloat16)
        return total.astype(jnp.float32)

    sums = [column_sum(k) for k in range(1, rows)]
    sums = [column_sum(0), *sums]
    summed, over_z = sums[0], []
    for ks, step in ((range(rows // 2, 0, -1), -1), (range(rows // 2 + 1, rows), 1)):
        total = None
        for k in ks:
            total = sums[k] if total is None else total + sums[k]
            over_z.append(ring_z(total.astype(jnp.bfloat16), step, f"out_z{k}"))
            total = over_z[-1].astype(jnp.float32)
        if total is not None:
            summed = summed + total
    summed = summed.astype(jnp.bfloat16)
    summed = pick("cr,rd->cd", reorder, summed.reshape(slots, width))
    returned = exchange(summed.reshape(owners, local_experts * capacity, width), "back")
    returned = jnp.concatenate(returned, axis=0)
    combined = pick("rt,rd->td", place, returned)

    rows_grad = jnp.concatenate([b for line in blocks_grad for b in line], axis=1)
    rows_tok = jnp.concatenate(rows_tok, axis=1)
    active = jnp.concatenate(active, axis=1)
    slope = jnp.concatenate(slope, axis=1)

    back_grad = jnp.einsum(
        "erd,efd->erf", rows_grad, down_weight, preferred_element_type=jnp.float32
    )
    pre_grad = lax.optimization_barrier((back_grad * slope).astype(jnp.bfloat16))
    down_part = jnp.einsum(
        "erf,erd->efd", active, rows_grad, preferred_element_type=jnp.float32
    ).astype(jnp.bfloat16)
    up_part = jnp.einsum(
        "erd,erf->edf", rows_tok, pre_grad, preferred_element_type=jnp.float32
    ).astype(jnp.bfloat16)
    return (combined, up_part, down_part)


def solution(mesh):
    in_specs = (
        P(("expert", "dp"), None),
        P(("expert", "dp")),
        P("expert", None, "dp"),
        P("expert", "dp", None),
        P(("expert", "dp"), None),
    )
    out_specs = (P(("expert", "dp"), None), P("expert", None, "dp"), P("expert", "dp", None))
    return jax.shard_map(
        on_device, mesh=mesh, in_specs=in_specs, out_specs=out_specs, check_vma=False
    )
```

time: 158 us -> 128 us (0.81)
  waiting for transfers between devices: 87.4 us -> 56.3 us
  starting transfers between devices: 37.8 us -> 30.5 us
  matrix products: 23.1 us -> 27.9 us
  local copies, waits for them, and re-layouts: 3.93 us -> 5.55 us
    ppermute x12 -> x11, waiting for transfers between devices: 56.3 us -> 20.3 us  [ring_y(): return lax.ppermute(value, 'dp', perm)]
    ppermute x9 -> x11, waiting for transfers between devices: 22.4 us -> 36 us  [ring_z(): return lax.ppermute(value, 'dp', perm)]
    dot_general x5 -> x28, matrix products: 6.37 us -> 18.6 us  [the longest x18 6.43 us: pick(): found = jnp.einsum(spec, onehot, values, preferred_element_type=jnp.float32)]
    ppermute x9 -> x14, waiting for transfers between devices: 8.58 us -> 0.04 us  [swap_expert(): return lax.ppermute(value, 'expert', [(i, i ^ mask) for i in range(n)])]
    ppermute x9 -> x11, starting transfers between devices: 12.9 us -> 4.79 us  [ring_z(): return lax.ppermute(value, 'dp', perm)]
    dot_general x1, matrix products: 12 us -> 4.65 us  [on_device(): jnp.einsum('erd,erf->edf', rows_tok, pre_grad, preferred_element_type=jnp...]
    convert_element_type x4 -> x12, other arithmetic: 2.77 us -> 0.53 us  [the longest x3 0.28 us: on_device(): over_z.append(ring_z(total.astype(jnp.bfloat16), step, f'out_z{k}'))]
    ppermute x9 -> x14, starting transfers between devices: 8.17 us -> 10.1 us  [swap_expert(): return lax.ppermute(value, 'expert', [(i, i ^ mask) for i in range(n)])]
  transfers between devices with their start and end apart: 30 -> 36, of which waited for: 17 -> 16; matrix products, arithmetic and copies ran while one was open for 16% -> 25% of each run, Pallas kernels for 0% -> 0%
where the time goes in v4:
time: 128 us; the launch traced here: 127 us
  waiting for transfers between devices  56.3 us (44%)
  starting transfers between devices  30.5 us (24%)
  matrix products  27.9 us (22%)
  local copies, waits for them, and re-layouts  5.55 us (4%)
  other arithmetic  5.36 us (4%)
  between operations  1.62 us (1%)
    ppermute x11, waiting for transfers between devices, ring_z(): return lax.ppermute(value, 'dp', perm)  36 us
    ppermute x11, waiting for transfers between devices, ring_y(): return lax.ppermute(value, 'dp', perm)  20.3 us
    ppermute x11, starting transfers between devices, ring_y(): return lax.ppermute(value, 'dp', perm)  15.6 us
    ppermute x14, starting transfers between devices, swap_expert(): return lax.ppermute(value, 'expert', [(i, i ^ mask) for i in range(n)])  10.1 us
    dot_general x18, matrix products, pick(): found = jnp.einsum(spec, onehot, values, preferred_element_type=jnp.float32)  6.43 us
    ppermute x11, starting transfers between devices, ring_z(): return lax.ppermute(value, 'dp', perm)  4.79 us
    dot_general x1, matrix products, on_device(): jnp.einsum('erf,erd->efd', active, rows_grad, preferred_element_type=jnp....  4.65 us
    dot_general x1, matrix products, on_device(): jnp.einsum('erd,erf->edf', rows_tok, pre_grad, preferred_element_type=jnp...  4.65 us
  transfers between devices with their start and end apart: 36, of which 16 were waited for; matrix products, arithmetic and copies ran while one was open for 25% of the time, Pallas kernels for 0%

profile of v4, /device:TPU:0, one launch (start us, length us, event | category | flops | bytes accessed | tf_op | source)
XLA Modules:
  0.0 127.3 jit_solution(1237662722957209129)
XLA Ops:
  3.2 3.0 %collective-permute-start = (bf16[136,1280]{1,0:T(8,128)(2,1)S(1)}, bf16[136,1280]{1,0:T(8,128)(2,1)S(1)}, u32[]{:S(2)}, u32[]{:S(2)}) collective-permute-start(bf16[136,1280]{1,0:T(8,128)(2,1)S(1)} %fusion.130), channel_id=1, source_target_pairs={{0,1},{1,0},{2,3},{3,2},{4,5},{5,4},{6,7},{7,6},{8,9},{9,8},{10,11... | collective-permute-start | bytes 1044488 | tf_op jit(solution)/shard_map/tok_y0/ppermute | solution.py:48
  10.7 3.7 %collective-permute-done = bf16[136,1280]{1,0:T(8,128)(2,1)S(1)} collective-permute-done((bf16[136,1280]{1,0:T(8,128)(2,1)S(1)}, bf16[136,1280]{1,0:T(8,128)(2,1)S(1)}, u32[]{:S(2)}, u32[]{:S(2)}) %collective-permute-start) | collective-permute-done | bytes 348192 | tf_op jit(solution)/shard_map/tok_y0/ppermute | solution.py:48
  14.4 3.3 %collective-permute-done.2 = bf16[136,1280]{1,0:T(8,128)(2,1)S(1)} collective-permute-done((bf16[136,1280]{1,0:T(8,128)(2,1)S(1)}, bf16[136,1280]{1,0:T(8,128)(2,1)S(1)}, u32[]{:S(2)}, u32[]{:S(2)}) %collective-permute-start.2) | collective-permute-done | bytes 348192 | tf_op jit(solution)/shard_map/tok_z1/ppermute | solution.py:40
  18.7 1.6 %collective-permute-start.29 = (bf16[4,40,1280]{2,1,0:T(8,128)(2,1)S(1)}, bf16[4,40,1280]{2,1,0:T(8,128)(2,1)S(1)}, u32[]{:S(2)}, u32[]{:S(2)}) collective-permute-start(bf16[4,40,1280]{2,1,0:T(8,128)(2,1)S(1)} %copy.65), channel_id=1, source_target_pairs={{0,1},{1,0},{2,3},{3,2},{4,5},{5,4},{6,7},{7,6},{8,9},{9,8},{10,11... | collective-permute-start | bytes 1228808 | tf_op jit(solution)/shard_map/grad_y0/ppermute | solution.py:48
  23.8 5.0 %collective-permute-done.3 = bf16[136,1280]{1,0:T(8,128)(2,1)S(1)} collective-permute-done((bf16[136,1280]{1,0:T(8,128)(2,1)S(1)}, bf16[136,1280]{1,0:T(8,128)(2,1)S(1)}, u32[]{:S(2)}, u32[]{:S(2)}) %collective-permute-start.3) | collective-permute-done | bytes 348192 | tf_op jit(solution)/shard_map/tok_y1/ppermute | solution.py:48
  28.8 2.3 %collective-permute-done.4 = bf16[136,1280]{1,0:T(8,128)(2,1)S(1)} collective-permute-done((bf16[136,1280]{1,0:T(8,128)(2,1)S(1)}, bf16[136,1280]{1,0:T(8,128)(2,1)S(1)}, u32[]{:S(2)}, u32[]{:S(2)}) %collective-permute-start.4) | collective-permute-done | bytes 348192 | tf_op jit(solution)/shard_map/tok_z2/ppermute | solution.py:40
  35.0 2.6 %collective-permute-done.29 = bf16[4,40,1280]{2,1,0:T(8,128)(2,1)S(1)} collective-permute-done((bf16[4,40,1280]{2,1,0:T(8,128)(2,1)S(1)}, bf16[4,40,1280]{2,1,0:T(8,128)(2,1)S(1)}, u32[]{:S(2)}, u32[]{:S(2)}) %collective-permute-start.29) | collective-permute-done | bytes 409632 | tf_op jit(solution)/shard_map/grad_y0/ppermute | solution.py:48
  37.6 2.3 %collective-permute-done.30 = bf16[4,40,1280]{2,1,0:T(8,128)(2,1)S(1)} collective-permute-done((bf16[4,40,1280]{2,1,0:T(8,128)(2,1)S(1)}, bf16[4,40,1280]{2,1,0:T(8,128)(2,1)S(1)}, u32[]{:S(2)}, u32[]{:S(2)}) %collective-permute-start.30) | collective-permute-done | bytes 409632 | tf_op jit(solution)/shard_map/grad_z1/ppermute | solution.py:40
  41.6 3.5 %collective-permute-done.7 = bf16[136,1280]{1,0:T(8,128)(2,1)S(1)} collective-permute-done((bf16[136,1280]{1,0:T(8,128)(2,1)S(1)}, bf16[136,1280]{1,0:T(8,128)(2,1)S(1)}, u32[]{:S(2)}, u32[]{:S(2)}) %collective-permute-start.7) | collective-permute-done | bytes 348192 | tf_op jit(solution)/shard_map/tok_y2/ppermute | solution.py:48
  45.1 2.3 %collective-permute-done.6 = bf16[136,1280]{1,0:T(8,128)(2,1)S(1)} collective-permute-done((bf16[136,1280]{1,0:T(8,128)(2,1)S(1)}, bf16[136,1280]{1,0:T(8,128)(2,1)S(1)}, u32[]{:S(2)}, u32[]{:S(2)}) %collective-permute-start.6) | collective-permute-done | bytes 348192 | tf_op jit(solution)/shard_map/tok_z3/ppermute | solution.py:40
  48.1 1.6 %collective-permute-start.9 = (bf16[64,1280]{1,0:T(8,128)(2,1)S(1)}, bf16[64,1280]{1,0:T(8,128)(2,1)S(1)}, u32[]{:S(2)}, u32[]{:S(2)}) collective-permute-start(bf16[64,1280]{1,0:T(8,128)(2,1)S(1)} %slice.419), channel_id=1, source_target_pairs={{0,1},{1,0},{2,3},{3,2},{4,5},{5,4},{6,7},{7,6},{8,9},{9,8},{10,11... | collective-permute-start | bytes 491528 | tf_op jit(solution)/shard_map/tok_y3/ppermute | solution.py:48
  63.0 1.6 %collective-permute-start.20 = (bf16[4,40,1280]{2,1,0:T(8,128)(2,1)S(1)}, bf16[4,40,1280]{2,1,0:T(8,128)(2,1)S(1)}, u32[]{:S(2)}, u32[]{:S(2)}) collective-permute-start(bf16[4,40,1280]{2,1,0:T(8,128)(2,1)S(1)} %fusion.66), channel_id=1, source_target_pairs={{0,1},{1,0},{2,3},{3,2},{4,5},{5,4},{6,7},{7,6},{8,9},{9,8},{10,11... | collective-permute-start | bytes 1228808 | tf_op jit(solution)/shard_map/out_y1/ppermute | solution.py:48
  64.6 3.4 %collective-permute-done.33 = bf16[4,40,1280]{2,1,0:T(8,128)(2,1)S(1)} collective-permute-done((bf16[4,40,1280]{2,1,0:T(8,128)(2,1)S(1)}, bf16[4,40,1280]{2,1,0:T(8,128)(2,1)S(1)}, u32[]{:S(2)}, u32[]{:S(2)}) %collective-permute-start.33) | collective-permute-done | bytes 409632 | tf_op jit(solution)/shard_map/grad_y2/ppermute | solution.py:48
  68.1 1.9 %collective-permute-done.34 = bf16[4,40,1280]{2,1,0:T(8,128)(2,1)S(1)} collective-permute-done((bf16[4,40,1280]{2,1,0:T(8,128)(2,1)S(1)}, bf16[4,40,1280]{2,1,0:T(8,128)(2,1)S(1)}, u32[]{:S(2)}, u32[]{:S(2)}) %collective-permute-start.34) | collective-permute-done | bytes 409632 | tf_op jit(solution)/shard_map/grad_z3/ppermute | solution.py:40
  73.5 1.6 %collective-permute-start.16 = (bf16[4,40,1280]{2,1,0:T(8,128)(2,1)S(1)}, bf16[4,40,1280]{2,1,0:T(8,128)(2,1)S(1)}, u32[]{:S(2)}, u32[]{:S(2)}) collective-permute-start(bf16[4,40,1280]{2,1,0:T(8,128)(2,1)S(1)} %fusion.65), channel_id=1, source_target_pairs={{0,1},{1,0},{2,3},{3,2},{4,5},{5,4},{6,7},{7,6},{8,9},{9,8},{10,11... | collective-permute-start | bytes 1228808 | tf_op jit(solution)/shard_map/out_y2/ppermute | solution.py:48
  75.2 5.5 %collective-permute-done.35 = bf16[4,40,1280]{2,1,0:T(8,128)(2,1)S(1)} collective-permute-done((bf16[4,40,1280]{2,1,0:T(8,128)(2,1)S(1)}, bf16[4,40,1280]{2,1,0:T(8,128)(2,1)S(1)}, u32[]{:S(2)}, u32[]{:S(2)}) %collective-permute-start.35) | collective-permute-done | bytes 409632 | tf_op jit(solution)/shard_map/grad_z4/ppermute | solution.py:40
  80.7 1.6 %copy-done.3 = bf16[4,320,1280]{2,1,0:T(8,128)(2,1)} copy-done((bf16[4,320,1280]{2,1,0:T(8,128)(2,1)}, bf16[4,320,1280]{2,1,0:T(8,128)(2,1)S(1)}, u32[]{:S(2)}) %copy-start.3) | copy-done | bytes 3276824
  86.2 3.8 %fusion = bf16[4,320,512]{2,1,0:T(8,128)(2,1)S(1)} fusion(f32[4,80,512]{2,1,0:T(8,128)S(1)} %get-tuple-element.56, f32[4,80,512]{2,1,0:T(8,128)S(1)} %get-tuple-element.55, f32[4,80,512]{2,1,0:T(8,128)S(1)} %get-tuple-element.54, f32[4,80,512]{2,1,0:T(8,128)S(1)} %get-tuple-element.53, bf16[4,320,1280]{2,1,0:T(8,128)(2,1)} %copy-done.3, ...), kind=kOutput, calls=%fused_computation.3 | convolution fusion | flops 1680998400 | bytes 12451840 | tf_op jit(solution)/shard_map/erd,efd->erf/dot_general | solution.py:221
  91.7 1.8 %collective-permute-start.17 = (bf16[4,40,1280]{2,1,0:T(8,128)(2,1)S(1)}, bf16[4,40,1280]{2,1,0:T(8,128)(2,1)S(1)}, u32[]{:S(2)}, u32[]{:S(2)}) collective-permute-start(bf16[4,40,1280]{2,1,0:T(8,128)(2,1)S(1)} %fusion.14), channel_id=1, source_target_pairs={{0,6},{1,7},{2,0},{3,1},{4,2},{5,3},{6,4},{7,5},{8,14},{9,15},{10,... | collective-permute-start | bytes 1228808 | tf_op jit(solution)/shard_map/out_z2/ppermute | solution.py:40
  93.5 2.1 %collective-permute-done.12 = bf16[4,40,1280]{2,1,0:T(8,128)(2,1)S(1)} collective-permute-done((bf16[4,40,1280]{2,1,0:T(8,128)(2,1)S(1)}, bf16[4,40,1280]{2,1,0:T(8,128)(2,1)S(1)}, u32[]{:S(2)}, u32[]{:S(2)}) %collective-permute-start.12) | collective-permute-done | bytes 409632 | tf_op jit(solution)/shard_map/out_y3/ppermute | solution.py:48
  96.5 13.6 %collective-permute-done.17 = bf16[4,40,1280]{2,1,0:T(8,128)(2,1)S(1)} collective-permute-done((bf16[4,40,1280]{2,1,0:T(8,128)(2,1)S(1)}, bf16[4,40,1280]{2,1,0:T(8,128)(2,1)S(1)}, u32[]{:S(2)}, u32[]{:S(2)}) %collective-permute-start.17) | collective-permute-done | bytes 409632 | tf_op jit(solution)/shard_map/out_z2/ppermute | solution.py:40
  110.3 4.7 %convolution_convert_fusion = bf16[4,512,1280]{2,1,0:T(8,128)(2,1)} fusion(bf16[4,320,1280]{2,1,0:T(8,128)(2,1)S(1)} %copy-done.4, bf16[4,80,512]{2,1,0:T(8,128)(2,1)S(1)} %get-tuple-element.37, bf16[4,80,512]{2,1,0:T(8,128)(2,1)S(1)} %get-tuple-element.41, bf16[4,80,512]{2,1,0:T(8,128)(2,1)S(1)} %get-tuple-element.44, ...), kind=kOutput, calls=%fused_computation | convolution fusion | flops 1685585920 | bytes 9830400 | tf_op jit(solution)/shard_map/erf,erd->efd/dot_general | solution.py:225
  115.0 4.1 %collective-permute-done.21 = bf16[4,40,1280]{2,1,0:T(8,128)(2,1)S(1)} collective-permute-done((bf16[4,40,1280]{2,1,0:T(8,128)(2,1)S(1)}, bf16[4,40,1280]{2,1,0:T(8,128)(2,1)S(1)}, u32[]{:S(2)}, u32[]{:S(2)}) %collective-permute-start.21) | collective-permute-done | bytes 409632 | tf_op jit(solution)/shard_map/out_z1/ppermute | solution.py:40
  121.6 4.7 %convolution_convert_fusion.1 = bf16[4,1280,512]{2,1,0:T(8,128)(2,1)} fusion(bf16[4,320,1280]{2,1,0:T(8,128)(2,1)S(1)} %copy-done.6, bf16[4,320,512]{2,1,0:T(8,128)(2,1)S(1)} %fusion), kind=kOutput, calls=%fused_computation.1 | convolution fusion | flops 1680343040 | bytes 9830400 | tf_op jit(solution)/shard_map/erd,erf->edf/dot_general | solution.py:228
  (196 shorter events, 44.2 us)
Async XLA Ops:
  3.2 11.2 %collective-permute-start = (bf16[136,1280]{1,0:T(8,128)(2,1)S(1)}, bf16[136,1280]{1,0:T(8,128)(2,1)S(1)}, u32[]{:S(2)}, u32[]{:S(2)}) collective-permute-start(bf16[136,1280]{1,0:T(8,128)(2,1)S(1)} %fusion.130), channel_id=1, source_target_pairs={{0,1},{1,0},{2,3},{3,2},{4,5},{5,4},{6,7},{7,6},{8,9},{9,8},{10,11... | collective-permute-start | bytes 1044488 | tf_op jit(solution)/shard_map/tok_y0/ppermute | solution.py:48
  6.2 11.5 %collective-permute-start.2 = (bf16[136,1280]{1,0:T(8,128)(2,1)S(1)}, bf16[136,1280]{1,0:T(8,128)(2,1)S(1)}, u32[]{:S(2)}, u32[]{:S(2)}) collective-permute-start(bf16[136,1280]{1,0:T(8,128)(2,1)S(1)} %fusion.130), channel_id=1, source_target_pairs={{0,2},{1,3},{2,4},{3,5},{4,6},{5,7},{6,0},{7,1},{8,10},{9,11},{10,... | collective-permute-start | bytes 1044488 | tf_op jit(solution)/shard_map/tok_z1/ppermute | solution.py:40
  17.7 11.1 %collective-permute-start.3 = (bf16[136,1280]{1,0:T(8,128)(2,1)S(1)}, bf16[136,1280]{1,0:T(8,128)(2,1)S(1)}, u32[]{:S(2)}, u32[]{:S(2)}) collective-permute-start(bf16[136,1280]{1,0:T(8,128)(2,1)S(1)} %collective-permute-done.2), channel_id=1, source_target_pairs={{0,1},{1,0},{2,3},{3,2},{4,5},{5,4},{6,7},{7,6},{8,9},{9,8},{10,11... | collective-permute-start | bytes 1044488 | tf_op jit(solution)/shard_map/tok_y1/ppermute | solution.py:48
  18.2 12.9 %collective-permute-start.4 = (bf16[136,1280]{1,0:T(8,128)(2,1)S(1)}, bf16[136,1280]{1,0:T(8,128)(2,1)S(1)}, u32[]{:S(2)}, u32[]{:S(2)}) collective-permute-start(bf16[136,1280]{1,0:T(8,128)(2,1)S(1)} %collective-permute-done.2), channel_id=1, source_target_pairs={{0,2},{1,3},{2,4},{3,5},{4,6},{5,7},{6,0},{7,1},{8,10},{9,11},{10,... | collective-permute-start | bytes 1044488 | tf_op jit(solution)/shard_map/tok_z2/ppermute | solution.py:40
  18.7 18.9 %collective-permute-start.29 = (bf16[4,40,1280]{2,1,0:T(8,128)(2,1)S(1)}, bf16[4,40,1280]{2,1,0:T(8,128)(2,1)S(1)}, u32[]{:S(2)}, u32[]{:S(2)}) collective-permute-start(bf16[4,40,1280]{2,1,0:T(8,128)(2,1)S(1)} %copy.65), channel_id=1, source_target_pairs={{0,1},{1,0},{2,3},{3,2},{4,5},{5,4},{6,7},{7,6},{8,9},{9,8},{10,11... | collective-permute-start | bytes 1228808 | tf_op jit(solution)/shard_map/grad_y0/ppermute | solution.py:48
  20.3 19.6 %collective-permute-start.30 = (bf16[4,40,1280]{2,1,0:T(8,128)(2,1)S(1)}, bf16[4,40,1280]{2,1,0:T(8,128)(2,1)S(1)}, u32[]{:S(2)}, u32[]{:S(2)}) collective-permute-start(bf16[4,40,1280]{2,1,0:T(8,128)(2,1)S(1)} %copy.65), channel_id=1, source_target_pairs={{0,2},{1,3},{2,4},{3,5},{4,6},{5,7},{6,0},{7,1},{8,10},{9,11},{10,... | collective-permute-start | bytes 1228808 | tf_op jit(solution)/shard_map/grad_z1/ppermute | solution.py:40
  22.0 11.4 %collective-permute-start.1 = (bf16[2,2,40,1280]{3,2,0,1:T(8,128)(2,1)S(1)}, bf16[2,2,40,1280]{3,2,0,1:T(8,128)(2,1)S(1)}, u32[]{:S(2)}, u32[]{:S(2)}) collective-permute-start(bf16[2,2,40,1280]{3,2,0,1:T(8,128)(2,1)S(1)} %get-tuple-element.65), channel_id=1, source_target_pairs={{0,16},{8,24},{16,0},{24,8},{1,17},{9,25},{17,1},{25,9},{2,18},{10... | collective-permute-start | bytes 1228808 | tf_op jit(solution)/shard_map/tok0_x2/ppermute | solution.py:54
  31.1 16.2 %collective-permute-start.6 = (bf16[136,1280]{1,0:T(8,128)(2,1)S(1)}, bf16[136,1280]{1,0:T(8,128)(2,1)S(1)}, u32[]{:S(2)}, u32[]{:S(2)}) collective-permute-start(bf16[136,1280]{1,0:T(8,128)(2,1)S(1)} %collective-permute-done.4), channel_id=1, source_target_pairs={{0,2},{1,3},{2,4},{3,5},{4,6},{5,7},{6,0},{7,1},{8,10},{9,11},{10,... | collective-permute-start | bytes 1044488 | tf_op jit(solution)/shard_map/tok_z3/ppermute | solution.py:40
  31.1 13.9 %collective-permute-start.7 = (bf16[136,1280]{1,0:T(8,128)(2,1)S(1)}, bf16[136,1280]{1,0:T(8,128)(2,1)S(1)}, u32[]{:S(2)}, u32[]{:S(2)}) collective-permute-start(bf16[136,1280]{1,0:T(8,128)(2,1)S(1)} %collective-permute-done.4), channel_id=1, source_target_pairs={{0,1},{1,0},{2,3},{3,2},{4,5},{5,4},{6,7},{7,6},{8,9},{9,8},{10,11... | collective-permute-start | bytes 1044488 | tf_op jit(solution)/shard_map/tok_y2/ppermute | solution.py:48
  33.3 14.8 %collective-permute-start.18 = (bf16[2,2,40,1280]{3,2,0,1:T(8,128)(2,1)S(1)}, bf16[2,2,40,1280]{3,2,0,1:T(8,128)(2,1)S(1)}, u32[]{:S(2)}, u32[]{:S(2)}) collective-permute-start(bf16[2,2,40,1280]{3,2,0,1:T(8,128)(2,1)S(1)} %get-tuple-element.63), channel_id=1, source_target_pairs={{0,16},{8,24},{16,0},{24,8},{1,17},{9,25},{17,1},{25,9},{2,18},{10... | collective-permute-start | bytes 1228808 | tf_op jit(solution)/shard_map/tok1_x2/ppermute | solution.py:54
  39.9 15.7 %collective-permute-start.31 = (bf16[4,40,1280]{2,1,0:T(8,128)(2,1)S(1)}, bf16[4,40,1280]{2,1,0:T(8,128)(2,1)S(1)}, u32[]{:S(2)}, u32[]{:S(2)}) collective-permute-start(bf16[4,40,1280]{2,1,0:T(8,128)(2,1)S(1)} %collective-permute-done.30), channel_id=1, source_target_pairs={{0,1},{1,0},{2,3},{3,2},{4,5},{5,4},{6,7},{7,6},{8,9},{9,8},{10,11... | collective-permute-start | bytes 1228808 | tf_op jit(solution)/shard_map/grad_y1/ppermute | solution.py:48
  41.4 14.3 %collective-permute-start.32 = (bf16[4,40,1280]{2,1,0:T(8,128)(2,1)S(1)}, bf16[4,40,1280]{2,1,0:T(8,128)(2,1)S(1)}, u32[]{:S(2)}, u32[]{:S(2)}) collective-permute-start(bf16[4,40,1280]{2,1,0:T(8,128)(2,1)S(1)} %collective-permute-done.30), channel_id=1, source_target_pairs={{0,2},{1,3},{2,4},{3,5},{4,6},{5,7},{6,0},{7,1},{8,10},{9,11},{10,... | collective-permute-start | bytes 1228808 | tf_op jit(solution)/shard_map/grad_z2/ppermute | solution.py:40
  47.3 10.4 %collective-permute-start.8 = (bf16[72,1280]{1,0:T(8,128)(2,1)S(1)}, bf16[72,1280]{1,0:T(8,128)(2,1)S(1)}, u32[]{:S(2)}, u32[]{:S(2)}) collective-permute-start(bf16[72,1280]{1,0:T(8,128)(2,1)S(1)} %slice.500), channel_id=1, source_target_pairs={{0,2},{1,3},{2,4},{3,5},{4,6},{5,7},{6,0},{7,1},{8,10},{9,11},{10,... | collective-permute-start | bytes 552968 | tf_op jit(solution)/shard_map/tok_z4/ppermute | solution.py:40
  55.7 12.3 %collective-permute-start.33 = (bf16[4,40,1280]{2,1,0:T(8,128)(2,1)S(1)}, bf16[4,40,1280]{2,1,0:T(8,128)(2,1)S(1)}, u32[]{:S(2)}, u32[]{:S(2)}) collective-permute-start(bf16[4,40,1280]{2,1,0:T(8,128)(2,1)S(1)} %collective-permute-done.32), channel_id=1, source_target_pairs={{0,1},{1,0},{2,3},{3,2},{4,5},{5,4},{6,7},{7,6},{8,9},{9,8},{10,11... | collective-permute-start | bytes 1228808 | tf_op jit(solution)/shard_map/grad_y2/ppermute | solution.py:48
  57.7 12.2 %collective-permute-start.34 = (bf16[4,40,1280]{2,1,0:T(8,128)(2,1)S(1)}, bf16[4,40,1280]{2,1,0:T(8,128)(2,1)S(1)}, u32[]{:S(2)}, u32[]{:S(2)}) collective-permute-start(bf16[4,40,1280]{2,1,0:T(8,128)(2,1)S(1)} %collective-permute-done.32), channel_id=1, source_target_pairs={{0,2},{1,3},{2,4},{3,5},{4,6},{5,7},{6,0},{7,1},{8,10},{9,11},{10,... | collective-permute-start | bytes 1228808 | tf_op jit(solution)/shard_map/grad_z3/ppermute | solution.py:40
  58.1 11.9 %collective-permute-start.10 = (bf16[2,2,40,1280]{3,2,1,0:T(8,128)(2,1)S(1)}, bf16[2,2,40,1280]{3,2,1,0:T(8,128)(2,1)S(1)}, u32[]{:S(2)}, u32[]{:S(2)}) collective-permute-start(bf16[2,2,40,1280]{3,2,1,0:T(8,128)(2,1)S(1)} %pad_maximum_fusion.3), channel_id=1, source_target_pairs={{0,16},{8,24},{16,0},{24,8},{1,17},{9,25},{17,1},{25,9},{2,18},{10... | collective-permute-start | bytes 1228808 | tf_op jit(solution)/shard_map/tok3_x2/ppermute | solution.py:54
  59.5 10.6 %collective-permute-start.15 = (bf16[2,2,40,1280]{3,2,1,0:T(8,128)(2,1)S(1)}, bf16[2,2,40,1280]{3,2,1,0:T(8,128)(2,1)S(1)}, u32[]{:S(2)}, u32[]{:S(2)}) collective-permute-start(bf16[2,2,40,1280]{3,2,1,0:T(8,128)(2,1)S(1)} %pad_maximum_fusion.6), channel_id=1, source_target_pairs={{0,8},{8,0},{16,24},{24,16},{1,9},{9,1},{17,25},{25,17},{2,10},{10... | collective-permute-start | bytes 1228808 | tf_op jit(solution)/shard_map/tok2_x1/ppermute | solution.py:54
  63.0 33.5 %collective-permute-start.20 = (bf16[4,40,1280]{2,1,0:T(8,128)(2,1)S(1)}, bf16[4,40,1280]{2,1,0:T(8,128)(2,1)S(1)}, u32[]{:S(2)}, u32[]{:S(2)}) collective-permute-start(bf16[4,40,1280]{2,1,0:T(8,128)(2,1)S(1)} %fusion.66), channel_id=1, source_target_pairs={{0,1},{1,0},{2,3},{3,2},{4,5},{5,4},{6,7},{7,6},{8,9},{9,8},{10,11... | collective-permute-start | bytes 1228808 | tf_op jit(solution)/shard_map/out_y1/ppermute | solution.py:48
  68.1 12.6 %collective-permute-start.35 = (bf16[4,40,1280]{2,1,0:T(8,128)(2,1)S(1)}, bf16[4,40,1280]{2,1,0:T(8,128)(2,1)S(1)}, u32[]{:S(2)}, u32[]{:S(2)}) collective-permute-start(bf16[4,40,1280]{2,1,0:T(8,128)(2,1)S(1)} %collective-permute-done.33), channel_id=1, source_target_pairs={{0,2},{1,3},{2,4},{3,5},{4,6},{5,7},{6,0},{7,1},{8,10},{9,11},{10,... | collective-permute-start | bytes 1228808 | tf_op jit(solution)/shard_map/grad_z4/ppermute | solution.py:40
  70.1 10.6 %collective-permute-start.11 = (bf16[2,2,40,1280]{3,2,1,0:T(8,128)(2,1)S(1)}, bf16[2,2,40,1280]{3,2,1,0:T(8,128)(2,1)S(1)}, u32[]{:S(2)}, u32[]{:S(2)}) collective-permute-start(bf16[2,2,40,1280]{3,2,1,0:T(8,128)(2,1)S(1)} %fusion.62), channel_id=1, source_target_pairs={{0,8},{8,0},{16,24},{24,16},{1,9},{9,1},{17,25},{25,17},{2,10},{10... | collective-permute-start | bytes 1228808 | tf_op jit(solution)/shard_map/tok3_x1/ppermute | solution.py:54
  73.5 18.1 %collective-permute-start.16 = (bf16[4,40,1280]{2,1,0:T(8,128)(2,1)S(1)}, bf16[4,40,1280]{2,1,0:T(8,128)(2,1)S(1)}, u32[]{:S(2)}, u32[]{:S(2)}) collective-permute-start(bf16[4,40,1280]{2,1,0:T(8,128)(2,1)S(1)} %fusion.65), channel_id=1, source_target_pairs={{0,1},{1,0},{2,3},{3,2},{4,5},{5,4},{6,7},{7,6},{8,9},{9,8},{10,11... | collective-permute-start | bytes 1228808 | tf_op jit(solution)/shard_map/out_y2/ppermute | solution.py:48
  91.7 18.4 %collective-permute-start.17 = (bf16[4,40,1280]{2,1,0:T(8,128)(2,1)S(1)}, bf16[4,40,1280]{2,1,0:T(8,128)(2,1)S(1)}, u32[]{:S(2)}, u32[]{:S(2)}) collective-permute-start(bf16[4,40,1280]{2,1,0:T(8,128)(2,1)S(1)} %fusion.14), channel_id=1, source_target_pairs={{0,6},{1,7},{2,0},{3,1},{4,2},{5,3},{6,4},{7,5},{8,14},{9,15},{10,... | collective-permute-start | bytes 1228808 | tf_op jit(solution)/shard_map/out_z2/ppermute | solution.py:40
  95.6 19.4 %collective-permute-start.22 = (bf16[4,40,1280]{2,1,0:T(8,128)(2,1)S(1)}, bf16[4,40,1280]{2,1,0:T(8,128)(2,1)S(1)}, u32[]{:S(2)}, u32[]{:S(2)}) collective-permute-start(bf16[4,40,1280]{2,1,0:T(8,128)(2,1)S(1)} %fusion.9), channel_id=1, source_target_pairs={{0,2},{1,3},{2,4},{3,5},{4,6},{5,7},{6,0},{7,1},{8,10},{9,11},{10,... | collective-permute-start | bytes 1228808 | tf_op jit(solution)/shard_map/out_z3/ppermute | solution.py:40
  95.7 19.3 %collective-permute-start.13 = (bf16[4,40,1280]{2,1,0:T(8,128)(2,1)S(1)}, bf16[4,40,1280]{2,1,0:T(8,128)(2,1)S(1)}, u32[]{:S(2)}, u32[]{:S(2)}) collective-permute-start(bf16[4,40,1280]{2,1,0:T(8,128)(2,1)S(1)} %fusion.63), channel_id=1, source_target_pairs={{0,1},{1,0},{2,3},{3,2},{4,5},{5,4},{6,7},{7,6},{8,9},{9,8},{10,11... | collective-permute-start | bytes 1228808 | tf_op jit(solution)/shard_map/out_y0/ppermute | solution.py:48
  (23 other events, 174.5 us)

commit v5 on v4

--- a/solution.py
+++ b/solution.py
@@ -54,11 +54,23 @@
         return lax.ppermute(value, "expert", [(i, i ^ mask) for i in range(n)])
 
 
+def ring_z_to(value, step, mask, name):
+    n, owners = lax.axis_size("dp"), lax.axis_size("expert")
+    rows, cols = grid_of(n)
+    perm = [
+        (e * n + i, (e ^ mask) * n + ((i // cols + step) % rows) * cols + i % cols)
+        for e in range(owners)
+        for i in range(n)
+    ]
+    with jax.named_scope(f"{name}_x{mask}"):
+        return lax.ppermute(value, ("expert", "dp"), perm)
+
+
 def exchange(packed, name):
     return [packed[0]] + [swap_expert(packed[m], m, name) for m in range(1, packed.shape[0])]
 
 
-def gather_step(blocks, k, name, hold=(), last_over_z=False):
+def gather_step(blocks, k, name, hold=()):
     rows, cols = grid_of(lax.axis_size("dp"))
     size = blocks[0][0].shape[0]
     half = size // 32 * 16 if size % 8 == 0 and size >= 32 else size // 2
@@ -68,11 +80,8 @@
     if wait:
         here, beyond, *_ = lax.optimization_barrier((here, beyond, *wait))
     if cols == 2 and k > 0 and k == rows - 1 and half > 0:
-        if last_over_z:
-            blocks[k].append(ring_z(after(blocks[k - 1][1], *hold), 1, f"{name}_z{k + 1}"))
-            return blocks[k][1:]
+        high = ring_z(beyond, 1, f"{name}_z{k + 1}")
         low = ring_y(here[:half], 1, f"{name}_y{k}")
-        high = ring_z(beyond, 1, f"{name}_z{k + 1}")
         blocks[k].append(jnp.concatenate([low, high], axis=0))
         return [low, high]
     if k < rows - 1:
@@ -95,7 +104,7 @@
     if hold:
         got = lax.optimization_barrier((*got, *hold))[: len(got)]
     back = swap_expert(jnp.stack([g[1] for g in got]), 1, name)
-    return [c for q in range(len(got)) for c in (got[q][0], back[q])], back
+    return [c for q in range(len(got)) for c in (got[q][0], back[q])]
 
 
 def on_device(tokens, expert_ids, up_weight, down_weight, out_grad):
@@ -143,15 +152,13 @@
     digits = jnp.pad(digits, ((0, 6), (0, width - tok_rows)))
     blocks_tok = [[jnp.concatenate([tokens, digits], axis=0)]]
     packed_grad = pack(out_grad)
-    came, crossed_tok = [], []
+    came, crossed_tok, blocks_grad = [], [], []
     for k in range(rows):
         came.append(gather_step(blocks_tok, k, "tok", came[-1] if came else ()))
         if k == 0:
             got_grad = exchange(packed_grad, "grad")
             got_grad = lax.optimization_barrier((*got_grad, *came[k]))[: len(got_grad)]
-            blocks_grad = [[block_of(got_grad)]]
-        gather_step(blocks_grad, k, "grad", came[k], True)
-    for k in range(rows):
+            blocks_grad.append([block_of(got_grad)])
         line = []
         for block in blocks_tok[k]:
             at = block[tok_rows : tok_rows + 2, :tok_rows].astype(jnp.int32)
@@ -159,10 +166,12 @@
             at = (at[None, :] == slot_iota[:, None]).astype(jnp.bfloat16)
             line.append(pick("rt,td->rd", at, block[:tok_rows]))
         crossed_tok.append(cross(in_chunks(line), f"tok{k}"))
+        if 0 < k:
+            gather_step(blocks_grad, k - 1, "grad", came[k])
 
     rows_tok, active, slope, parts = [], [], [], []
     for k in range(rows):
-        got, settled = settle(crossed_tok[k], f"tok{k}", came[k + 1] if k + 1 < rows else ())
+        got = settle(crossed_tok[k], f"tok{k}", came[k + 1] if k + 1 < rows else ())
         rows_k = [
             pick("cr,cd->rd", reorder, v).reshape(local_experts, owners * capacity, width)
             for v in by_column(got)
@@ -182,42 +191,30 @@
         rows_tok.append(rows_k)
         active.append(active_k)
         slope.append(slope_k)
-
-    over_y = []
-
-    def column_sum(k):
+    over_y, sums = {}, {}
+    for k in [*range(1, rows), 0]:
         total = parts[k][:, cols - 1].astype(jnp.bfloat16)
-        if k == 0 and over_y:
-            total = after(total, over_y[-1])
+        hold = over_y.get(1) if 1 < k == rows - 1 else over_y.get(rows // 2) if k == 0 else None
+        if hold is not None:
+            total = after(total, hold)
         for j in reversed(range(cols - 1)):
-            over_y.append(ring_y(total, -1, f"out_y{k}"))
-            total = over_y[-1].astype(jnp.float32) + parts[k][:, j]
+            over_y[k] = ring_y(total, -1, f"out_y{k}")
+            total = over_y[k].astype(jnp.float32) + parts[k][:, j]
             if j > 0:
                 total = total.astype(jnp.bfloat16)
-        return total.astype(jnp.float32)
-
-    sums = [column_sum(k) for k in range(1, rows)]
-    sums = [column_sum(0), *sums]
-    summed, over_z = sums[0], []
-    for ks, step in ((range(rows // 2, 0, -1), -1), (range(rows // 2 + 1, rows), 1)):
-        total = None
-        for k in ks:
-            total = sums[k] if total is None else total + sums[k]
-            over_z.append(ring_z(total.astype(jnp.bfloat16), step, f"out_z{k}"))
-            total = over_z[-1].astype(jnp.float32)
-        if total is not None:
-            summed = summed + total
-    summed = summed.astype(jnp.bfloat16)
-    summed = pick("cr,rd->cd", reorder, summed.reshape(slots, width))
-    returned = exchange(summed.reshape(owners, local_experts * capacity, width), "back")
-    returned = jnp.concatenate(returned, axis=0)
-    combined = pick("rt,rd->td", place, returned)
-
+        sums[k] = total.astype(jnp.float32)
+
+    if cols == 2 and rows > 1:
+        blocks_grad[-1].append(ring_z(blocks_grad[-2][1], 1, f"grad_z{rows}"))
+    else:
+        gather_step(blocks_grad, rows - 1, "grad")
+    if rows - 1 in over_y:
+        blocks_grad[-1][-1] = after(blocks_grad[-1][-1], over_y[rows - 1])
     rows_grad = jnp.concatenate([b for line in blocks_grad for b in line], axis=1)
+
     rows_tok = jnp.concatenate(rows_tok, axis=1)
     active = jnp.concatenate(active, axis=1)
     slope = jnp.concatenate(slope, axis=1)
-
     back_grad = jnp.einsum(
         "erd,efd->erf", rows_grad, down_weight, preferred_element_type=jnp.float32
     )
@@ -228,6 +225,30 @@
     up_part = jnp.einsum(
         "erd,erf->edf", rows_tok, pre_grad, preferred_element_type=jnp.float32
     ).astype(jnp.bfloat16)
+
+    def by_owner(total):
+        total = pick("cr,rd->cd", reorder, total.astype(jnp.bfloat16).reshape(slots, width))
+        return list(total.reshape(owners // 2, 2, local_experts * capacity, width))
+
+    total = by_owner(sums[0])
+    arrived = [
+        [total[0]] + [swap_expert(total[q], 2 * q, "own") for q in range(1, owners // 2)]
+    ]
+    for ks, step in ((range(rows // 2, 0, -1), -1), (range(rows // 2 + 1, rows), 1)):
+        total = None
+        for k in ks:
+            total = sums[k] if total is None else total + sums[k]
+            if k == ks[-1]:
+                total = by_owner(total)
+                arrived.append(
+                    [ring_z_to(t, step, 2 * q, f"out_z{k}") for q, t in enumerate(total)]
+                )
+            else:
+                total = ring_z(total.astype(jnp.bfloat16), step, f"out_z{k}").astype(jnp.float32)
+    total = [sum(t.astype(jnp.float32) for t in ts).astype(jnp.bfloat16) for ts in zip(*arrived)]
+    back = swap_expert(jnp.stack([t[1] for t in total]), 1, "back")
+    returned = jnp.concatenate([v for t, other in zip(total, back) for v in (t[0], other)], axis=0)
+    combined = pick("rt,rd->td", place, returned)
     return (combined, up_part, down_part)
 
 

time: 128 us -> 124 us (0.969)
  local copies, waits for them, and re-layouts: 5.55 us -> 2.52 us
  starting transfers between devices: 30.5 us -> 32.8 us
  waiting for transfers between devices: 56.3 us -> 54.3 us
    ppermute x11 -> x9, waiting for transfers between devices: 36 us -> 17.4 us  [ring_z(): return lax.ppermute(value, 'dp', perm)]
    ppermute x11, waiting for transfers between devices: 20.3 us -> 31.6 us  [ring_y(): return lax.ppermute(value, 'dp', perm)]
    ppermute x0 -> x4, starting transfers between devices: none -> 6.66 us  [ring_z_to(): return lax.ppermute(value, ('expert', 'dp'), perm)]
    ppermute x11, starting transfers between devices: 15.6 us -> 11.9 us  [ring_y(): return lax.ppermute(value, 'dp', perm)]
    ppermute x0 -> x4, waiting for transfers between devices: none -> 2.96 us  [ring_z_to(): return lax.ppermute(value, ('expert', 'dp'), perm)]
    unnamed x36 -> x28, local copies, waits for them, and re-layouts: 3.55 us -> 1.17 us
    ppermute x14 -> x13, waiting for transfers between devices: 0.04 us -> 2.39 us  [swap_expert(): return lax.ppermute(value, 'expert', [(i, i ^ mask) for i in range(n)])]
    dot_general x1, matrix products: 3.83 us -> 1.89 us  [on_device(): jnp.einsum('erd,efd->erf', rows_grad, down_weight, preferred_element_type...]
  transfers between devices with their start and end apart: 36 -> 37, of which waited for: 16 -> 16; matrix products, arithmetic and copies ran while one was open for 25% -> 24% of each run, Pallas kernels for 0% -> 0%
where the time goes in v5:
time: 124 us; the launch traced here: 123 us
  waiting for transfers between devices  54.3 us (44%)
  starting transfers between devices  32.8 us (26%)
  matrix products  26.7 us (22%)
  other arithmetic  5.4 us (4%)
  local copies, waits for them, and re-layouts  2.52 us (2%)
  between operations  1.68 us (1%)
    ppermute x11, waiting for transfers between devices, ring_y(): return lax.ppermute(value, 'dp', perm)  31.6 us
    ppermute x9, waiting for transfers between devices, ring_z(): return lax.ppermute(value, 'dp', perm)  17.4 us
    ppermute x11, starting transfers between devices, ring_y(): return lax.ppermute(value, 'dp', perm)  11.9 us
    ppermute x13, starting transfers between devices, swap_expert(): return lax.ppermute(value, 'expert', [(i, i ^ mask) for i in range(n)])  8.41 us
    dot_general x20, matrix products, pick(): found = jnp.einsum(spec, onehot, values, preferred_element_type=jnp.float32)  7.06 us
    ppermute x4, starting transfers between devices, ring_z_to(): return lax.ppermute(value, ('expert', 'dp'), perm)  6.66 us
    ppermute x9, starting transfers between devices, ring_z(): return lax.ppermute(value, 'dp', perm)  5.77 us
    dot_general x1, matrix products, on_device(): jnp.einsum('erd,erf->edf', rows_tok, pre_grad, preferred_element_type=jnp...  4.67 us
  transfers between devices with their start and end apart: 37, of which 16 were waited for; matrix products, arithmetic and copies ran while one was open for 24% of the time, Pallas kernels for 0%

profile of v5, /device:TPU:0, one launch (start us, length us, event | category | flops | bytes accessed | tf_op | source)
XLA Modules:
  0.0 123.3 jit_solution(3495199998724250356)
XLA Ops:
  3.2 3.1 %collective-permute-start.2 = (bf16[136,1280]{1,0:T(8,128)(2,1)S(1)}, bf16[136,1280]{1,0:T(8,128)(2,1)S(1)}, u32[]{:S(2)}, u32[]{:S(2)}) collective-permute-start(bf16[136,1280]{1,0:T(8,128)(2,1)S(1)} %fusion.130), channel_id=1, source_target_pairs={{0,2},{1,3},{2,4},{3,5},{4,6},{5,7},{6,0},{7,1},{8,10},{9,11},{10,... | collective-permute-start | bytes 1044488 | tf_op jit(solution)/shard_map/tok_z1/ppermute | solution.py:40
  6.3 1.5 %collective-permute-start = (bf16[136,1280]{1,0:T(8,128)(2,1)S(1)}, bf16[136,1280]{1,0:T(8,128)(2,1)S(1)}, u32[]{:S(2)}, u32[]{:S(2)}) collective-permute-start(bf16[136,1280]{1,0:T(8,128)(2,1)S(1)} %fusion.130), channel_id=1, source_target_pairs={{0,1},{1,0},{2,3},{3,2},{4,5},{5,4},{6,7},{7,6},{8,9},{9,8},{10,11... | collective-permute-start | bytes 1044488 | tf_op jit(solution)/shard_map/tok_y0/ppermute | solution.py:48
  8.3 1.6 %collective-permute-start.28 = (bf16[4,10,1280]{2,1,0:T(8,128)(2,1)S(1)}, bf16[4,10,1280]{2,1,0:T(8,128)(2,1)S(1)}, u32[]{:S(2)}, u32[]{:S(2)}) collective-permute-start(bf16[4,10,1280]{2,1,0:T(8,128)(2,1)S(1)} %squeeze.196), channel_id=1, source_target_pairs={{0,16},{8,24},{16,0},{24,8},{1,17},{9,25},{17,1},{25,9},{2,18},{10... | collective-permute-start | bytes 307208 | tf_op jit(solution)/shard_map/grad_x2/ppermute | solution.py:54
  10.7 5.8 %collective-permute-done.2 = bf16[136,1280]{1,0:T(8,128)(2,1)S(1)} collective-permute-done((bf16[136,1280]{1,0:T(8,128)(2,1)S(1)}, bf16[136,1280]{1,0:T(8,128)(2,1)S(1)}, u32[]{:S(2)}, u32[]{:S(2)}) %collective-permute-start.2) | collective-permute-done | bytes 348192 | tf_op jit(solution)/shard_map/tok_z1/ppermute | solution.py:40
  17.5 1.5 %collective-permute-start.3 = (bf16[136,1280]{1,0:T(8,128)(2,1)S(1)}, bf16[136,1280]{1,0:T(8,128)(2,1)S(1)}, u32[]{:S(2)}, u32[]{:S(2)}) collective-permute-start(bf16[136,1280]{1,0:T(8,128)(2,1)S(1)} %collective-permute-done.2), channel_id=1, source_target_pairs={{0,1},{1,0},{2,3},{3,2},{4,5},{5,4},{6,7},{7,6},{8,9},{9,8},{10,11... | collective-permute-start | bytes 1044488 | tf_op jit(solution)/shard_map/tok_y1/ppermute | solution.py:48
  19.8 1.6 %collective-permute-start.1 = (bf16[2,2,40,1280]{3,2,0,1:T(8,128)(2,1)S(1)}, bf16[2,2,40,1280]{3,2,0,1:T(8,128)(2,1)S(1)}, u32[]{:S(2)}, u32[]{:S(2)}) collective-permute-start(bf16[2,2,40,1280]{3,2,0,1:T(8,128)(2,1)S(1)} %get-tuple-element.63), channel_id=1, source_target_pairs={{0,16},{8,24},{16,0},{24,8},{1,17},{9,25},{17,1},{25,9},{2,18},{10... | collective-permute-start | bytes 1228808 | tf_op jit(solution)/shard_map/tok0_x2/ppermute | solution.py:54
  21.7 5.9 %collective-permute-done.4 = bf16[136,1280]{1,0:T(8,128)(2,1)S(1)} collective-permute-done((bf16[136,1280]{1,0:T(8,128)(2,1)S(1)}, bf16[136,1280]{1,0:T(8,128)(2,1)S(1)}, u32[]{:S(2)}, u32[]{:S(2)}) %collective-permute-start.4) | collective-permute-done | bytes 348192 | tf_op jit(solution)/shard_map/tok_z2/ppermute | solution.py:40
  31.0 1.5 %collective-permute-start.15 = (bf16[2,2,40,1280]{3,2,0,1:T(8,128)(2,1)S(1)}, bf16[2,2,40,1280]{3,2,0,1:T(8,128)(2,1)S(1)}, u32[]{:S(2)}, u32[]{:S(2)}) collective-permute-start(bf16[2,2,40,1280]{3,2,0,1:T(8,128)(2,1)S(1)} %get-tuple-element.67), channel_id=1, source_target_pairs={{0,16},{8,24},{16,0},{24,8},{1,17},{9,25},{17,1},{25,9},{2,18},{10... | collective-permute-start | bytes 1228808 | tf_op jit(solution)/shard_map/tok1_x2/ppermute | solution.py:54
  32.6 6.1 %collective-permute-done.6 = bf16[136,1280]{1,0:T(8,128)(2,1)S(1)} collective-permute-done((bf16[136,1280]{1,0:T(8,128)(2,1)S(1)}, bf16[136,1280]{1,0:T(8,128)(2,1)S(1)}, u32[]{:S(2)}, u32[]{:S(2)}) %collective-permute-start.6) | collective-permute-done | bytes 348192 | tf_op jit(solution)/shard_map/tok_y2/ppermute | solution.py:48
  38.7 1.8 %collective-permute-done.8 = bf16[136,1280]{1,0:T(8,128)(2,1)S(1)} collective-permute-done((bf16[136,1280]{1,0:T(8,128)(2,1)S(1)}, bf16[136,1280]{1,0:T(8,128)(2,1)S(1)}, u32[]{:S(2)}, u32[]{:S(2)}) %collective-permute-start.8) | collective-permute-done | bytes 348192 | tf_op jit(solution)/shard_map/tok_z3/ppermute | solution.py:40
  42.7 3.9 %collective-permute-done.30 = bf16[4,40,1280]{2,1,0:T(8,128)(2,1)S(1)} collective-permute-done((bf16[4,40,1280]{2,1,0:T(8,128)(2,1)S(1)}, bf16[4,40,1280]{2,1,0:T(8,128)(2,1)S(1)}, u32[]{:S(2)}, u32[]{:S(2)}) %collective-permute-start.30) | collective-permute-done | bytes 409632 | tf_op jit(solution)/shard_map/grad_y0/ppermute | solution.py:48
  47.2 1.4 %collective-permute-done.31 = bf16[4,40,1280]{2,1,0:T(8,128)(2,1)S(1)} collective-permute-done((bf16[4,40,1280]{2,1,0:T(8,128)(2,1)S(1)}, bf16[4,40,1280]{2,1,0:T(8,128)(2,1)S(1)}, u32[]{:S(2)}, u32[]{:S(2)}) %collective-permute-start.31) | collective-permute-done | bytes 409632 | tf_op jit(solution)/shard_map/grad_z1/ppermute | solution.py:40
  54.4 1.6 %collective-permute-start.19 = (bf16[2,2,40,1280]{3,2,1,0:T(8,128)(2,1)S(1)}, bf16[2,2,40,1280]{3,2,1,0:T(8,128)(2,1)S(1)}, u32[]{:S(2)}, u32[]{:S(2)}) collective-permute-start(bf16[2,2,40,1280]{3,2,1,0:T(8,128)(2,1)S(1)} %pad_maximum_fusion.1), channel_id=1, source_target_pairs={{0,16},{8,24},{16,0},{24,8},{1,17},{9,25},{17,1},{25,9},{2,18},{10... | collective-permute-start | bytes 1228808 | tf_op jit(solution)/shard_map/tok3_x2/ppermute | solution.py:54
  57.1 2.5 %collective-permute-done.33 = bf16[4,40,1280]{2,1,0:T(8,128)(2,1)S(1)} collective-permute-done((bf16[4,40,1280]{2,1,0:T(8,128)(2,1)S(1)}, bf16[4,40,1280]{2,1,0:T(8,128)(2,1)S(1)}, u32[]{:S(2)}, u32[]{:S(2)}) %collective-permute-start.33) | collective-permute-done | bytes 409632 | tf_op jit(solution)/shard_map/grad_z2/ppermute | solution.py:40
  75.4 5.4 %collective-permute-done.17 = bf16[4,40,1280]{2,1,0:T(8,128)(2,1)S(1)} collective-permute-done((bf16[4,40,1280]{2,1,0:T(8,128)(2,1)S(1)}, bf16[4,40,1280]{2,1,0:T(8,128)(2,1)S(1)}, u32[]{:S(2)}, u32[]{:S(2)}) %collective-permute-start.17) | collective-permute-done | bytes 409632 | tf_op jit(solution)/shard_map/out_y1/ppermute | solution.py:48
  81.0 8.5 %collective-permute-done.12 = bf16[4,40,1280]{2,1,0:T(8,128)(2,1)S(1)} collective-permute-done((bf16[4,40,1280]{2,1,0:T(8,128)(2,1)S(1)}, bf16[4,40,1280]{2,1,0:T(8,128)(2,1)S(1)}, u32[]{:S(2)}, u32[]{:S(2)}) %collective-permute-start.12) | collective-permute-done | bytes 409632 | tf_op jit(solution)/shard_map/out_y2/ppermute | solution.py:48
  91.7 6.1 %collective-permute-done.21 = bf16[4,40,1280]{2,1,0:T(8,128)(2,1)S(1)} collective-permute-done((bf16[4,40,1280]{2,1,0:T(8,128)(2,1)S(1)}, bf16[4,40,1280]{2,1,0:T(8,128)(2,1)S(1)}, u32[]{:S(2)}, u32[]{:S(2)}) %collective-permute-start.21) | collective-permute-done | bytes 409632 | tf_op jit(solution)/shard_map/out_y3/ppermute | solution.py:48
  99.5 4.7 %convolution_convert_fusion = bf16[4,512,1280]{2,1,0:T(8,128)(2,1)} fusion(bf16[4,320,1280]{2,1,0:T(8,128)(2,1)S(1)} %constant_dynamic-update-slice_fusion.8, bf16[4,80,512]{2,1,0:T(8,128)(2,1)S(1)} %get-tuple-element.45, bf16[4,80,512]{2,1,0:T(8,128)(2,1)S(1)} %get-tuple-element.40, bf16[4,80,512]{2,1,0:T(8,128)(2,1)S(1)} %get-tuple-element.44, ...), kind=kOutput, calls=%fused_computation | convolution fusion | flops 1685585920 | bytes 9830400 | tf_op jit(solution)/shard_map/erf,erd->efd/dot_general | solution.py:222
  104.7 3.9 %collective-permute-start.24 = (bf16[2,40,1280]{2,1,0:T(8,128)(2,1)S(1)}, bf16[2,40,1280]{2,1,0:T(8,128)(2,1)S(1)}, u32[]{:S(2)}, u32[]{:S(2)}) collective-permute-start(bf16[2,40,1280]{2,1,0:T(8,128)(2,1)S(1)} %bitcast.229), channel_id=1, source_target_pairs={{0,22},{1,23},{2,16},{3,17},{4,18},{5,19},{6,20},{7,21},{8,30},{9,... | collective-permute-start | bytes 614408 | tf_op jit(solution)/shard_map/out_z1_x2/ppermute | solution.py:66
  109.7 1.9 %fusion = bf16[4,320,512]{2,1,0:T(8,128)(2,1)S(1)} fusion(f32[4,80,512]{2,1,0:T(8,128)S(1)} %get-tuple-element.58, f32[4,80,512]{2,1,0:T(8,128)S(1)} %get-tuple-element.57, f32[4,80,512]{2,1,0:T(8,128)S(1)} %get-tuple-element.56, f32[4,80,512]{2,1,0:T(8,128)S(1)} %get-tuple-element.55, bf16[4,320,1280]{2,1,0:T(8,128)(2,1)S(1)} %constant_dynamic-update-slice_fusion.8, ...), kind=kOutput, calls=%fused_computation.3 | convolution fusion | flops 1680998400 | bytes 12451840 | tf_op jit(solution)/shard_map/erd,efd->erf/dot_general | solution.py:218
  111.6 1.6 %collective-permute-start.18 = (bf16[2,40,1280]{2,1,0:T(8,128)(2,1)S(1)}, bf16[2,40,1280]{2,1,0:T(8,128)(2,1)S(1)}, u32[]{:S(2)}, u32[]{:S(2)}) collective-permute-start(bf16[2,40,1280]{2,1,0:T(8,128)(2,1)S(1)} %bitcast.228), channel_id=1, source_target_pairs={{0,6},{1,7},{2,0},{3,1},{4,2},{5,3},{6,4},{7,5},{8,14},{9,15},{10,... | collective-permute-start | bytes 614408 | tf_op jit(solution)/shard_map/out_z1_x0/ppermute | solution.py:66
  113.2 1.6 %collective-permute-done.24 = bf16[2,40,1280]{2,1,0:T(8,128)(2,1)S(1)} collective-permute-done((bf16[2,40,1280]{2,1,0:T(8,128)(2,1)S(1)}, bf16[2,40,1280]{2,1,0:T(8,128)(2,1)S(1)}, u32[]{:S(2)}, u32[]{:S(2)}) %collective-permute-start.24) | collective-permute-done | bytes 204832 | tf_op jit(solution)/shard_map/out_z1_x2/ppermute | solution.py:66
  116.0 1.4 %collective-permute-done.18 = bf16[2,40,1280]{2,1,0:T(8,128)(2,1)S(1)} collective-permute-done((bf16[2,40,1280]{2,1,0:T(8,128)(2,1)S(1)}, bf16[2,40,1280]{2,1,0:T(8,128)(2,1)S(1)}, u32[]{:S(2)}, u32[]{:S(2)}) %collective-permute-start.18) | collective-permute-done | bytes 204832 | tf_op jit(solution)/shard_map/out_z1_x0/ppermute | solution.py:66
  117.6 4.7 %convolution_convert_fusion.1 = bf16[4,1280,512]{2,1,0:T(8,128)(2,1)} fusion(bf16[4,320,1280]{2,1,0:T(8,128)(2,1)S(1)} %constant_dynamic-update-slice_fusion, bf16[4,320,512]{2,1,0:T(8,128)(2,1)S(1)} %fusion), kind=kOutput, calls=%fused_computation.1 | convolution fusion | flops 1680343040 | bytes 9830400 | tf_op jit(solution)/shard_map/erd,erf->edf/dot_general | solution.py:225
  (200 shorter events, 42.4 us)
Async XLA Ops:
  3.2 13.3 %collective-permute-start.2 = (bf16[136,1280]{1,0:T(8,128)(2,1)S(1)}, bf16[136,1280]{1,0:T(8,128)(2,1)S(1)}, u32[]{:S(2)}, u32[]{:S(2)}) collective-permute-start(bf16[136,1280]{1,0:T(8,128)(2,1)S(1)} %fusion.130), channel_id=1, source_target_pairs={{0,2},{1,3},{2,4},{3,5},{4,6},{5,7},{6,0},{7,1},{8,10},{9,11},{10,... | collective-permute-start | bytes 1044488 | tf_op jit(solution)/shard_map/tok_z1/ppermute | solution.py:40
  8.2 10.8 %collective-permute-start.27 = (bf16[4,10,1280]{2,1,0:T(8,128)(2,1)S(1)}, bf16[4,10,1280]{2,1,0:T(8,128)(2,1)S(1)}, u32[]{:S(2)}, u32[]{:S(2)}) collective-permute-start(bf16[4,10,1280]{2,1,0:T(8,128)(2,1)S(1)} %squeeze.195), channel_id=1, source_target_pairs={{0,8},{8,0},{16,24},{24,16},{1,9},{9,1},{17,25},{25,17},{2,10},{10... | collective-permute-start | bytes 307208 | tf_op jit(solution)/shard_map/grad_x1/ppermute | solution.py:54
  8.3 10.7 %collective-permute-start.28 = (bf16[4,10,1280]{2,1,0:T(8,128)(2,1)S(1)}, bf16[4,10,1280]{2,1,0:T(8,128)(2,1)S(1)}, u32[]{:S(2)}, u32[]{:S(2)}) collective-permute-start(bf16[4,10,1280]{2,1,0:T(8,128)(2,1)S(1)} %squeeze.196), channel_id=1, source_target_pairs={{0,16},{8,24},{16,0},{24,8},{1,17},{9,25},{17,1},{25,9},{2,18},{10... | collective-permute-start | bytes 307208 | tf_op jit(solution)/shard_map/grad_x2/ppermute | solution.py:54
  16.5 11.1 %collective-permute-start.4 = (bf16[136,1280]{1,0:T(8,128)(2,1)S(1)}, bf16[136,1280]{1,0:T(8,128)(2,1)S(1)}, u32[]{:S(2)}, u32[]{:S(2)}) collective-permute-start(bf16[136,1280]{1,0:T(8,128)(2,1)S(1)} %collective-permute-done.2), channel_id=1, source_target_pairs={{0,2},{1,3},{2,4},{3,5},{4,6},{5,7},{6,0},{7,1},{8,10},{9,11},{10,... | collective-permute-start | bytes 1044488 | tf_op jit(solution)/shard_map/tok_z2/ppermute | solution.py:40
  19.8 11.1 %collective-permute-start.1 = (bf16[2,2,40,1280]{3,2,0,1:T(8,128)(2,1)S(1)}, bf16[2,2,40,1280]{3,2,0,1:T(8,128)(2,1)S(1)}, u32[]{:S(2)}, u32[]{:S(2)}) collective-permute-start(bf16[2,2,40,1280]{3,2,0,1:T(8,128)(2,1)S(1)} %get-tuple-element.63), channel_id=1, source_target_pairs={{0,16},{8,24},{16,0},{24,8},{1,17},{9,25},{17,1},{25,9},{2,18},{10... | collective-permute-start | bytes 1228808 | tf_op jit(solution)/shard_map/tok0_x2/ppermute | solution.py:54
  27.6 12.9 %collective-permute-start.8 = (bf16[136,1280]{1,0:T(8,128)(2,1)S(1)}, bf16[136,1280]{1,0:T(8,128)(2,1)S(1)}, u32[]{:S(2)}, u32[]{:S(2)}) collective-permute-start(bf16[136,1280]{1,0:T(8,128)(2,1)S(1)} %collective-permute-done.4), channel_id=1, source_target_pairs={{0,2},{1,3},{2,4},{3,5},{4,6},{5,7},{6,0},{7,1},{8,10},{9,11},{10,... | collective-permute-start | bytes 1044488 | tf_op jit(solution)/shard_map/tok_z3/ppermute | solution.py:40
  27.6 11.1 %collective-permute-start.6 = (bf16[136,1280]{1,0:T(8,128)(2,1)S(1)}, bf16[136,1280]{1,0:T(8,128)(2,1)S(1)}, u32[]{:S(2)}, u32[]{:S(2)}) collective-permute-start(bf16[136,1280]{1,0:T(8,128)(2,1)S(1)} %collective-permute-done.4), channel_id=1, source_target_pairs={{0,1},{1,0},{2,3},{3,2},{4,5},{5,4},{6,7},{7,6},{8,9},{9,8},{10,11... | collective-permute-start | bytes 1044488 | tf_op jit(solution)/shard_map/tok_y2/ppermute | solution.py:48
  29.0 17.5 %collective-permute-start.30 = (bf16[4,40,1280]{2,1,0:T(8,128)(2,1)S(1)}, bf16[4,40,1280]{2,1,0:T(8,128)(2,1)S(1)}, u32[]{:S(2)}, u32[]{:S(2)}) collective-permute-start(bf16[4,40,1280]{2,1,0:T(8,128)(2,1)S(1)} %copy.59), channel_id=1, source_target_pairs={{0,1},{1,0},{2,3},{3,2},{4,5},{5,4},{6,7},{7,6},{8,9},{9,8},{10,11... | collective-permute-start | bytes 1228808 | tf_op jit(solution)/shard_map/grad_y0/ppermute | solution.py:48
  29.7 18.8 %collective-permute-start.31 = (bf16[4,40,1280]{2,1,0:T(8,128)(2,1)S(1)}, bf16[4,40,1280]{2,1,0:T(8,128)(2,1)S(1)}, u32[]{:S(2)}, u32[]{:S(2)}) collective-permute-start(bf16[4,40,1280]{2,1,0:T(8,128)(2,1)S(1)} %copy.59), channel_id=1, source_target_pairs={{0,2},{1,3},{2,4},{3,5},{4,6},{5,7},{6,0},{7,1},{8,10},{9,11},{10,... | collective-permute-start | bytes 1228808 | tf_op jit(solution)/shard_map/grad_z1/ppermute | solution.py:40
  38.7 11.0 %collective-permute-start.5 = (bf16[2,2,40,1280]{3,2,1,0:T(8,128)(2,1)S(1)}, bf16[2,2,40,1280]{3,2,1,0:T(8,128)(2,1)S(1)}, u32[]{:S(2)}, u32[]{:S(2)}) collective-permute-start(bf16[2,2,40,1280]{3,2,1,0:T(8,128)(2,1)S(1)} %pad_maximum_fusion.5), channel_id=1, source_target_pairs={{0,8},{8,0},{16,24},{24,16},{1,9},{9,1},{17,25},{25,17},{2,10},{10... | collective-permute-start | bytes 1228808 | tf_op jit(solution)/shard_map/tok0_x1/ppermute | solution.py:54
  40.5 13.5 %collective-permute-start.10 = (bf16[72,1280]{1,0:T(8,128)(2,1)S(1)}, bf16[72,1280]{1,0:T(8,128)(2,1)S(1)}, u32[]{:S(2)}, u32[]{:S(2)}) collective-permute-start(bf16[72,1280]{1,0:T(8,128)(2,1)S(1)} %slice.505), channel_id=1, source_target_pairs={{0,2},{1,3},{2,4},{3,5},{4,6},{5,7},{6,0},{7,1},{8,10},{9,11},{10,... | collective-permute-start | bytes 552968 | tf_op jit(solution)/shard_map/tok_z4/ppermute | solution.py:40
  41.2 12.8 %collective-permute-start.9 = (bf16[64,1280]{1,0:T(8,128)(2,1)S(1)}, bf16[64,1280]{1,0:T(8,128)(2,1)S(1)}, u32[]{:S(2)}, u32[]{:S(2)}) collective-permute-start(bf16[64,1280]{1,0:T(8,128)(2,1)S(1)} %slice.423), channel_id=1, source_target_pairs={{0,1},{1,0},{2,3},{3,2},{4,5},{5,4},{6,7},{7,6},{8,9},{9,8},{10,11... | collective-permute-start | bytes 491528 | tf_op jit(solution)/shard_map/tok_y3/ppermute | solution.py:48
  54.4 11.9 %collective-permute-start.19 = (bf16[2,2,40,1280]{3,2,1,0:T(8,128)(2,1)S(1)}, bf16[2,2,40,1280]{3,2,1,0:T(8,128)(2,1)S(1)}, u32[]{:S(2)}, u32[]{:S(2)}) collective-permute-start(bf16[2,2,40,1280]{3,2,1,0:T(8,128)(2,1)S(1)} %pad_maximum_fusion.1), channel_id=1, source_target_pairs={{0,16},{8,24},{16,0},{24,8},{1,17},{9,25},{17,1},{25,9},{2,18},{10... | collective-permute-start | bytes 1228808 | tf_op jit(solution)/shard_map/tok3_x2/ppermute | solution.py:54
  56.1 10.4 %collective-permute-start.11 = (bf16[2,2,40,1280]{3,2,1,0:T(8,128)(2,1)S(1)}, bf16[2,2,40,1280]{3,2,1,0:T(8,128)(2,1)S(1)}, u32[]{:S(2)}, u32[]{:S(2)}) collective-permute-start(bf16[2,2,40,1280]{3,2,1,0:T(8,128)(2,1)S(1)} %pad_maximum_fusion.6), channel_id=1, source_target_pairs={{0,8},{8,0},{16,24},{24,16},{1,9},{9,1},{17,25},{25,17},{2,10},{10... | collective-permute-start | bytes 1228808 | tf_op jit(solution)/shard_map/tok2_x1/ppermute | solution.py:54
  59.5 12.4 %collective-permute-start.34 = (bf16[4,40,1280]{2,1,0:T(8,128)(2,1)S(1)}, bf16[4,40,1280]{2,1,0:T(8,128)(2,1)S(1)}, u32[]{:S(2)}, u32[]{:S(2)}) collective-permute-start(bf16[4,40,1280]{2,1,0:T(8,128)(2,1)S(1)} %collective-permute-done.33), channel_id=1, source_target_pairs={{0,1},{1,0},{2,3},{3,2},{4,5},{5,4},{6,7},{7,6},{8,9},{9,8},{10,11... | collective-permute-start | bytes 1228808 | tf_op jit(solution)/shard_map/grad_y2/ppermute | solution.py:48
  60.5 11.4 %collective-permute-start.35 = (bf16[4,40,1280]{2,1,0:T(8,128)(2,1)S(1)}, bf16[4,40,1280]{2,1,0:T(8,128)(2,1)S(1)}, u32[]{:S(2)}, u32[]{:S(2)}) collective-permute-start(bf16[4,40,1280]{2,1,0:T(8,128)(2,1)S(1)} %collective-permute-done.33), channel_id=1, source_target_pairs={{0,2},{1,3},{2,4},{3,5},{4,6},{5,7},{6,0},{7,1},{8,10},{9,11},{10,... | collective-permute-start | bytes 1228808 | tf_op jit(solution)/shard_map/grad_z3/ppermute | solution.py:40
  63.9 16.9 %collective-permute-start.17 = (bf16[4,40,1280]{2,1,0:T(8,128)(2,1)S(1)}, bf16[4,40,1280]{2,1,0:T(8,128)(2,1)S(1)}, u32[]{:S(2)}, u32[]{:S(2)}) collective-permute-start(bf16[4,40,1280]{2,1,0:T(8,128)(2,1)S(1)} %fusion.63), channel_id=1, source_target_pairs={{0,1},{1,0},{2,3},{3,2},{4,5},{5,4},{6,7},{7,6},{8,9},{9,8},{10,11... | collective-permute-start | bytes 1228808 | tf_op jit(solution)/shard_map/out_y1/ppermute | solution.py:48
  69.8 19.7 %collective-permute-start.12 = (bf16[4,40,1280]{2,1,0:T(8,128)(2,1)S(1)}, bf16[4,40,1280]{2,1,0:T(8,128)(2,1)S(1)}, u32[]{:S(2)}, u32[]{:S(2)}) collective-permute-start(bf16[4,40,1280]{2,1,0:T(8,128)(2,1)S(1)} %fusion.62), channel_id=1, source_target_pairs={{0,1},{1,0},{2,3},{3,2},{4,5},{5,4},{6,7},{7,6},{8,9},{9,8},{10,11... | collective-permute-start | bytes 1228808 | tf_op jit(solution)/shard_map/out_y2/ppermute | solution.py:48
  71.9 27.5 %collective-permute-start.36 = (bf16[4,40,1280]{2,1,0:T(8,128)(2,1)S(1)}, bf16[4,40,1280]{2,1,0:T(8,128)(2,1)S(1)}, u32[]{:S(2)}, u32[]{:S(2)}) collective-permute-start(bf16[4,40,1280]{2,1,0:T(8,128)(2,1)S(1)} %collective-permute-done.34), channel_id=1, source_target_pairs={{0,2},{1,3},{2,4},{3,5},{4,6},{5,7},{6,0},{7,1},{8,10},{9,11},{10,... | collective-permute-start | bytes 1228808 | tf_op jit(solution)/shard_map/grad_z4/ppermute | solution.py:40
  80.7 17.1 %collective-permute-start.21 = (bf16[4,40,1280]{2,1,0:T(8,128)(2,1)S(1)}, bf16[4,40,1280]{2,1,0:T(8,128)(2,1)S(1)}, u32[]{:S(2)}, u32[]{:S(2)}) collective-permute-start(bf16[4,40,1280]{2,1,0:T(8,128)(2,1)S(1)} %fusion.64), channel_id=1, source_target_pairs={{0,1},{1,0},{2,3},{3,2},{4,5},{5,4},{6,7},{7,6},{8,9},{9,8},{10,11... | collective-permute-start | bytes 1228808 | tf_op jit(solution)/shard_map/out_y3/ppermute | solution.py:48
  89.6 14.6 %collective-permute-start.14 = (bf16[4,40,1280]{2,1,0:T(8,128)(2,1)S(1)}, bf16[4,40,1280]{2,1,0:T(8,128)(2,1)S(1)}, u32[]{:S(2)}, u32[]{:S(2)}) collective-permute-start(bf16[4,40,1280]{2,1,0:T(8,128)(2,1)S(1)} %fusion.16), channel_id=1, source_target_pairs={{0,6},{1,7},{2,0},{3,1},{4,2},{5,3},{6,4},{7,5},{8,14},{9,15},{10,... | collective-permute-start | bytes 1228808 | tf_op jit(solution)/shard_map/out_z2/ppermute | solution.py:40
  90.6 17.9 %collective-permute-start.13 = (bf16[4,40,1280]{2,1,0:T(8,128)(2,1)S(1)}, bf16[4,40,1280]{2,1,0:T(8,128)(2,1)S(1)}, u32[]{:S(2)}, u32[]{:S(2)}) collective-permute-start(bf16[4,40,1280]{2,1,0:T(8,128)(2,1)S(1)} %fusion.61), channel_id=1, source_target_pairs={{0,1},{1,0},{2,3},{3,2},{4,5},{5,4},{6,7},{7,6},{8,9},{9,8},{10,11... | collective-permute-start | bytes 1228808 | tf_op jit(solution)/shard_map/out_y0/ppermute | solution.py:48
  98.3 14.9 %collective-permute-start.25 = (bf16[2,40,1280]{2,1,0:T(8,128)(2,1)S(1)}, bf16[2,40,1280]{2,1,0:T(8,128)(2,1)S(1)}, u32[]{:S(2)}, u32[]{:S(2)}) collective-permute-start(bf16[2,40,1280]{2,1,0:T(8,128)(2,1)S(1)} %bitcast.227), channel_id=1, source_target_pairs={{0,18},{1,19},{2,20},{3,21},{4,22},{5,23},{6,16},{7,17},{8,26},{9,... | collective-permute-start | bytes 614408 | tf_op jit(solution)/shard_map/out_z3_x2/ppermute | solution.py:66
  98.4 17.6 %collective-permute-start.22 = (bf16[2,40,1280]{2,1,0:T(8,128)(2,1)S(1)}, bf16[2,40,1280]{2,1,0:T(8,128)(2,1)S(1)}, u32[]{:S(2)}, u32[]{:S(2)}) collective-permute-start(bf16[2,40,1280]{2,1,0:T(8,128)(2,1)S(1)} %bitcast.226), channel_id=1, source_target_pairs={{0,2},{1,3},{2,4},{3,5},{4,6},{5,7},{6,0},{7,1},{8,10},{9,11},{10,... | collective-permute-start | bytes 614408 | tf_op jit(solution)/shard_map/out_z3_x0/ppermute | solution.py:66
  (20 other events, 148.5 us)

commit v6 on v5

--- a/solution.py
+++ b/solution.py
@@ -208,24 +208,6 @@
         blocks_grad[-1].append(ring_z(blocks_grad[-2][1], 1, f"grad_z{rows}"))
     else:
         gather_step(blocks_grad, rows - 1, "grad")
-    if rows - 1 in over_y:
-        blocks_grad[-1][-1] = after(blocks_grad[-1][-1], over_y[rows - 1])
-    rows_grad = jnp.concatenate([b for line in blocks_grad for b in line], axis=1)
-
-    rows_tok = jnp.concatenate(rows_tok, axis=1)
-    active = jnp.concatenate(active, axis=1)
-    slope = jnp.concatenate(slope, axis=1)
-    back_grad = jnp.einsum(
-        "erd,efd->erf", rows_grad, down_weight, preferred_element_type=jnp.float32
-    )
-    pre_grad = lax.optimization_barrier((back_grad * slope).astype(jnp.bfloat16))
-    down_part = jnp.einsum(
-        "erf,erd->efd", active, rows_grad, preferred_element_type=jnp.float32
-    ).astype(jnp.bfloat16)
-    up_part = jnp.einsum(
-        "erd,erf->edf", rows_tok, pre_grad, preferred_element_type=jnp.float32
-    ).astype(jnp.bfloat16)
-
     def by_owner(total):
         total = pick("cr,rd->cd", reorder, total.astype(jnp.bfloat16).reshape(slots, width))
         return list(total.reshape(owners // 2, 2, local_experts * capacity, width))
@@ -234,6 +216,7 @@
     arrived = [
         [total[0]] + [swap_expert(total[q], 2 * q, "own") for q in range(1, owners // 2)]
     ]
+    over_z = None
     for ks, step in ((range(rows // 2, 0, -1), -1), (range(rows // 2 + 1, rows), 1)):
         total = None
         for k in ks:
@@ -244,9 +227,28 @@
                     [ring_z_to(t, step, 2 * q, f"out_z{k}") for q, t in enumerate(total)]
                 )
             else:
-                total = ring_z(total.astype(jnp.bfloat16), step, f"out_z{k}").astype(jnp.float32)
+                over_z = ring_z(total.astype(jnp.bfloat16), step, f"out_z{k}")
+                total = over_z.astype(jnp.float32)
+    if over_z is not None:
+        blocks_grad[-1][-1] = after(blocks_grad[-1][-1], over_z)
+    rows_grad = jnp.concatenate([b for line in blocks_grad for b in line], axis=1)
+
+    rows_tok = jnp.concatenate(rows_tok, axis=1)
+    active = jnp.concatenate(active, axis=1)
+    slope = jnp.concatenate(slope, axis=1)
+    back_grad = jnp.einsum(
+        "erd,efd->erf", rows_grad, down_weight, preferred_element_type=jnp.float32
+    )
+    pre_grad = lax.optimization_barrier((back_grad * slope).astype(jnp.bfloat16))
+    down_part = jnp.einsum(
+        "erf,erd->efd", active, rows_grad, preferred_element_type=jnp.float32
+    ).astype(jnp.bfloat16)
+    up_part = jnp.einsum(
+        "erd,erf->edf", rows_tok, pre_grad, preferred_element_type=jnp.float32
+    ).astype(jnp.bfloat16)
+
     total = [sum(t.astype(jnp.float32) for t in ts).astype(jnp.bfloat16) for ts in zip(*arrived)]
-    back = swap_expert(jnp.stack([t[1] for t in total]), 1, "back")
+    back = swap_expert(after(jnp.stack([t[1] for t in total]), up_part, down_part), 1, "back")
     returned = jnp.concatenate([v for t, other in zip(total, back) for v in (t[0], other)], axis=0)
     combined = pick("rt,rd->td", place, returned)
     return (combined, up_part, down_part)

time: 124 us -> 123 us (level)
  waiting for transfers between devices: 54.3 us -> 52.8 us
    ppermute x4, waiting for transfers between devices: 2.96 us -> 0.01 us  [ring_z_to(): return lax.ppermute(value, ('expert', 'dp'), perm)]
    ppermute x13, starting transfers between devices: 8.41 us -> 10 us  [swap_expert(): return lax.ppermute(value, 'expert', [(i, i ^ mask) for i in range(n)])]
  transfers between devices with their start and end apart: 37 -> 37, of which waited for: 16 -> 15; matrix products, arithmetic and copies ran while one was open for 24% -> 25% of each run, Pallas kernels for 0% -> 0%
where the time goes in v6:
time: 123 us; the launch traced here: 122 us
  waiting for transfers between devices  52.8 us (43%)
  starting transfers between devices  33.2 us (27%)
  matrix products  26.7 us (22%)
  other arithmetic  5.44 us (4%)
  local copies, waits for them, and re-layouts  2.52 us (2%)
  between operations  1.69 us (1%)
    ppermute x11, waiting for transfers between devices, ring_y(): return lax.ppermute(value, 'dp', perm)  31.6 us
    ppermute x9, waiting for transfers between devices, ring_z(): return lax.ppermute(value, 'dp', perm)  18.5 us
    ppermute x11, starting transfers between devices, ring_y(): return lax.ppermute(value, 'dp', perm)  11.9 us
    ppermute x13, starting transfers between devices, swap_expert(): return lax.ppermute(value, 'expert', [(i, i ^ mask) for i in range(n)])  10 us
    dot_general x20, matrix products, pick(): found = jnp.einsum(spec, onehot, values, preferred_element_type=jnp.float32)  7.07 us
    ppermute x9, starting transfers between devices, ring_z(): return lax.ppermute(value, 'dp', perm)  5.77 us
    ppermute x4, starting transfers between devices, ring_z_to(): return lax.ppermute(value, ('expert', 'dp'), perm)  5.48 us
    dot_general x1, matrix products, on_device(): jnp.einsum('erf,erd->efd', active, rows_grad, preferred_element_type=jnp....  4.69 us
  transfers between devices with their start and end apart: 37, of which 15 were waited for; matrix products, arithmetic and copies ran while one was open for 25% of the time, Pallas kernels for 0%

profile of v6, /device:TPU:0, one launch (start us, length us, event | category | flops | bytes accessed | tf_op | source)
XLA Modules:
  0.0 122.3 jit_solution(13524153589890582291)
XLA Ops:
  3.2 3.1 %collective-permute-start.2 = (bf16[136,1280]{1,0:T(8,128)(2,1)S(1)}, bf16[136,1280]{1,0:T(8,128)(2,1)S(1)}, u32[]{:S(2)}, u32[]{:S(2)}) collective-permute-start(bf16[136,1280]{1,0:T(8,128)(2,1)S(1)} %fusion.130), channel_id=1, source_target_pairs={{0,2},{1,3},{2,4},{3,5},{4,6},{5,7},{6,0},{7,1},{8,10},{9,11},{10,... | collective-permute-start | bytes 1044488 | tf_op jit(solution)/shard_map/tok_z1/ppermute | solution.py:40
  6.3 1.5 %collective-permute-start = (bf16[136,1280]{1,0:T(8,128)(2,1)S(1)}, bf16[136,1280]{1,0:T(8,128)(2,1)S(1)}, u32[]{:S(2)}, u32[]{:S(2)}) collective-permute-start(bf16[136,1280]{1,0:T(8,128)(2,1)S(1)} %fusion.130), channel_id=1, source_target_pairs={{0,1},{1,0},{2,3},{3,2},{4,5},{5,4},{6,7},{7,6},{8,9},{9,8},{10,11... | collective-permute-start | bytes 1044488 | tf_op jit(solution)/shard_map/tok_y0/ppermute | solution.py:48
  8.3 1.6 %collective-permute-start.27 = (bf16[4,10,1280]{2,1,0:T(8,128)(2,1)S(1)}, bf16[4,10,1280]{2,1,0:T(8,128)(2,1)S(1)}, u32[]{:S(2)}, u32[]{:S(2)}) collective-permute-start(bf16[4,10,1280]{2,1,0:T(8,128)(2,1)S(1)} %squeeze.195), channel_id=1, source_target_pairs={{0,16},{8,24},{16,0},{24,8},{1,17},{9,25},{17,1},{25,9},{2,18},{10... | collective-permute-start | bytes 307208 | tf_op jit(solution)/shard_map/grad_x2/ppermute | solution.py:54
  10.7 5.8 %collective-permute-done.2 = bf16[136,1280]{1,0:T(8,128)(2,1)S(1)} collective-permute-done((bf16[136,1280]{1,0:T(8,128)(2,1)S(1)}, bf16[136,1280]{1,0:T(8,128)(2,1)S(1)}, u32[]{:S(2)}, u32[]{:S(2)}) %collective-permute-start.2) | collective-permute-done | bytes 348192 | tf_op jit(solution)/shard_map/tok_z1/ppermute | solution.py:40
  17.5 1.5 %collective-permute-start.3 = (bf16[136,1280]{1,0:T(8,128)(2,1)S(1)}, bf16[136,1280]{1,0:T(8,128)(2,1)S(1)}, u32[]{:S(2)}, u32[]{:S(2)}) collective-permute-start(bf16[136,1280]{1,0:T(8,128)(2,1)S(1)} %collective-permute-done.2), channel_id=1, source_target_pairs={{0,1},{1,0},{2,3},{3,2},{4,5},{5,4},{6,7},{7,6},{8,9},{9,8},{10,11... | collective-permute-start | bytes 1044488 | tf_op jit(solution)/shard_map/tok_y1/ppermute | solution.py:48
  19.4 1.6 %collective-permute-start.1 = (bf16[2,2,40,1280]{3,2,0,1:T(8,128)(2,1)S(1)}, bf16[2,2,40,1280]{3,2,0,1:T(8,128)(2,1)S(1)}, u32[]{:S(2)}, u32[]{:S(2)}) collective-permute-start(bf16[2,2,40,1280]{3,2,0,1:T(8,128)(2,1)S(1)} %get-tuple-element.65), channel_id=1, source_target_pairs={{0,16},{8,24},{16,0},{24,8},{1,17},{9,25},{17,1},{25,9},{2,18},{10... | collective-permute-start | bytes 1228808 | tf_op jit(solution)/shard_map/tok0_x2/ppermute | solution.py:54
  21.7 5.9 %collective-permute-done.4 = bf16[136,1280]{1,0:T(8,128)(2,1)S(1)} collective-permute-done((bf16[136,1280]{1,0:T(8,128)(2,1)S(1)}, bf16[136,1280]{1,0:T(8,128)(2,1)S(1)}, u32[]{:S(2)}, u32[]{:S(2)}) %collective-permute-start.4) | collective-permute-done | bytes 348192 | tf_op jit(solution)/shard_map/tok_z2/ppermute | solution.py:40
  27.6 1.4 %collective-permute-start.6 = (bf16[136,1280]{1,0:T(8,128)(2,1)S(1)}, bf16[136,1280]{1,0:T(8,128)(2,1)S(1)}, u32[]{:S(2)}, u32[]{:S(2)}) collective-permute-start(bf16[136,1280]{1,0:T(8,128)(2,1)S(1)} %collective-permute-done.4), channel_id=1, source_target_pairs={{0,1},{1,0},{2,3},{3,2},{4,5},{5,4},{6,7},{7,6},{8,9},{9,8},{10,11... | collective-permute-start | bytes 1044488 | tf_op jit(solution)/shard_map/tok_y2/ppermute | solution.py:48
  31.0 1.5 %collective-permute-start.15 = (bf16[2,2,40,1280]{3,2,0,1:T(8,128)(2,1)S(1)}, bf16[2,2,40,1280]{3,2,0,1:T(8,128)(2,1)S(1)}, u32[]{:S(2)}, u32[]{:S(2)}) collective-permute-start(bf16[2,2,40,1280]{3,2,0,1:T(8,128)(2,1)S(1)} %get-tuple-element.69), channel_id=1, source_target_pairs={{0,16},{8,24},{16,0},{24,8},{1,17},{9,25},{17,1},{25,9},{2,18},{10... | collective-permute-start | bytes 1228808 | tf_op jit(solution)/shard_map/tok1_x2/ppermute | solution.py:54
  32.6 6.1 %collective-permute-done.6 = bf16[136,1280]{1,0:T(8,128)(2,1)S(1)} collective-permute-done((bf16[136,1280]{1,0:T(8,128)(2,1)S(1)}, bf16[136,1280]{1,0:T(8,128)(2,1)S(1)}, u32[]{:S(2)}, u32[]{:S(2)}) %collective-permute-start.6) | collective-permute-done | bytes 348192 | tf_op jit(solution)/shard_map/tok_y2/ppermute | solution.py:48
  38.7 1.8 %collective-permute-done.8 = bf16[136,1280]{1,0:T(8,128)(2,1)S(1)} collective-permute-done((bf16[136,1280]{1,0:T(8,128)(2,1)S(1)}, bf16[136,1280]{1,0:T(8,128)(2,1)S(1)}, u32[]{:S(2)}, u32[]{:S(2)}) %collective-permute-start.8) | collective-permute-done | bytes 348192 | tf_op jit(solution)/shard_map/tok_z3/ppermute | solution.py:40
  42.7 3.9 %collective-permute-done.29 = bf16[4,40,1280]{2,1,0:T(8,128)(2,1)S(1)} collective-permute-done((bf16[4,40,1280]{2,1,0:T(8,128)(2,1)S(1)}, bf16[4,40,1280]{2,1,0:T(8,128)(2,1)S(1)}, u32[]{:S(2)}, u32[]{:S(2)}) %collective-permute-start.29) | collective-permute-done | bytes 409632 | tf_op jit(solution)/shard_map/grad_y0/ppermute | solution.py:48
  47.2 1.4 %collective-permute-done.30 = bf16[4,40,1280]{2,1,0:T(8,128)(2,1)S(1)} collective-permute-done((bf16[4,40,1280]{2,1,0:T(8,128)(2,1)S(1)}, bf16[4,40,1280]{2,1,0:T(8,128)(2,1)S(1)}, u32[]{:S(2)}, u32[]{:S(2)}) %collective-permute-start.30) | collective-permute-done | bytes 409632 | tf_op jit(solution)/shard_map/grad_z1/ppermute | solution.py:40
  54.4 1.6 %collective-permute-start.19 = (bf16[2,2,40,1280]{3,2,1,0:T(8,128)(2,1)S(1)}, bf16[2,2,40,1280]{3,2,1,0:T(8,128)(2,1)S(1)}, u32[]{:S(2)}, u32[]{:S(2)}) collective-permute-start(bf16[2,2,40,1280]{3,2,1,0:T(8,128)(2,1)S(1)} %pad_maximum_fusion.1), channel_id=1, source_target_pairs={{0,16},{8,24},{16,0},{24,8},{1,17},{9,25},{17,1},{25,9},{2,18},{10... | collective-permute-start | bytes 1228808 | tf_op jit(solution)/shard_map/tok3_x2/ppermute | solution.py:54
  57.1 2.5 %collective-permute-done.32 = bf16[4,40,1280]{2,1,0:T(8,128)(2,1)S(1)} collective-permute-done((bf16[4,40,1280]{2,1,0:T(8,128)(2,1)S(1)}, bf16[4,40,1280]{2,1,0:T(8,128)(2,1)S(1)}, u32[]{:S(2)}, u32[]{:S(2)}) %collective-permute-start.32) | collective-permute-done | bytes 409632 | tf_op jit(solution)/shard_map/grad_z2/ppermute | solution.py:40
  75.4 5.4 %collective-permute-done.17 = bf16[4,40,1280]{2,1,0:T(8,128)(2,1)S(1)} collective-permute-done((bf16[4,40,1280]{2,1,0:T(8,128)(2,1)S(1)}, bf16[4,40,1280]{2,1,0:T(8,128)(2,1)S(1)}, u32[]{:S(2)}, u32[]{:S(2)}) %collective-permute-start.17) | collective-permute-done | bytes 409632 | tf_op jit(solution)/shard_map/out_y1/ppermute | solution.py:48
  80.9 8.6 %collective-permute-done.12 = bf16[4,40,1280]{2,1,0:T(8,128)(2,1)S(1)} collective-permute-done((bf16[4,40,1280]{2,1,0:T(8,128)(2,1)S(1)}, bf16[4,40,1280]{2,1,0:T(8,128)(2,1)S(1)}, u32[]{:S(2)}, u32[]{:S(2)}) %collective-permute-start.12) | collective-permute-done | bytes 409632 | tf_op jit(solution)/shard_map/out_y2/ppermute | solution.py:48
  91.8 6.1 %collective-permute-done.21 = bf16[4,40,1280]{2,1,0:T(8,128)(2,1)S(1)} collective-permute-done((bf16[4,40,1280]{2,1,0:T(8,128)(2,1)S(1)}, bf16[4,40,1280]{2,1,0:T(8,128)(2,1)S(1)}, u32[]{:S(2)}, u32[]{:S(2)}) %collective-permute-start.21) | collective-permute-done | bytes 409632 | tf_op jit(solution)/shard_map/out_y3/ppermute | solution.py:48
  101.1 3.6 %collective-permute-start.24 = (bf16[2,40,1280]{2,1,0:T(8,128)(2,1)S(1)}, bf16[2,40,1280]{2,1,0:T(8,128)(2,1)S(1)}, u32[]{:S(2)}, u32[]{:S(2)}) collective-permute-start(bf16[2,40,1280]{2,1,0:T(8,128)(2,1)S(1)} %bitcast.229), channel_id=1, source_target_pairs={{0,22},{1,23},{2,16},{3,17},{4,18},{5,19},{6,20},{7,21},{8,30},{9,... | collective-permute-start | bytes 614408 | tf_op jit(solution)/shard_map/out_z1_x2/ppermute | solution.py:66
  105.1 2.3 %collective-permute-start.23 = (bf16[2,40,1280]{2,1,0:T(8,128)(2,1)S(1)}, bf16[2,40,1280]{2,1,0:T(8,128)(2,1)S(1)}, u32[]{:S(2)}, u32[]{:S(2)}) collective-permute-start(bf16[2,40,1280]{2,1,0:T(8,128)(2,1)S(1)} %bitcast.230), channel_id=1, source_target_pairs={{0,16},{8,24},{16,0},{24,8},{1,17},{9,25},{17,1},{25,9},{2,18},{10... | collective-permute-start | bytes 614408 | tf_op jit(solution)/shard_map/own_x2/ppermute | solution.py:54
  108.2 4.7 %convolution_convert_fusion = bf16[4,512,1280]{2,1,0:T(8,128)(2,1)} fusion(bf16[4,320,1280]{2,1,0:T(8,128)(2,1)S(1)} %constant_dynamic-update-slice_fusion.8, bf16[4,80,512]{2,1,0:T(8,128)(2,1)S(1)} %get-tuple-element.46, bf16[4,80,512]{2,1,0:T(8,128)(2,1)S(1)} %get-tuple-element.41, bf16[4,80,512]{2,1,0:T(8,128)(2,1)S(1)} %get-tuple-element.45, ...), kind=kOutput, calls=%fused_computation | convolution fusion | flops 1685585920 | bytes 9830400 | tf_op jit(solution)/shard_map/erf,erd->efd/dot_general | solution.py:243
  112.9 1.9 %fusion = bf16[4,320,512]{2,1,0:T(8,128)(2,1)S(1)} fusion(f32[4,80,512]{2,1,0:T(8,128)S(1)} %get-tuple-element.59, f32[4,80,512]{2,1,0:T(8,128)S(1)} %get-tuple-element.58, f32[4,80,512]{2,1,0:T(8,128)S(1)} %get-tuple-element.57, f32[4,80,512]{2,1,0:T(8,128)S(1)} %get-tuple-element.56, bf16[4,320,1280]{2,1,0:T(8,128)(2,1)S(1)} %constant_dynamic-update-slice_fusion.8, ...), kind=kOutput, calls=%fused_computation.3 | convolution fusion | flops 1680998400 | bytes 12451840 | tf_op jit(solution)/shard_map/erd,efd->erf/dot_general | solution.py:239
  114.8 4.7 %convolution_convert_fusion.1 = bf16[4,1280,512]{2,1,0:T(8,128)(2,1)} fusion(bf16[4,320,1280]{2,1,0:T(8,128)(2,1)S(1)} %constant_dynamic-update-slice_fusion, bf16[4,320,512]{2,1,0:T(8,128)(2,1)S(1)} %fusion), kind=kOutput, calls=%fused_computation.1 | convolution fusion | flops 1680343040 | bytes 9830400 | tf_op jit(solution)/shard_map/erd,erf->edf/dot_general | solution.py:246
  119.8 1.4 %collective-permute-done.36 = bf16[2,40,1280]{2,1,0:T(8,128)(2,1)S(1)} collective-permute-done((bf16[2,40,1280]{2,1,0:T(8,128)(2,1)S(1)}, bf16[2,40,1280]{2,1,0:T(8,128)(2,1)S(1)}, u32[]{:S(2)}, u32[]{:S(2)}) %collective-permute-start.36) | collective-permute-done | bytes 204832 | tf_op jit(solution)/shard_map/back_x1/ppermute | solution.py:54
  (200 shorter events, 41.1 us)
Async XLA Ops:
  3.2 13.3 %collective-permute-start.2 = (bf16[136,1280]{1,0:T(8,128)(2,1)S(1)}, bf16[136,1280]{1,0:T(8,128)(2,1)S(1)}, u32[]{:S(2)}, u32[]{:S(2)}) collective-permute-start(bf16[136,1280]{1,0:T(8,128)(2,1)S(1)} %fusion.130), channel_id=1, source_target_pairs={{0,2},{1,3},{2,4},{3,5},{4,6},{5,7},{6,0},{7,1},{8,10},{9,11},{10,... | collective-permute-start | bytes 1044488 | tf_op jit(solution)/shard_map/tok_z1/ppermute | solution.py:40
  8.2 11.2 %collective-permute-start.26 = (bf16[4,10,1280]{2,1,0:T(8,128)(2,1)S(1)}, bf16[4,10,1280]{2,1,0:T(8,128)(2,1)S(1)}, u32[]{:S(2)}, u32[]{:S(2)}) collective-permute-start(bf16[4,10,1280]{2,1,0:T(8,128)(2,1)S(1)} %squeeze.194), channel_id=1, source_target_pairs={{0,8},{8,0},{16,24},{24,16},{1,9},{9,1},{17,25},{25,17},{2,10},{10... | collective-permute-start | bytes 307208 | tf_op jit(solution)/shard_map/grad_x1/ppermute | solution.py:54
  8.3 12.6 %collective-permute-start.27 = (bf16[4,10,1280]{2,1,0:T(8,128)(2,1)S(1)}, bf16[4,10,1280]{2,1,0:T(8,128)(2,1)S(1)}, u32[]{:S(2)}, u32[]{:S(2)}) collective-permute-start(bf16[4,10,1280]{2,1,0:T(8,128)(2,1)S(1)} %squeeze.195), channel_id=1, source_target_pairs={{0,16},{8,24},{16,0},{24,8},{1,17},{9,25},{17,1},{25,9},{2,18},{10... | collective-permute-start | bytes 307208 | tf_op jit(solution)/shard_map/grad_x2/ppermute | solution.py:54
  16.5 11.1 %collective-permute-start.4 = (bf16[136,1280]{1,0:T(8,128)(2,1)S(1)}, bf16[136,1280]{1,0:T(8,128)(2,1)S(1)}, u32[]{:S(2)}, u32[]{:S(2)}) collective-permute-start(bf16[136,1280]{1,0:T(8,128)(2,1)S(1)} %collective-permute-done.2), channel_id=1, source_target_pairs={{0,2},{1,3},{2,4},{3,5},{4,6},{5,7},{6,0},{7,1},{8,10},{9,11},{10,... | collective-permute-start | bytes 1044488 | tf_op jit(solution)/shard_map/tok_z2/ppermute | solution.py:40
  19.4 11.6 %collective-permute-start.1 = (bf16[2,2,40,1280]{3,2,0,1:T(8,128)(2,1)S(1)}, bf16[2,2,40,1280]{3,2,0,1:T(8,128)(2,1)S(1)}, u32[]{:S(2)}, u32[]{:S(2)}) collective-permute-start(bf16[2,2,40,1280]{3,2,0,1:T(8,128)(2,1)S(1)} %get-tuple-element.65), channel_id=1, source_target_pairs={{0,16},{8,24},{16,0},{24,8},{1,17},{9,25},{17,1},{25,9},{2,18},{10... | collective-permute-start | bytes 1228808 | tf_op jit(solution)/shard_map/tok0_x2/ppermute | solution.py:54
  27.6 12.9 %collective-permute-start.8 = (bf16[136,1280]{1,0:T(8,128)(2,1)S(1)}, bf16[136,1280]{1,0:T(8,128)(2,1)S(1)}, u32[]{:S(2)}, u32[]{:S(2)}) collective-permute-start(bf16[136,1280]{1,0:T(8,128)(2,1)S(1)} %collective-permute-done.4), channel_id=1, source_target_pairs={{0,2},{1,3},{2,4},{3,5},{4,6},{5,7},{6,0},{7,1},{8,10},{9,11},{10,... | collective-permute-start | bytes 1044488 | tf_op jit(solution)/shard_map/tok_z3/ppermute | solution.py:40
  27.6 11.1 %collective-permute-start.6 = (bf16[136,1280]{1,0:T(8,128)(2,1)S(1)}, bf16[136,1280]{1,0:T(8,128)(2,1)S(1)}, u32[]{:S(2)}, u32[]{:S(2)}) collective-permute-start(bf16[136,1280]{1,0:T(8,128)(2,1)S(1)} %collective-permute-done.4), channel_id=1, source_target_pairs={{0,1},{1,0},{2,3},{3,2},{4,5},{5,4},{6,7},{7,6},{8,9},{9,8},{10,11... | collective-permute-start | bytes 1044488 | tf_op jit(solution)/shard_map/tok_y2/ppermute | solution.py:48
  29.0 17.5 %collective-permute-start.29 = (bf16[4,40,1280]{2,1,0:T(8,128)(2,1)S(1)}, bf16[4,40,1280]{2,1,0:T(8,128)(2,1)S(1)}, u32[]{:S(2)}, u32[]{:S(2)}) collective-permute-start(bf16[4,40,1280]{2,1,0:T(8,128)(2,1)S(1)} %copy.59), channel_id=1, source_target_pairs={{0,1},{1,0},{2,3},{3,2},{4,5},{5,4},{6,7},{7,6},{8,9},{9,8},{10,11... | collective-permute-start | bytes 1228808 | tf_op jit(solution)/shard_map/grad_y0/ppermute | solution.py:48
  29.7 18.8 %collective-permute-start.30 = (bf16[4,40,1280]{2,1,0:T(8,128)(2,1)S(1)}, bf16[4,40,1280]{2,1,0:T(8,128)(2,1)S(1)}, u32[]{:S(2)}, u32[]{:S(2)}) collective-permute-start(bf16[4,40,1280]{2,1,0:T(8,128)(2,1)S(1)} %copy.59), channel_id=1, source_target_pairs={{0,2},{1,3},{2,4},{3,5},{4,6},{5,7},{6,0},{7,1},{8,10},{9,11},{10,... | collective-permute-start | bytes 1228808 | tf_op jit(solution)/shard_map/grad_z1/ppermute | solution.py:40
  40.5 13.5 %collective-permute-start.10 = (bf16[72,1280]{1,0:T(8,128)(2,1)S(1)}, bf16[72,1280]{1,0:T(8,128)(2,1)S(1)}, u32[]{:S(2)}, u32[]{:S(2)}) collective-permute-start(bf16[72,1280]{1,0:T(8,128)(2,1)S(1)} %slice.505), channel_id=1, source_target_pairs={{0,2},{1,3},{2,4},{3,5},{4,6},{5,7},{6,0},{7,1},{8,10},{9,11},{10,... | collective-permute-start | bytes 552968 | tf_op jit(solution)/shard_map/tok_z4/ppermute | solution.py:40
  41.2 12.8 %collective-permute-start.9 = (bf16[64,1280]{1,0:T(8,128)(2,1)S(1)}, bf16[64,1280]{1,0:T(8,128)(2,1)S(1)}, u32[]{:S(2)}, u32[]{:S(2)}) collective-permute-start(bf16[64,1280]{1,0:T(8,128)(2,1)S(1)} %slice.423), channel_id=1, source_target_pairs={{0,1},{1,0},{2,3},{3,2},{4,5},{5,4},{6,7},{7,6},{8,9},{9,8},{10,11... | collective-permute-start | bytes 491528 | tf_op jit(solution)/shard_map/tok_y3/ppermute | solution.py:48
  54.4 11.9 %collective-permute-start.19 = (bf16[2,2,40,1280]{3,2,1,0:T(8,128)(2,1)S(1)}, bf16[2,2,40,1280]{3,2,1,0:T(8,128)(2,1)S(1)}, u32[]{:S(2)}, u32[]{:S(2)}) collective-permute-start(bf16[2,2,40,1280]{3,2,1,0:T(8,128)(2,1)S(1)} %pad_maximum_fusion.1), channel_id=1, source_target_pairs={{0,16},{8,24},{16,0},{24,8},{1,17},{9,25},{17,1},{25,9},{2,18},{10... | collective-permute-start | bytes 1228808 | tf_op jit(solution)/shard_map/tok3_x2/ppermute | solution.py:54
  59.5 12.4 %collective-permute-start.33 = (bf16[4,40,1280]{2,1,0:T(8,128)(2,1)S(1)}, bf16[4,40,1280]{2,1,0:T(8,128)(2,1)S(1)}, u32[]{:S(2)}, u32[]{:S(2)}) collective-permute-start(bf16[4,40,1280]{2,1,0:T(8,128)(2,1)S(1)} %collective-permute-done.32), channel_id=1, source_target_pairs={{0,1},{1,0},{2,3},{3,2},{4,5},{5,4},{6,7},{7,6},{8,9},{9,8},{10,11... | collective-permute-start | bytes 1228808 | tf_op jit(solution)/shard_map/grad_y2/ppermute | solution.py:48
  60.5 11.4 %collective-permute-start.34 = (bf16[4,40,1280]{2,1,0:T(8,128)(2,1)S(1)}, bf16[4,40,1280]{2,1,0:T(8,128)(2,1)S(1)}, u32[]{:S(2)}, u32[]{:S(2)}) collective-permute-start(bf16[4,40,1280]{2,1,0:T(8,128)(2,1)S(1)} %collective-permute-done.32), channel_id=1, source_target_pairs={{0,2},{1,3},{2,4},{3,5},{4,6},{5,7},{6,0},{7,1},{8,10},{9,11},{10,... | collective-permute-start | bytes 1228808 | tf_op jit(solution)/shard_map/grad_z3/ppermute | solution.py:40
  63.9 16.9 %collective-permute-start.17 = (bf16[4,40,1280]{2,1,0:T(8,128)(2,1)S(1)}, bf16[4,40,1280]{2,1,0:T(8,128)(2,1)S(1)}, u32[]{:S(2)}, u32[]{:S(2)}) collective-permute-start(bf16[4,40,1280]{2,1,0:T(8,128)(2,1)S(1)} %fusion.63), channel_id=1, source_target_pairs={{0,1},{1,0},{2,3},{3,2},{4,5},{5,4},{6,7},{7,6},{8,9},{9,8},{10,11... | collective-permute-start | bytes 1228808 | tf_op jit(solution)/shard_map/out_y1/ppermute | solution.py:48
  69.8 19.7 %collective-permute-start.12 = (bf16[4,40,1280]{2,1,0:T(8,128)(2,1)S(1)}, bf16[4,40,1280]{2,1,0:T(8,128)(2,1)S(1)}, u32[]{:S(2)}, u32[]{:S(2)}) collective-permute-start(bf16[4,40,1280]{2,1,0:T(8,128)(2,1)S(1)} %fusion.62), channel_id=1, source_target_pairs={{0,1},{1,0},{2,3},{3,2},{4,5},{5,4},{6,7},{7,6},{8,9},{9,8},{10,11... | collective-permute-start | bytes 1228808 | tf_op jit(solution)/shard_map/out_y2/ppermute | solution.py:48
  71.9 35.5 %collective-permute-start.35 = (bf16[4,40,1280]{2,1,0:T(8,128)(2,1)S(1)}, bf16[4,40,1280]{2,1,0:T(8,128)(2,1)S(1)}, u32[]{:S(2)}, u32[]{:S(2)}) collective-permute-start(bf16[4,40,1280]{2,1,0:T(8,128)(2,1)S(1)} %collective-permute-done.33), channel_id=1, source_target_pairs={{0,2},{1,3},{2,4},{3,5},{4,6},{5,7},{6,0},{7,1},{8,10},{9,11},{10,... | collective-permute-start | bytes 1228808 | tf_op jit(solution)/shard_map/grad_z4/ppermute | solution.py:40
  80.7 17.1 %collective-permute-start.21 = (bf16[4,40,1280]{2,1,0:T(8,128)(2,1)S(1)}, bf16[4,40,1280]{2,1,0:T(8,128)(2,1)S(1)}, u32[]{:S(2)}, u32[]{:S(2)}) collective-permute-start(bf16[4,40,1280]{2,1,0:T(8,128)(2,1)S(1)} %fusion.64), channel_id=1, source_target_pairs={{0,1},{1,0},{2,3},{3,2},{4,5},{5,4},{6,7},{7,6},{8,9},{9,8},{10,11... | collective-permute-start | bytes 1228808 | tf_op jit(solution)/shard_map/out_y3/ppermute | solution.py:48
  90.7 14.0 %collective-permute-start.13 = (bf16[4,40,1280]{2,1,0:T(8,128)(2,1)S(1)}, bf16[4,40,1280]{2,1,0:T(8,128)(2,1)S(1)}, u32[]{:S(2)}, u32[]{:S(2)}) collective-permute-start(bf16[4,40,1280]{2,1,0:T(8,128)(2,1)S(1)} %fusion.61), channel_id=1, source_target_pairs={{0,1},{1,0},{2,3},{3,2},{4,5},{5,4},{6,7},{7,6},{8,9},{9,8},{10,11... | collective-permute-start | bytes 1228808 | tf_op jit(solution)/shard_map/out_y0/ppermute | solution.py:48
  98.3 21.2 %collective-permute-start.25 = (bf16[2,40,1280]{2,1,0:T(8,128)(2,1)S(1)}, bf16[2,40,1280]{2,1,0:T(8,128)(2,1)S(1)}, u32[]{:S(2)}, u32[]{:S(2)}) collective-permute-start(bf16[2,40,1280]{2,1,0:T(8,128)(2,1)S(1)} %bitcast.227), channel_id=1, source_target_pairs={{0,18},{1,19},{2,20},{3,21},{4,22},{5,23},{6,16},{7,17},{8,26},{9,... | collective-permute-start | bytes 614408 | tf_op jit(solution)/shard_map/out_z3_x2/ppermute | solution.py:66
  98.3 21.3 %collective-permute-start.22 = (bf16[2,40,1280]{2,1,0:T(8,128)(2,1)S(1)}, bf16[2,40,1280]{2,1,0:T(8,128)(2,1)S(1)}, u32[]{:S(2)}, u32[]{:S(2)}) collective-permute-start(bf16[2,40,1280]{2,1,0:T(8,128)(2,1)S(1)} %bitcast.226), channel_id=1, source_target_pairs={{0,2},{1,3},{2,4},{3,5},{4,6},{5,7},{6,0},{7,1},{8,10},{9,11},{10,... | collective-permute-start | bytes 614408 | tf_op jit(solution)/shard_map/out_z3_x0/ppermute | solution.py:66
  101.1 18.4 %collective-permute-start.24 = (bf16[2,40,1280]{2,1,0:T(8,128)(2,1)S(1)}, bf16[2,40,1280]{2,1,0:T(8,128)(2,1)S(1)}, u32[]{:S(2)}, u32[]{:S(2)}) collective-permute-start(bf16[2,40,1280]{2,1,0:T(8,128)(2,1)S(1)} %bitcast.229), channel_id=1, source_target_pairs={{0,22},{1,23},{2,16},{3,17},{4,18},{5,19},{6,20},{7,21},{8,30},{9,... | collective-permute-start | bytes 614408 | tf_op jit(solution)/shard_map/out_z1_x2/ppermute | solution.py:66
  105.1 14.4 %collective-permute-start.23 = (bf16[2,40,1280]{2,1,0:T(8,128)(2,1)S(1)}, bf16[2,40,1280]{2,1,0:T(8,128)(2,1)S(1)}, u32[]{:S(2)}, u32[]{:S(2)}) collective-permute-start(bf16[2,40,1280]{2,1,0:T(8,128)(2,1)S(1)} %bitcast.230), channel_id=1, source_target_pairs={{0,16},{8,24},{16,0},{24,8},{1,17},{9,25},{17,1},{25,9},{2,18},{10... | collective-permute-start | bytes 614408 | tf_op jit(solution)/shard_map/own_x2/ppermute | solution.py:54
  107.4 12.2 %collective-permute-start.18 = (bf16[2,40,1280]{2,1,0:T(8,128)(2,1)S(1)}, bf16[2,40,1280]{2,1,0:T(8,128)(2,1)S(1)}, u32[]{:S(2)}, u32[]{:S(2)}) collective-permute-start(bf16[2,40,1280]{2,1,0:T(8,128)(2,1)S(1)} %bitcast.228), channel_id=1, source_target_pairs={{0,6},{1,7},{2,0},{3,1},{4,2},{5,3},{6,4},{7,5},{8,14},{9,15},{10,... | collective-permute-start | bytes 614408 | tf_op jit(solution)/shard_map/out_z1_x0/ppermute | solution.py:66
  (20 other events, 158.5 us)

commit v7 on v6

--- a/solution.py
+++ b/solution.py
@@ -166,8 +166,8 @@
             at = (at[None, :] == slot_iota[:, None]).astype(jnp.bfloat16)
             line.append(pick("rt,td->rd", at, block[:tok_rows]))
         crossed_tok.append(cross(in_chunks(line), f"tok{k}"))
-        if 0 < k:
-            gather_step(blocks_grad, k - 1, "grad", came[k])
+        if k < rows - 1:
+            gather_step(blocks_grad, k, "grad", came[k])
 
     rows_tok, active, slope, parts = [], [], [], []
     for k in range(rows):

time: 123 us -> 122 us (level)
  waiting for transfers between devices: 52.8 us -> 43.5 us
  starting transfers between devices: 33.2 us -> 42.2 us
    ppermute x11, waiting for transfers between devices: 31.6 us -> 23.2 us  [ring_y(): return lax.ppermute(value, 'dp', perm)]
    ppermute x4, starting transfers between devices: 5.48 us -> 11.2 us  [ring_z_to(): return lax.ppermute(value, ('expert', 'dp'), perm)]
    ppermute x9, starting transfers between devices: 5.77 us -> 10.1 us  [ring_z(): return lax.ppermute(value, 'dp', perm)]
    ppermute x9, waiting for transfers between devices: 18.5 us -> 15.3 us  [ring_z(): return lax.ppermute(value, 'dp', perm)]
    ppermute x13, waiting for transfers between devices: 2.7 us -> 4.95 us  [swap_expert(): return lax.ppermute(value, 'expert', [(i, i ^ mask) for i in range(n)])]
    ppermute x13, starting transfers between devices: 10 us -> 8.63 us  [swap_expert(): return lax.ppermute(value, 'expert', [(i, i ^ mask) for i in range(n)])]
  transfers between devices with their start and end apart: 37 -> 37, of which waited for: 15 -> 14; matrix products, arithmetic and copies ran while one was open for 25% -> 25% of each run, Pallas kernels for 0% -> 0%
where the time goes in v7:
time: 122 us
  waiting for transfers between devices  43.5 us (36%)
  starting transfers between devices  42.2 us (35%)
  matrix products  26.7 us (22%)
  other arithmetic  5.44 us (4%)
  local copies, waits for them, and re-layouts  2.48 us (2%)
  between operations  1.69 us (1%)
    ppermute x11, waiting for transfers between devices, ring_y(): return lax.ppermute(value, 'dp', perm)  23.2 us
    ppermute x9, waiting for transfers between devices, ring_z(): return lax.ppermute(value, 'dp', perm)  15.3 us
    ppermute x11, starting transfers between devices, ring_y(): return lax.ppermute(value, 'dp', perm)  12.2 us
    ppermute x4, starting transfers between devices, ring_z_to(): return lax.ppermute(value, ('expert', 'dp'), perm)  11.2 us
    ppermute x9, starting transfers between devices, ring_z(): return lax.ppermute(value, 'dp', perm)  10.1 us
    ppermute x13, starting transfers between devices, swap_expert(): return lax.ppermute(value, 'expert', [(i, i ^ mask) for i in range(n)])  8.63 us
    dot_general x20, matrix products, pick(): found = jnp.einsum(spec, onehot, values, preferred_element_type=jnp.float32)  7.07 us
    ppermute x13, waiting for transfers between devices, swap_expert(): return lax.ppermute(value, 'expert', [(i, i ^ mask) for i in range(n)])  4.95 us
  transfers between devices with their start and end apart: 37, of which 14 were waited for; matrix products, arithmetic and copies ran while one was open for 25% of the time, Pallas kernels for 0%

profile of v7, /device:TPU:0, one launch (start us, length us, event | category | flops | bytes accessed | tf_op | source)
XLA Modules:
  0.0 122.0 jit_solution(1118613311047097885)
XLA Ops:
  3.2 3.1 %collective-permute-start.2 = (bf16[136,1280]{1,0:T(8,128)(2,1)S(1)}, bf16[136,1280]{1,0:T(8,128)(2,1)S(1)}, u32[]{:S(2)}, u32[]{:S(2)}) collective-permute-start(bf16[136,1280]{1,0:T(8,128)(2,1)S(1)} %fusion.130), channel_id=1, source_target_pairs={{0,2},{1,3},{2,4},{3,5},{4,6},{5,7},{6,0},{7,1},{8,10},{9,11},{10,... | collective-permute-start | bytes 1044488 | tf_op jit(solution)/shard_map/tok_z1/ppermute | solution.py:40
  6.3 1.5 %collective-permute-start = (bf16[136,1280]{1,0:T(8,128)(2,1)S(1)}, bf16[136,1280]{1,0:T(8,128)(2,1)S(1)}, u32[]{:S(2)}, u32[]{:S(2)}) collective-permute-start(bf16[136,1280]{1,0:T(8,128)(2,1)S(1)} %fusion.130), channel_id=1, source_target_pairs={{0,1},{1,0},{2,3},{3,2},{4,5},{5,4},{6,7},{7,6},{8,9},{9,8},{10,11... | collective-permute-start | bytes 1044488 | tf_op jit(solution)/shard_map/tok_y0/ppermute | solution.py:48
  8.3 1.6 %collective-permute-start.27 = (bf16[4,10,1280]{2,1,0:T(8,128)(2,1)S(1)}, bf16[4,10,1280]{2,1,0:T(8,128)(2,1)S(1)}, u32[]{:S(2)}, u32[]{:S(2)}) collective-permute-start(bf16[4,10,1280]{2,1,0:T(8,128)(2,1)S(1)} %squeeze.195), channel_id=1, source_target_pairs={{0,16},{8,24},{16,0},{24,8},{1,17},{9,25},{17,1},{25,9},{2,18},{10... | collective-permute-start | bytes 307208 | tf_op jit(solution)/shard_map/grad_x2/ppermute | solution.py:54
  10.7 5.8 %collective-permute-done.2 = bf16[136,1280]{1,0:T(8,128)(2,1)S(1)} collective-permute-done((bf16[136,1280]{1,0:T(8,128)(2,1)S(1)}, bf16[136,1280]{1,0:T(8,128)(2,1)S(1)}, u32[]{:S(2)}, u32[]{:S(2)}) %collective-permute-start.2) | collective-permute-done | bytes 348192 | tf_op jit(solution)/shard_map/tok_z1/ppermute | solution.py:40
  17.5 1.5 %collective-permute-start.3 = (bf16[136,1280]{1,0:T(8,128)(2,1)S(1)}, bf16[136,1280]{1,0:T(8,128)(2,1)S(1)}, u32[]{:S(2)}, u32[]{:S(2)}) collective-permute-start(bf16[136,1280]{1,0:T(8,128)(2,1)S(1)} %collective-permute-done.2), channel_id=1, source_target_pairs={{0,1},{1,0},{2,3},{3,2},{4,5},{5,4},{6,7},{7,6},{8,9},{9,8},{10,11... | collective-permute-start | bytes 1044488 | tf_op jit(solution)/shard_map/tok_y1/ppermute | solution.py:48
  20.0 1.6 %collective-permute-start.30 = (bf16[4,40,1280]{2,1,0:T(8,128)(2,1)S(1)}, bf16[4,40,1280]{2,1,0:T(8,128)(2,1)S(1)}, u32[]{:S(2)}, u32[]{:S(2)}) collective-permute-start(bf16[4,40,1280]{2,1,0:T(8,128)(2,1)S(1)} %copy.59), channel_id=1, source_target_pairs={{0,2},{1,3},{2,4},{3,5},{4,6},{5,7},{6,0},{7,1},{8,10},{9,11},{10,... | collective-permute-start | bytes 1228808 | tf_op jit(solution)/shard_map/grad_z1/ppermute | solution.py:40
  22.0 1.6 %collective-permute-start.1 = (bf16[2,2,40,1280]{3,2,0,1:T(8,128)(2,1)S(1)}, bf16[2,2,40,1280]{3,2,0,1:T(8,128)(2,1)S(1)}, u32[]{:S(2)}, u32[]{:S(2)}) collective-permute-start(bf16[2,2,40,1280]{3,2,0,1:T(8,128)(2,1)S(1)} %get-tuple-element.65), channel_id=1, source_target_pairs={{0,16},{8,24},{16,0},{24,8},{1,17},{9,25},{17,1},{25,9},{2,18},{10... | collective-permute-start | bytes 1228808 | tf_op jit(solution)/shard_map/tok0_x2/ppermute | solution.py:54
  23.8 5.5 %collective-permute-done.4 = bf16[136,1280]{1,0:T(8,128)(2,1)S(1)} collective-permute-done((bf16[136,1280]{1,0:T(8,128)(2,1)S(1)}, bf16[136,1280]{1,0:T(8,128)(2,1)S(1)}, u32[]{:S(2)}, u32[]{:S(2)}) %collective-permute-start.4) | collective-permute-done | bytes 348192 | tf_op jit(solution)/shard_map/tok_z2/ppermute | solution.py:40
  32.3 1.6 %collective-permute-start.15 = (bf16[2,2,40,1280]{3,2,0,1:T(8,128)(2,1)S(1)}, bf16[2,2,40,1280]{3,2,0,1:T(8,128)(2,1)S(1)}, u32[]{:S(2)}, u32[]{:S(2)}) collective-permute-start(bf16[2,2,40,1280]{3,2,0,1:T(8,128)(2,1)S(1)} %get-tuple-element.69), channel_id=1, source_target_pairs={{0,16},{8,24},{16,0},{24,8},{1,17},{9,25},{17,1},{25,9},{2,18},{10... | collective-permute-start | bytes 1228808 | tf_op jit(solution)/shard_map/tok1_x2/ppermute | solution.py:54
  34.0 3.3 %collective-permute-done.29 = bf16[4,40,1280]{2,1,0:T(8,128)(2,1)S(1)} collective-permute-done((bf16[4,40,1280]{2,1,0:T(8,128)(2,1)S(1)}, bf16[4,40,1280]{2,1,0:T(8,128)(2,1)S(1)}, u32[]{:S(2)}, u32[]{:S(2)}) %collective-permute-start.29) | collective-permute-done | bytes 409632 | tf_op jit(solution)/shard_map/grad_y0/ppermute | solution.py:48
  40.6 4.2 %collective-permute-done.6 = bf16[136,1280]{1,0:T(8,128)(2,1)S(1)} collective-permute-done((bf16[136,1280]{1,0:T(8,128)(2,1)S(1)}, bf16[136,1280]{1,0:T(8,128)(2,1)S(1)}, u32[]{:S(2)}, u32[]{:S(2)}) %collective-permute-start.6) | collective-permute-done | bytes 348192 | tf_op jit(solution)/shard_map/tok_y2/ppermute | solution.py:48
  47.2 1.6 %collective-permute-start.9 = (bf16[64,1280]{1,0:T(8,128)(2,1)S(1)}, bf16[64,1280]{1,0:T(8,128)(2,1)S(1)}, u32[]{:S(2)}, u32[]{:S(2)}) collective-permute-start(bf16[64,1280]{1,0:T(8,128)(2,1)S(1)} %slice.423), channel_id=1, source_target_pairs={{0,1},{1,0},{2,3},{3,2},{4,5},{5,4},{6,7},{7,6},{8,9},{9,8},{10,11... | collective-permute-start | bytes 491528 | tf_op jit(solution)/shard_map/tok_y3/ppermute | solution.py:48
  49.0 1.6 %collective-permute-start.7 = (bf16[2,2,40,1280]{3,2,0,1:T(8,128)(2,1)S(1)}, bf16[2,2,40,1280]{3,2,0,1:T(8,128)(2,1)S(1)}, u32[]{:S(2)}, u32[]{:S(2)}) collective-permute-start(bf16[2,2,40,1280]{3,2,0,1:T(8,128)(2,1)S(1)} %get-tuple-element.67), channel_id=1, source_target_pairs={{0,16},{8,24},{16,0},{24,8},{1,17},{9,25},{17,1},{25,9},{2,18},{10... | collective-permute-start | bytes 1228808 | tf_op jit(solution)/shard_map/tok2_x2/ppermute | solution.py:54
  58.2 3.2 %collective-permute-done.7 = bf16[2,2,40,1280]{3,2,0,1:T(8,128)(2,1)S(1)} collective-permute-done((bf16[2,2,40,1280]{3,2,0,1:T(8,128)(2,1)S(1)}, bf16[2,2,40,1280]{3,2,0,1:T(8,128)(2,1)S(1)}, u32[]{:S(2)}, u32[]{:S(2)}) %collective-permute-start.7) | collective-permute-done | bytes 409632 | tf_op jit(solution)/shard_map/tok2_x2/ppermute | solution.py:54
  67.0 1.7 %collective-permute-done.34 = bf16[4,40,1280]{2,1,0:T(8,128)(2,1)S(1)} collective-permute-done((bf16[4,40,1280]{2,1,0:T(8,128)(2,1)S(1)}, bf16[4,40,1280]{2,1,0:T(8,128)(2,1)S(1)}, u32[]{:S(2)}, u32[]{:S(2)}) %collective-permute-start.34) | collective-permute-done | bytes 409632 | tf_op jit(solution)/shard_map/grad_z3/ppermute | solution.py:40
  78.3 7.8 %collective-permute-done.12 = bf16[4,40,1280]{2,1,0:T(8,128)(2,1)S(1)} collective-permute-done((bf16[4,40,1280]{2,1,0:T(8,128)(2,1)S(1)}, bf16[4,40,1280]{2,1,0:T(8,128)(2,1)S(1)}, u32[]{:S(2)}, u32[]{:S(2)}) %collective-permute-start.12) | collective-permute-done | bytes 409632 | tf_op jit(solution)/shard_map/out_y2/ppermute | solution.py:48
  86.2 1.7 %collective-permute-start.14 = (bf16[4,40,1280]{2,1,0:T(8,128)(2,1)S(1)}, bf16[4,40,1280]{2,1,0:T(8,128)(2,1)S(1)}, u32[]{:S(2)}, u32[]{:S(2)}) collective-permute-start(bf16[4,40,1280]{2,1,0:T(8,128)(2,1)S(1)} %fusion.16), channel_id=1, source_target_pairs={{0,6},{1,7},{2,0},{3,1},{4,2},{5,3},{6,4},{7,5},{8,14},{9,15},{10,... | collective-permute-start | bytes 1228808 | tf_op jit(solution)/shard_map/out_z2/ppermute | solution.py:40
  88.4 6.4 %collective-permute-done.21 = bf16[4,40,1280]{2,1,0:T(8,128)(2,1)S(1)} collective-permute-done((bf16[4,40,1280]{2,1,0:T(8,128)(2,1)S(1)}, bf16[4,40,1280]{2,1,0:T(8,128)(2,1)S(1)}, u32[]{:S(2)}, u32[]{:S(2)}) %collective-permute-start.21) | collective-permute-done | bytes 409632 | tf_op jit(solution)/shard_map/out_y3/ppermute | solution.py:48
  96.5 2.1 %collective-permute-start.22 = (bf16[2,40,1280]{2,1,0:T(8,128)(2,1)S(1)}, bf16[2,40,1280]{2,1,0:T(8,128)(2,1)S(1)}, u32[]{:S(2)}, u32[]{:S(2)}) collective-permute-start(bf16[2,40,1280]{2,1,0:T(8,128)(2,1)S(1)} %bitcast.226), channel_id=1, source_target_pairs={{0,2},{1,3},{2,4},{3,5},{4,6},{5,7},{6,0},{7,1},{8,10},{9,11},{10,... | collective-permute-start | bytes 614408 | tf_op jit(solution)/shard_map/out_z3_x0/ppermute | solution.py:66
  99.2 5.3 %collective-permute-start.24 = (bf16[2,40,1280]{2,1,0:T(8,128)(2,1)S(1)}, bf16[2,40,1280]{2,1,0:T(8,128)(2,1)S(1)}, u32[]{:S(2)}, u32[]{:S(2)}) collective-permute-start(bf16[2,40,1280]{2,1,0:T(8,128)(2,1)S(1)} %bitcast.229), channel_id=1, source_target_pairs={{0,22},{1,23},{2,16},{3,17},{4,18},{5,19},{6,20},{7,21},{8,30},{9,... | collective-permute-start | bytes 614408 | tf_op jit(solution)/shard_map/out_z1_x2/ppermute | solution.py:66
  105.2 2.6 %collective-permute-start.18 = (bf16[2,40,1280]{2,1,0:T(8,128)(2,1)S(1)}, bf16[2,40,1280]{2,1,0:T(8,128)(2,1)S(1)}, u32[]{:S(2)}, u32[]{:S(2)}) collective-permute-start(bf16[2,40,1280]{2,1,0:T(8,128)(2,1)S(1)} %bitcast.228), channel_id=1, source_target_pairs={{0,6},{1,7},{2,0},{3,1},{4,2},{5,3},{6,4},{7,5},{8,14},{9,15},{10,... | collective-permute-start | bytes 614408 | tf_op jit(solution)/shard_map/out_z1_x0/ppermute | solution.py:66
  107.8 4.7 %convolution_convert_fusion = bf16[4,512,1280]{2,1,0:T(8,128)(2,1)} fusion(bf16[4,320,1280]{2,1,0:T(8,128)(2,1)S(1)} %constant_dynamic-update-slice_fusion.8, bf16[4,80,512]{2,1,0:T(8,128)(2,1)S(1)} %get-tuple-element.46, bf16[4,80,512]{2,1,0:T(8,128)(2,1)S(1)} %get-tuple-element.41, bf16[4,80,512]{2,1,0:T(8,128)(2,1)S(1)} %get-tuple-element.45, ...), kind=kOutput, calls=%fused_computation | convolution fusion | flops 1685585920 | bytes 9830400 | tf_op jit(solution)/shard_map/erf,erd->efd/dot_general | solution.py:243
  112.5 1.9 %fusion = bf16[4,320,512]{2,1,0:T(8,128)(2,1)S(1)} fusion(f32[4,80,512]{2,1,0:T(8,128)S(1)} %get-tuple-element.59, f32[4,80,512]{2,1,0:T(8,128)S(1)} %get-tuple-element.58, f32[4,80,512]{2,1,0:T(8,128)S(1)} %get-tuple-element.57, f32[4,80,512]{2,1,0:T(8,128)S(1)} %get-tuple-element.56, bf16[4,320,1280]{2,1,0:T(8,128)(2,1)S(1)} %constant_dynamic-update-slice_fusion.8, ...), kind=kOutput, calls=%fused_computation.3 | convolution fusion | flops 1680998400 | bytes 12451840 | tf_op jit(solution)/shard_map/erd,efd->erf/dot_general | solution.py:239
  114.5 4.7 %convolution_convert_fusion.1 = bf16[4,1280,512]{2,1,0:T(8,128)(2,1)} fusion(bf16[4,320,1280]{2,1,0:T(8,128)(2,1)S(1)} %constant_dynamic-update-slice_fusion, bf16[4,320,512]{2,1,0:T(8,128)(2,1)S(1)} %fusion), kind=kOutput, calls=%fused_computation.1 | convolution fusion | flops 1680343040 | bytes 9830400 | tf_op jit(solution)/shard_map/erd,erf->edf/dot_general | solution.py:246
  (200 shorter events, 43.9 us)
Async XLA Ops:
  3.2 13.3 %collective-permute-start.2 = (bf16[136,1280]{1,0:T(8,128)(2,1)S(1)}, bf16[136,1280]{1,0:T(8,128)(2,1)S(1)}, u32[]{:S(2)}, u32[]{:S(2)}) collective-permute-start(bf16[136,1280]{1,0:T(8,128)(2,1)S(1)} %fusion.130), channel_id=1, source_target_pairs={{0,2},{1,3},{2,4},{3,5},{4,6},{5,7},{6,0},{7,1},{8,10},{9,11},{10,... | collective-permute-start | bytes 1044488 | tf_op jit(solution)/shard_map/tok_z1/ppermute | solution.py:40
  16.5 12.9 %collective-permute-start.4 = (bf16[136,1280]{1,0:T(8,128)(2,1)S(1)}, bf16[136,1280]{1,0:T(8,128)(2,1)S(1)}, u32[]{:S(2)}, u32[]{:S(2)}) collective-permute-start(bf16[136,1280]{1,0:T(8,128)(2,1)S(1)} %collective-permute-done.2), channel_id=1, source_target_pairs={{0,2},{1,3},{2,4},{3,5},{4,6},{5,7},{6,0},{7,1},{8,10},{9,11},{10,... | collective-permute-start | bytes 1044488 | tf_op jit(solution)/shard_map/tok_z2/ppermute | solution.py:40
  17.5 11.9 %collective-permute-start.3 = (bf16[136,1280]{1,0:T(8,128)(2,1)S(1)}, bf16[136,1280]{1,0:T(8,128)(2,1)S(1)}, u32[]{:S(2)}, u32[]{:S(2)}) collective-permute-start(bf16[136,1280]{1,0:T(8,128)(2,1)S(1)} %collective-permute-done.2), channel_id=1, source_target_pairs={{0,1},{1,0},{2,3},{3,2},{4,5},{5,4},{6,7},{7,6},{8,9},{9,8},{10,11... | collective-permute-start | bytes 1044488 | tf_op jit(solution)/shard_map/tok_y1/ppermute | solution.py:48
  19.5 17.9 %collective-permute-start.29 = (bf16[4,40,1280]{2,1,0:T(8,128)(2,1)S(1)}, bf16[4,40,1280]{2,1,0:T(8,128)(2,1)S(1)}, u32[]{:S(2)}, u32[]{:S(2)}) collective-permute-start(bf16[4,40,1280]{2,1,0:T(8,128)(2,1)S(1)} %copy.59), channel_id=1, source_target_pairs={{0,1},{1,0},{2,3},{3,2},{4,5},{5,4},{6,7},{7,6},{8,9},{9,8},{10,11... | collective-permute-start | bytes 1228808 | tf_op jit(solution)/shard_map/grad_y0/ppermute | solution.py:48
  20.0 18.1 %collective-permute-start.30 = (bf16[4,40,1280]{2,1,0:T(8,128)(2,1)S(1)}, bf16[4,40,1280]{2,1,0:T(8,128)(2,1)S(1)}, u32[]{:S(2)}, u32[]{:S(2)}) collective-permute-start(bf16[4,40,1280]{2,1,0:T(8,128)(2,1)S(1)} %copy.59), channel_id=1, source_target_pairs={{0,2},{1,3},{2,4},{3,5},{4,6},{5,7},{6,0},{7,1},{8,10},{9,11},{10,... | collective-permute-start | bytes 1228808 | tf_op jit(solution)/shard_map/grad_z1/ppermute | solution.py:40
  29.4 16.2 %collective-permute-start.8 = (bf16[136,1280]{1,0:T(8,128)(2,1)S(1)}, bf16[136,1280]{1,0:T(8,128)(2,1)S(1)}, u32[]{:S(2)}, u32[]{:S(2)}) collective-permute-start(bf16[136,1280]{1,0:T(8,128)(2,1)S(1)} %collective-permute-done.4), channel_id=1, source_target_pairs={{0,2},{1,3},{2,4},{3,5},{4,6},{5,7},{6,0},{7,1},{8,10},{9,11},{10,... | collective-permute-start | bytes 1044488 | tf_op jit(solution)/shard_map/tok_z3/ppermute | solution.py:40
  30.1 14.7 %collective-permute-start.6 = (bf16[136,1280]{1,0:T(8,128)(2,1)S(1)}, bf16[136,1280]{1,0:T(8,128)(2,1)S(1)}, u32[]{:S(2)}, u32[]{:S(2)}) collective-permute-start(bf16[136,1280]{1,0:T(8,128)(2,1)S(1)} %collective-permute-done.4), channel_id=1, source_target_pairs={{0,1},{1,0},{2,3},{3,2},{4,5},{5,4},{6,7},{7,6},{8,9},{9,8},{10,11... | collective-permute-start | bytes 1044488 | tf_op jit(solution)/shard_map/tok_y2/ppermute | solution.py:48
  32.3 14.9 %collective-permute-start.15 = (bf16[2,2,40,1280]{3,2,0,1:T(8,128)(2,1)S(1)}, bf16[2,2,40,1280]{3,2,0,1:T(8,128)(2,1)S(1)}, u32[]{:S(2)}, u32[]{:S(2)}) collective-permute-start(bf16[2,2,40,1280]{3,2,0,1:T(8,128)(2,1)S(1)} %get-tuple-element.69), channel_id=1, source_target_pairs={{0,16},{8,24},{16,0},{24,8},{1,17},{9,25},{17,1},{25,9},{2,18},{10... | collective-permute-start | bytes 1228808 | tf_op jit(solution)/shard_map/tok1_x2/ppermute | solution.py:54
  38.1 16.5 %collective-permute-start.31 = (bf16[4,40,1280]{2,1,0:T(8,128)(2,1)S(1)}, bf16[4,40,1280]{2,1,0:T(8,128)(2,1)S(1)}, u32[]{:S(2)}, u32[]{:S(2)}) collective-permute-start(bf16[4,40,1280]{2,1,0:T(8,128)(2,1)S(1)} %collective-permute-done.30), channel_id=1, source_target_pairs={{0,1},{1,0},{2,3},{3,2},{4,5},{5,4},{6,7},{7,6},{8,9},{9,8},{10,11... | collective-permute-start | bytes 1228808 | tf_op jit(solution)/shard_map/grad_y1/ppermute | solution.py:48
  39.6 15.1 %collective-permute-start.32 = (bf16[4,40,1280]{2,1,0:T(8,128)(2,1)S(1)}, bf16[4,40,1280]{2,1,0:T(8,128)(2,1)S(1)}, u32[]{:S(2)}, u32[]{:S(2)}) collective-permute-start(bf16[4,40,1280]{2,1,0:T(8,128)(2,1)S(1)} %collective-permute-done.30), channel_id=1, source_target_pairs={{0,2},{1,3},{2,4},{3,5},{4,6},{5,7},{6,0},{7,1},{8,10},{9,11},{10,... | collective-permute-start | bytes 1228808 | tf_op jit(solution)/shard_map/grad_z2/ppermute | solution.py:40
  49.0 12.4 %collective-permute-start.7 = (bf16[2,2,40,1280]{3,2,0,1:T(8,128)(2,1)S(1)}, bf16[2,2,40,1280]{3,2,0,1:T(8,128)(2,1)S(1)}, u32[]{:S(2)}, u32[]{:S(2)}) collective-permute-start(bf16[2,2,40,1280]{3,2,0,1:T(8,128)(2,1)S(1)} %get-tuple-element.67), channel_id=1, source_target_pairs={{0,16},{8,24},{16,0},{24,8},{1,17},{9,25},{17,1},{25,9},{2,18},{10... | collective-permute-start | bytes 1228808 | tf_op jit(solution)/shard_map/tok2_x2/ppermute | solution.py:54
  56.6 12.2 %collective-permute-start.34 = (bf16[4,40,1280]{2,1,0:T(8,128)(2,1)S(1)}, bf16[4,40,1280]{2,1,0:T(8,128)(2,1)S(1)}, u32[]{:S(2)}, u32[]{:S(2)}) collective-permute-start(bf16[4,40,1280]{2,1,0:T(8,128)(2,1)S(1)} %collective-permute-done.32), channel_id=1, source_target_pairs={{0,2},{1,3},{2,4},{3,5},{4,6},{5,7},{6,0},{7,1},{8,10},{9,11},{10,... | collective-permute-start | bytes 1228808 | tf_op jit(solution)/shard_map/grad_z3/ppermute | solution.py:40
  56.9 12.2 %collective-permute-start.19 = (bf16[2,2,40,1280]{3,2,1,0:T(8,128)(2,1)S(1)}, bf16[2,2,40,1280]{3,2,1,0:T(8,128)(2,1)S(1)}, u32[]{:S(2)}, u32[]{:S(2)}) collective-permute-start(bf16[2,2,40,1280]{3,2,1,0:T(8,128)(2,1)S(1)} %pad_maximum_fusion.1), channel_id=1, source_target_pairs={{0,16},{8,24},{16,0},{24,8},{1,17},{9,25},{17,1},{25,9},{2,18},{10... | collective-permute-start | bytes 1228808 | tf_op jit(solution)/shard_map/tok3_x2/ppermute | solution.py:54
  65.0 12.3 %collective-permute-start.17 = (bf16[4,40,1280]{2,1,0:T(8,128)(2,1)S(1)}, bf16[4,40,1280]{2,1,0:T(8,128)(2,1)S(1)}, u32[]{:S(2)}, u32[]{:S(2)}) collective-permute-start(bf16[4,40,1280]{2,1,0:T(8,128)(2,1)S(1)} %fusion.63), channel_id=1, source_target_pairs={{0,1},{1,0},{2,3},{3,2},{4,5},{5,4},{6,7},{7,6},{8,9},{9,8},{10,11... | collective-permute-start | bytes 1228808 | tf_op jit(solution)/shard_map/out_y1/ppermute | solution.py:48
  66.6 38.6 %collective-permute-start.35 = (bf16[4,40,1280]{2,1,0:T(8,128)(2,1)S(1)}, bf16[4,40,1280]{2,1,0:T(8,128)(2,1)S(1)}, u32[]{:S(2)}, u32[]{:S(2)}) collective-permute-start(bf16[4,40,1280]{2,1,0:T(8,128)(2,1)S(1)} %collective-permute-done.33), channel_id=1, source_target_pairs={{0,2},{1,3},{2,4},{3,5},{4,6},{5,7},{6,0},{7,1},{8,10},{9,11},{10,... | collective-permute-start | bytes 1228808 | tf_op jit(solution)/shard_map/grad_z4/ppermute | solution.py:40
  72.6 13.4 %collective-permute-start.12 = (bf16[4,40,1280]{2,1,0:T(8,128)(2,1)S(1)}, bf16[4,40,1280]{2,1,0:T(8,128)(2,1)S(1)}, u32[]{:S(2)}, u32[]{:S(2)}) collective-permute-start(bf16[4,40,1280]{2,1,0:T(8,128)(2,1)S(1)} %fusion.62), channel_id=1, source_target_pairs={{0,1},{1,0},{2,3},{3,2},{4,5},{5,4},{6,7},{7,6},{8,9},{9,8},{10,11... | collective-permute-start | bytes 1228808 | tf_op jit(solution)/shard_map/out_y2/ppermute | solution.py:48
  77.3 17.5 %collective-permute-start.21 = (bf16[4,40,1280]{2,1,0:T(8,128)(2,1)S(1)}, bf16[4,40,1280]{2,1,0:T(8,128)(2,1)S(1)}, u32[]{:S(2)}, u32[]{:S(2)}) collective-permute-start(bf16[4,40,1280]{2,1,0:T(8,128)(2,1)S(1)} %fusion.64), channel_id=1, source_target_pairs={{0,1},{1,0},{2,3},{3,2},{4,5},{5,4},{6,7},{7,6},{8,9},{9,8},{10,11... | collective-permute-start | bytes 1228808 | tf_op jit(solution)/shard_map/out_y3/ppermute | solution.py:48
  86.2 12.5 %collective-permute-start.14 = (bf16[4,40,1280]{2,1,0:T(8,128)(2,1)S(1)}, bf16[4,40,1280]{2,1,0:T(8,128)(2,1)S(1)}, u32[]{:S(2)}, u32[]{:S(2)}) collective-permute-start(bf16[4,40,1280]{2,1,0:T(8,128)(2,1)S(1)} %fusion.16), channel_id=1, source_target_pairs={{0,6},{1,7},{2,0},{3,1},{4,2},{5,3},{6,4},{7,5},{8,14},{9,15},{10,... | collective-permute-start | bytes 1228808 | tf_op jit(solution)/shard_map/out_z2/ppermute | solution.py:40
  87.8 16.6 %collective-permute-start.13 = (bf16[4,40,1280]{2,1,0:T(8,128)(2,1)S(1)}, bf16[4,40,1280]{2,1,0:T(8,128)(2,1)S(1)}, u32[]{:S(2)}, u32[]{:S(2)}) collective-permute-start(bf16[4,40,1280]{2,1,0:T(8,128)(2,1)S(1)} %fusion.61), channel_id=1, source_target_pairs={{0,1},{1,0},{2,3},{3,2},{4,5},{5,4},{6,7},{7,6},{8,9},{9,8},{10,11... | collective-permute-start | bytes 1228808 | tf_op jit(solution)/shard_map/out_y0/ppermute | solution.py:48
  95.3 23.8 %collective-permute-start.25 = (bf16[2,40,1280]{2,1,0:T(8,128)(2,1)S(1)}, bf16[2,40,1280]{2,1,0:T(8,128)(2,1)S(1)}, u32[]{:S(2)}, u32[]{:S(2)}) collective-permute-start(bf16[2,40,1280]{2,1,0:T(8,128)(2,1)S(1)} %bitcast.227), channel_id=1, source_target_pairs={{0,18},{1,19},{2,20},{3,21},{4,22},{5,23},{6,16},{7,17},{8,26},{9,... | collective-permute-start | bytes 614408 | tf_op jit(solution)/shard_map/out_z3_x2/ppermute | solution.py:66
  96.5 22.7 %collective-permute-start.22 = (bf16[2,40,1280]{2,1,0:T(8,128)(2,1)S(1)}, bf16[2,40,1280]{2,1,0:T(8,128)(2,1)S(1)}, u32[]{:S(2)}, u32[]{:S(2)}) collective-permute-start(bf16[2,40,1280]{2,1,0:T(8,128)(2,1)S(1)} %bitcast.226), channel_id=1, source_target_pairs={{0,2},{1,3},{2,4},{3,5},{4,6},{5,7},{6,0},{7,1},{8,10},{9,11},{10,... | collective-permute-start | bytes 614408 | tf_op jit(solution)/shard_map/out_z3_x0/ppermute | solution.py:66
  99.2 20.0 %collective-permute-start.24 = (bf16[2,40,1280]{2,1,0:T(8,128)(2,1)S(1)}, bf16[2,40,1280]{2,1,0:T(8,128)(2,1)S(1)}, u32[]{:S(2)}, u32[]{:S(2)}) collective-permute-start(bf16[2,40,1280]{2,1,0:T(8,128)(2,1)S(1)} %bitcast.229), channel_id=1, source_target_pairs={{0,22},{1,23},{2,16},{3,17},{4,18},{5,19},{6,20},{7,21},{8,30},{9,... | collective-permute-start | bytes 614408 | tf_op jit(solution)/shard_map/out_z1_x2/ppermute | solution.py:66
  104.9 14.2 %collective-permute-start.23 = (bf16[2,40,1280]{2,1,0:T(8,128)(2,1)S(1)}, bf16[2,40,1280]{2,1,0:T(8,128)(2,1)S(1)}, u32[]{:S(2)}, u32[]{:S(2)}) collective-permute-start(bf16[2,40,1280]{2,1,0:T(8,128)(2,1)S(1)} %bitcast.230), channel_id=1, source_target_pairs={{0,16},{8,24},{16,0},{24,8},{1,17},{9,25},{17,1},{25,9},{2,18},{10... | collective-permute-start | bytes 614408 | tf_op jit(solution)/shard_map/own_x2/ppermute | solution.py:54
  105.2 14.0 %collective-permute-start.18 = (bf16[2,40,1280]{2,1,0:T(8,128)(2,1)S(1)}, bf16[2,40,1280]{2,1,0:T(8,128)(2,1)S(1)}, u32[]{:S(2)}, u32[]{:S(2)}) collective-permute-start(bf16[2,40,1280]{2,1,0:T(8,128)(2,1)S(1)} %bitcast.228), channel_id=1, source_target_pairs={{0,6},{1,7},{2,0},{3,1},{4,2},{5,3},{6,4},{7,5},{8,14},{9,15},{10,... | collective-permute-start | bytes 614408 | tf_op jit(solution)/shard_map/out_z1_x0/ppermute | solution.py:66
  (20 other events, 152.5 us)
